TPU v7x, 128 devices: a whole 4x4x4 slice. The times are simulated.
128 devices in a mesh: row: 8 (over x_hi, y), col: 16 (over z, x_lo, core).
Axes of the slice: x: 4 (x_hi: 2, x_lo: 2; x = x_hi * 2 + x_lo), y: 4, z: 4, core: 2. Of those that a mesh axis runs over, the one named last changes fastest.
Arguments:
- pair: bfloat16 [640, 640, 128], P('row', 'col'), may hold values from -6 to 6
- block_chain: int32 [10], replicated, may hold values from 0 to 4, never falling along the last dimension, each value on 1 to 4 neighbouring positions
- block_valid: int32 [10], replicated, may hold values 0 or 1
- tri_norm_gain: float32 [128], replicated, may hold values from 0.25 to 1.75
- tri_norm_bias: float32 [128], replicated, may hold values from -3 to 3
- tri_in_weight: bfloat16 [128, 512], replicated, may hold values from -0.5 to 0.5
- tri_gate_weight: bfloat16 [128, 128], replicated, may hold values from -0.5 to 0.5
- out_norm_gain: float32 [128], replicated, may hold values from 0.25 to 1.75
- out_norm_bias: float32 [128], replicated, may hold values from -3 to 3
- tri_out_weight: bfloat16 [128, 128], replicated, may hold values from -0.5 to 0.5
- att_norm_gain: float32 [128], replicated, may hold values from 0.25 to 1.75
- att_norm_bias: float32 [128], replicated, may hold values from -3 to 3
- qkvg_weight: bfloat16 [128, 512], replicated, may hold values from -0.5 to 0.5
- bias_weight: bfloat16 [128, 4], replicated, may hold values from -1 to 1
- inter_chain: float32 [4], replicated, may hold values from -3 to 3
- att_out_weight: bfloat16 [128, 128], replicated, may hold values from -0.5 to 0.5
Outputs:
- pair_out: bfloat16 [640, 640, 128], P('row', 'col')
Inputs may be any that keep to these rules, and one draw needn't show every extreme that they name: `block_chain`: chain numbers never fall along the crop; each chain covers 1 to 4 blocks and every number from 0 up appears.
All inputs are finite; a program needn't handle non-finite values.
Results may differ from a plain program's by a relative error of at most 0.0095.
Values may be sent and summed in bfloat16 or wider, within the bound.
No kernel may reach another device: no remote copies, remote signals or barrier semaphores. Data moves between devices by JAX's collectives and lax.ppermute only.
A program may use at most 128 MiB of HBM per device.

v0:
```python
import jax
import jax.numpy as jnp
from jax import lax
from jax.sharding import PartitionSpec as P

H = 4
DH = 32
MB = 64


MASK_NEG = 10000.0
EPS = 1e-05


def layer_norm(values, gain, shift):
    middle = jnp.mean(values, axis=-1, keepdims=True)
    centred = values - middle
    spread = jnp.mean(centred * centred, axis=-1, keepdims=True)
    return centred * lax.rsqrt(spread + EPS) * gain + shift


def extra_terms(bias_part, inter_chain, key_chain, query_chain, key_valid):
    crossing = (key_chain[:, None] != query_chain[None, :]).astype(jnp.float32)
    masking = MASK_NEG * (key_valid - 1.0)
    return (
        bias_part.astype(jnp.float32)
        + inter_chain[:, None, None] * crossing[None]
        + masking[None, :, None]
    )


def attend(queries, keys, values, extra):
    scores = jnp.einsum("khd,ihd->hki", keys, queries, preferred_element_type=jnp.float32) + extra
    highest = jnp.max(scores, axis=1, keepdims=True)
    powers = jnp.exp(scores - highest)
    weights = (powers / jnp.sum(powers, axis=1, keepdims=True)).astype(jnp.bfloat16)
    return jnp.einsum("hki,khd->ihd", weights, values, preferred_element_type=jnp.float32)


def whole_bias(bias_local, row_devices, col_devices, residues):
    row_count, col_count = (bias_local.shape[0], bias_local.shape[1])
    bias_block = jnp.transpose(bias_local, (2, 0, 1))[None]
    bias_pieces = lax.all_gather(bias_block, ("row", "col"), axis=0, tiled=True)
    return (
        bias_pieces.reshape(row_devices, col_devices, H, row_count, col_count)
        .transpose(2, 0, 3, 1, 4)
        .reshape(H, residues, residues)
    )


def on_device(
    pair,
    block_chain,
    block_valid,
    tri_norm_gain,
    tri_norm_bias,
    tri_in_weight,
    tri_gate_weight,
    out_norm_gain,
    out_norm_bias,
    tri_out_weight,
    att_norm_gain,
    att_norm_bias,
    qkvg_weight,
    bias_weight,
    inter_chain,
    att_out_weight,
):
    row_count, col_count, channels = pair.shape
    hidden = tri_out_weight.shape[0]
    head_width = H * DH
    row_devices = lax.axis_size("row")
    col_devices = lax.axis_size("col")
    residues = row_count * row_devices
    row_start = lax.axis_index("row") * row_count
    col_start = lax.axis_index("col") * col_count
    residue_valid = jnp.repeat(block_valid, MB).astype(jnp.float32)
    residue_chain = jnp.repeat(block_chain, MB)
    valid_rows = lax.dynamic_slice_in_dim(residue_valid, row_start, row_count)
    valid_cols = lax.dynamic_slice_in_dim(residue_valid, col_start, col_count)
    pair_mask = (valid_rows[:, None] * valid_cols[None, :])[:, :, None]
    tri_normed = layer_norm(pair.astype(jnp.float32), tri_norm_gain, tri_norm_bias).astype(
        jnp.bfloat16
    )
    flat_normed = tri_normed.reshape(row_count * col_count, channels)
    tri_proj = jnp.dot(flat_normed, tri_in_weight, preferred_element_type=jnp.float32).reshape(
        row_count, col_count, 4 * hidden
    )
    left_side = (
        pair_mask * jax.nn.sigmoid(tri_proj[:, :, :hidden]) * tri_proj[:, :, hidden : 2 * hidden]
    ).astype(jnp.bfloat16)
    right_side = (
        pair_mask
        * jax.nn.sigmoid(tri_proj[:, :, 2 * hidden : 3 * hidden])
        * tri_proj[:, :, 3 * hidden :]
    ).astype(jnp.bfloat16)
    tri_gate = jax.nn.sigmoid(
        jnp.dot(flat_normed, tri_gate_weight, preferred_element_type=jnp.float32)
    ).reshape(row_count, col_count, channels)
    right_rows = lax.all_gather(right_side, "row", axis=0, tiled=True)
    right_cols = lax.all_to_all(right_rows, "col", split_axis=0, concat_axis=1, tiled=True)
    product = jnp.einsum(
        "ikc,jkc->ijc",
        lax.all_gather(left_side, "col", axis=1, tiled=True),
        right_cols,
        preferred_element_type=jnp.float32,
    )
    product_normed = layer_norm(product, out_norm_gain, out_norm_bias).astype(jnp.bfloat16)
    update = jnp.dot(
        product_normed.reshape(row_count * col_count, hidden),
        tri_out_weight,
        preferred_element_type=jnp.float32,
    ).reshape(row_count, col_count, channels)
    pair_mid = (pair.astype(jnp.float32) + tri_gate * update).astype(jnp.bfloat16)
    att_normed = layer_norm(pair_mid.astype(jnp.float32), att_norm_gain, att_norm_bias).astype(
        jnp.bfloat16
    )
    flat_att = att_normed.reshape(row_count * col_count, channels)
    bias_local = (
        jnp.dot(flat_att, bias_weight, preferred_element_type=jnp.float32)
        .astype(jnp.bfloat16)
        .reshape(row_count, col_count, H)
    )
    bias_full = whole_bias(bias_local, row_devices, col_devices, residues)
    bias_rows = lax.dynamic_slice_in_dim(bias_full, row_start, row_count, 2)
    projected = jnp.dot(flat_att, qkvg_weight, preferred_element_type=jnp.float32).reshape(
        row_count, col_count, 4, H, DH
    )
    queries = (projected[:, :, 0] * DH ** (-0.5)).astype(jnp.bfloat16)
    keys_vals = (
        projected[:, :, 1:3].astype(jnp.bfloat16).reshape(row_count, col_count, 2 * head_width)
    )
    gate_values = jax.nn.sigmoid(projected[:, :, 3]).reshape(row_count, col_count, head_width)
    gathered = lax.all_gather(keys_vals, "row", axis=0, tiled=True)
    chain_rows = lax.dynamic_slice_in_dim(residue_chain, row_start, row_count)
    extra_rows = extra_terms(bias_rows, inter_chain, residue_chain, chain_rows, residue_valid)
    block_cols = 8

    def one_column(query_part, key_part, value_part):
        return attend(query_part, key_part, value_part, extra_rows)

    def column_block(index):
        query_block = lax.dynamic_slice_in_dim(queries, index * block_cols, block_cols, 1)
        pair_block = lax.dynamic_slice_in_dim(gathered, index * block_cols, block_cols, 1).reshape(
            residues, block_cols, 2, H, DH
        )
        return jax.vmap(one_column, in_axes=(1, 1, 1), out_axes=1)(
            query_block, pair_block[:, :, 0], pair_block[:, :, 1]
        )

    results = lax.map(column_block, jnp.arange(col_count // block_cols))
    attended = jnp.moveaxis(results, 0, 1).reshape(row_count, col_count, head_width)
    gated_local = (gate_values * attended).astype(jnp.bfloat16)
    final_update = jnp.dot(
        gated_local.reshape(row_count * col_count, head_width),
        att_out_weight,
        preferred_element_type=jnp.float32,
    ).reshape(row_count, col_count, channels)
    return (pair_mid.astype(jnp.float32) + pair_mask * final_update).astype(jnp.bfloat16)


def solution(mesh):
    placed = (
        P("row", "col", None),
        P(),
        P(),
        P(),
        P(),
        P(),
        P(),
        P(),
        P(),
        P(),
        P(),
        P(),
        P(),
        P(),
        P(),
        P(),
    )
    return jax.shard_map(
        on_device, mesh=mesh, in_specs=placed, out_specs=P("row", "col", None), check_vma=False
    )
```

profile of v0, /device:TPU:1, one launch (start us, length us, event | category | flops | bytes accessed | tf_op | source)
XLA Modules:
  0.0 738.1 jit_solution(5190120572371510073)
XLA Ops:
  17.1 93.2 %all-gather.6.cloned.1.call-done = bf16[640,40,128]{2,1,0:T(8,128)(2,1)} async-done(((bf16[80,40,128]{2,1,0:T(8,128)(2,1)}), bf16[640,40,128]{2,1,0:T(8,128)(2,1)}) %all-gather.6.cloned.1.call-update) | async-done | bytes 6553616 | tf_op jit(solution)/shard_map/all_gather | solution.py:100
  110.3 5.5 all-to-all-start
  117.9 126.8 %all-to-all-done = bf16[640,40,128]{2,1,0:T(8,128)(2,1)} async-done(((bf16[640,40,128]{2,1,0:T(8,128)(2,1)}), bf16[640,40,128]{2,1,0:T(8,128)(2,1)}, u32[]{:S(2)}, u32[]{:S(2)}) %all-to-all-start) | async-done | bytes 6553632 | tf_op jit(solution)/shard_map/all_to_all | solution.py:101
  244.7 7.5 %copy.79 = bf16[40,16,40,128]{3,2,1,0:T(8,128)(2,1)} copy(bf16[40,16,40,128]{3,2,0,1:T(8,128)(2,1)} %bitcast.10) | data formatting | bytes 13107200 | tf_op jit(solution)/shard_map/all_to_all | solution.py:101
  252.1 10.8 %copy.80 = bf16[40,640,128]{1,0,2:T(8,128)(2,1)} copy(bf16[40,640,128]{2,1,0:T(8,128)(2,1)} %bitcast.95) | data formatting | bytes 13107200 | tf_op jit(solution)/shard_map/all_to_all | solution.py:101
  263.0 27.2 %copy.81 = bf16[80,640,128]{0,1,2:T(8,128)(2,1)} copy(bf16[80,640,128]{2,1,0:T(8,128)(2,1)} %all-gather.8.cloned.1.call-done) | data formatting | bytes 26214400 | tf_op jit(solution)/shard_map/all_gather | solution.py:104
  290.2 10.9 %bitcast_reduce_fusion = (f32[80,40]{0,1:T(8,128)S(1)}, f32[128,40,80]{2,1,0:T(8,128)S(1)}) fusion(bf16[40,640,128]{1,0,2:T(8,128)(2,1)} %copy.80, bf16[80,640,128]{0,1,2:T(8,128)(2,1)} %copy.81), kind=kOutput, calls=%fused_computation.29 | convolution fusion | flops 524694400 | bytes 21312000 | tf_op jit(solution)/shard_map/ikc,jkc->ijc/dot_general | solution.py:102
  311.9 8.6 %fusion.43 = f32[80,40,4,4,32]{1,4,3,2,0:T(8,128)} fusion(bf16[4,4,32,128,1]{3,2,1,0,4:T(8,128)(2,1)S(1)} %bitcast.102, bf16[80,40,128]{2,1,0:T(8,128)(2,1)S(1)} %fusion.26), kind=kOutput, calls=%fused_computation.67 | convolution fusion | flops 419430400 | bytes 7503872 | tf_op jit(solution)/shard_map/dot_general | solution.py:126
  320.5 7.8 %slice.93 = bf16[80,40,2,4,32]{1,4,3,2,0:T(8,128)(2,1)} slice(f32[80,40,4,4,32]{1,4,3,2,0:T(8,128)} %fusion.43), slice={[0:80], [0:40], [1:3], [0:4], [0:32]} | slice | bytes 3276800 | tf_op jit(solution)/shard_map/slice | solution.py:131
  328.3 5.8 copy.88
  335.2 6.5 fusion.18
  341.7 4.7 copy.92
  346.3 5.2 copy.93
  351.5 156.9 %all-gather.12.cloned.1.call-done = bf16[512,80,40]{1,2,0:T(8,128)(2,1)} async-done(((bf16[4,80,40]{1,2,0:T(8,128)(2,1)}), bf16[512,80,40]{1,2,0:T(8,128)(2,1)}) %all-gather.12.cloned.1.call-update) | async-done | bytes 3276816 | tf_op jit(solution)/shard_map/all_gather | solution.py:43
  508.4 10.9 %copy.90 = bf16[4,8,80,16,40]{2,1,4,3,0:T(8,128)(2,1)} copy(bf16[4,8,80,16,40]{2,4,0,3,1:T(8,128)(2,1)} %bitcast.99) | data formatting | bytes 6553600 | tf_op jit(solution)/shard_map/transpose | solution.py:46
  519.2 7.4 reshape.178
  528.6 129.8 %all-gather.10.cloned.1.call-done = bf16[640,40,256]{2,1,0:T(8,128)(2,1)} async-done(((bf16[80,40,256]{2,1,0:T(8,128)(2,1)}), bf16[640,40,256]{2,1,0:T(8,128)(2,1)}) %all-gather.10.cloned.1.call-update) | async-done | bytes 13107216 | tf_op jit(solution)/shard_map/all_gather | solution.py:134
  658.5 67.6 %while.10 = (s32[]{:T(128)}, f32[5,80,8,4,32]{1,4,3,2,0:T(8,128)}, s32[5]{0:T(128)S(1)}, bf16[640,40,256]{2,1,0:T(8,128)(2,1)}, bf16[80,40,4,32]{0,3,2,1:T(8,128...) while((s32[]{:T(128)}, f32[5,80,8,4,32]{1,4,3,2,0:T(8,128)}, ...), condition=%wide.region_9.10_spmd, body=%wide.region_6.9_spmd.sunk | while | flops 219546240 | bytes 54717148 | solution.py:151
  661.8 3.4 copy.100
  675.3 3.4 copy.100
  688.8 3.4 copy.100
  702.3 3.4 copy.100
  715.8 3.4 copy.100
  728.7 2.9 fusion.32
  (127 shorter events, 75.5 us)
Async XLA Ops:
  6.5 6.9 copy-start
  6.5 103.8 %all-gather.6.cloned.1.call-start = ((), (), s32[]{:S(2)}) async-start(), calls=%async_computation.1 | async-start | bytes 7372800 | tf_op jit(solution)/shard_map/all_gather | solution.py:100
  16.4 246.6 %all-gather.8.cloned.1.call-start = ((), (), s32[]{:S(2)}) async-start(), calls=%async_computation.2 | async-start | bytes 13926400 | tf_op jit(solution)/shard_map/all_gather | solution.py:104
  17.1 98.9 %copy-start.17 = (bf16[128,128]{1,0:T(8,128)(2,1)S(1)}, bf16[128,128]{1,0:T(8,128)(2,1)}, u32[]{:S(2)}) copy-start(bf16[128,128]{1,0:T(8,128)(2,1)} %param.24) | copy-start | bytes 98308
  110.3 134.4 %all-to-all-start = ((bf16[640,40,128]{2,1,0:T(8,128)(2,1)}), bf16[640,40,128]{2,1,0:T(8,128)(2,1)}, u32[]{:S(2)}, u32[]{:S(2)}) async-start(bf16[640,40,128]{2,1,0:T(8,128)(2,1)} %all-gather.6.cloned.1.call-done), calls=%async_computation | async-start | bytes 13107200 | tf_op jit(solution)/shard_map/all_to_all | solution.py:101
  115.8 392.6 %all-gather.12.cloned.1.call-start = ((), (), s32[]{:S(2)}) async-start(), calls=%async_computation.4 | async-start | bytes 5283840 | tf_op jit(solution)/shard_map/all_gather | solution.py:43
  301.9 4.1 copy-start.8
  303.5 2.6 copy-start.6
  306.0 3.2 copy-start.14
  306.1 3.2 copy-start.15
  306.1 4.2 copy-start.10
  308.2 3.6 copy-start.7
  311.5 347.0 %all-gather.10.cloned.1.call-start = ((), (), s32[]{:S(2)}) async-start(), calls=%async_computation.3 | async-start | bytes 14745600 | tf_op jit(solution)/shard_map/all_gather | solution.py:134
  328.3 5.8 copy-start.16
  519.2 7.4 copy-start.11
  665.2 2.5 copy-start.3
  667.7 2.2 copy-start.2
  678.7 2.5 copy-start.3
  692.2 2.5 copy-start.3
  705.7 2.5 copy-start.3
  719.3 2.5 copy-start.3
  726.1 2.6 copy-start.5
  726.1 2.6 copy-start.9
  726.1 5.5 copy-start.1
  (7 other events, 11.2 us)
Sparse Core Ops, SparseCore 0:
  16.5 93.7 all-gather.5
  112.0 142.8 all-gather.7
  311.6 196.6 all-gather.11
  510.5 147.9 all-gather.9
where the time goes:
time: 740 us; the launch traced here: 738 us
  waiting for transfers between devices  507 us (69%)
  local copies, waits for them, and re-layouts  124 us (17%)
  matrix products  50.8 us (7%)
  other arithmetic  32.5 us (4%)
  between operations  13.5 us (2%)
    all_gather x1, waiting for transfers between devices, whole_bias(): bias_pieces = lax.all_gather(bias_block, ('row', 'col'), axis=0, tiled=True)  157 us
    all_gather x1, waiting for transfers between devices, on_device(): gathered = lax.all_gather(keys_vals, 'row', axis=0, tiled=True)  130 us
    all_to_all x1, waiting for transfers between devices, on_device(): lax.all_to_all(right_rows, 'col', split_axis=0, concat_axis=1, tiled=True)  127 us
    all_gather x1, waiting for transfers between devices, on_device(): right_rows = lax.all_gather(right_side, 'row', axis=0, tiled=True)  93.2 us
    all_gather x1, local copies, waits for them, and re-layouts, on_device(): lax.all_gather(left_side, 'col', axis=1, tiled=True)  27.2 us
    dynamic_slice x10, local copies, waits for them, and re-layouts, column_block(): lax.dynamic_slice_in_dim(gathered, index * block_cols, block_cols, 1)  26.7 us
    all_to_all x2, local copies, waits for them, and re-layouts, on_device(): lax.all_to_all(right_rows, 'col', split_axis=0, concat_axis=1, tiled=True)  18.3 us
  transfers between devices with their start and end apart: 5, of which 4 were waited for; matrix products, arithmetic and copies ran while one was open for 11% of the time, Pallas kernels for 0%

commit v1 on v0

v1 whole, which is shorter than its diff:
```python
import functools

import jax
import jax.numpy as jnp
from jax import lax
from jax.experimental import pallas as pl
from jax.experimental.pallas import tpu as pltpu
from jax.sharding import PartitionSpec as P

H = 4
DH = 32
MB = 64
C = 128
N = 640
ROWS = 8
COLS = 16
RI = N // ROWS
CJ = N // COLS
T = CJ // ROWS
L = N // C
SEND = 56
BACK = 32
PAY = 24
CHUNK = RI

MASK_NEG = 10000.0
EPS = 1e-05

F32 = jnp.float32
BF16 = jnp.bfloat16
PARAMS = pltpu.CompilerParams(vmem_limit_bytes=48 * 1024 * 1024)
VMEM = pl.BlockSpec(memory_space=pltpu.VMEM)
SMEM = pl.BlockSpec(memory_space=pltpu.SMEM)


def dot(a, b, over):
    return lax.dot_general(a, b, (over, ((), ())), preferred_element_type=F32)


def layer_norm(values, gain, shift, axis=-1):
    middle = jnp.mean(values, axis=axis, keepdims=True)
    centred = values - middle
    spread = jnp.mean(centred * centred, axis=axis, keepdims=True)
    return centred * lax.rsqrt(spread + EPS) * gain + shift


def sigmoid(x):
    return 0.5 * jnp.tanh(0.5 * x) + 0.5


def call(kernel, out_shape, scratch, specs, cost=None):
    return pl.pallas_call(
        kernel,
        out_shape=out_shape,
        in_specs=specs,
        out_specs=jax.tree.map(lambda _: VMEM, out_shape),
        scratch_shapes=scratch,
        compiler_params=PARAMS,
        cost_estimate=cost,
    )


def struct(shape, dtype=BF16):
    return jax.ShapeDtypeStruct(shape, dtype)


def turn_kernel(pair_ref, out_ref, wide):
    wide[...] = pair_ref[...].astype(F32).reshape(RI * CJ, C)
    for j in range(CJ):
        out_ref[j] = wide[pl.ds(j, RI, stride=CJ), :].astype(BF16)


def turn_back_kernel(in_ref, out_ref, wide):
    for j in range(CJ):
        wide[pl.ds(j, RI, stride=CJ), :] = in_ref[j].astype(F32)
    out_ref[...] = wide[...].reshape(RI, CJ, C).astype(BF16)


def column(ref, t):
    return jnp.concatenate([ref[r * T + t] for r in range(ROWS)], axis=0)


def project_kernel(x_ref, valid_t_ref, valid_ref, gain_ref, bias_ref, w_ref, out_ref, wide):
    wide[...] = jnp.zeros_like(wide)
    for t in range(T):
        x = column(x_ref, t).astype(F32)
        normed = layer_norm(x, gain_ref[...], bias_ref[...]).astype(BF16)
        proj = dot(w_ref[...], normed, ((1,), (1,)))
        mask = valid_ref[...] * valid_t_ref[t]
        for side in range(2):
            gate = proj[2 * side * C : (2 * side + 1) * C]
            value = proj[(2 * side + 1) * C : (2 * side + 2) * C]
            part = mask * sigmoid(gate) * value
            for l in range(L):
                wide[pl.ds(side * T * L + t * L + l, C, stride=SEND), :] = part[
                    :, l * C : (l + 1) * C
                ]
    out_ref[...] = wide[...].reshape(C, SEND, C).astype(BF16)


def gate_kernel(x_ref, gain_ref, bias_ref, w_ref, out_ref):
    for t in range(T):
        x = column(x_ref, t).astype(F32)
        normed = layer_norm(x, gain_ref[...], bias_ref[...]).astype(BF16)
        out_ref[t] = sigmoid(dot(normed, w_ref[...], ((1,), (0,))))


def product_kernel(in_ref, out_ref, wide, left, right, prod, back):
    wide[...] = in_ref[...].astype(F32).reshape(C * SEND, C)
    for t in range(T):
        for l in range(L):
            left[t * C : (t + 1) * C, l * C : (l + 1) * C] = wide[
                pl.ds(t * L + l, C, stride=SEND), :
            ].astype(BF16)
            right[t * C : (t + 1) * C, l * C : (l + 1) * C] = wide[
                pl.ds(T * L + t * L + l, C, stride=SEND), :
            ].astype(BF16)
    back[...] = jnp.zeros_like(back)
    for l in range(L):
        prod[l] = dot(right[...], left[:, l * C : (l + 1) * C], ((0,), (0,)))
        for t in range(T):
            back[pl.ds(t * L + l, C, stride=BACK), :] = prod[l, pl.ds(t, C, stride=T), :]
    out_ref[...] = back[...].reshape(C, BACK, C).astype(BF16)


def middle_kernel(
    in_ref, x_ref, gate_ref, gain_ref, bias_ref, w_ref, gain2_ref, bias2_ref, wb_ref,
    mid_ref, att_ref, pay_ref, wide,
):
    wide[...] = in_ref[...].astype(F32).reshape(C * BACK, C)
    for t in range(T):
        prod = jnp.concatenate(
            [wide[pl.ds(t * L + l, C, stride=BACK), :] for l in range(L)], axis=1
        )
        normed = layer_norm(prod, gain_ref[...], bias_ref[...], 0).astype(BF16)
        update = dot(normed, w_ref[...], ((0,), (0,)))
        mid = (column(x_ref, t).astype(F32) + gate_ref[t] * update).astype(BF16)
        att = layer_norm(mid.astype(F32), gain2_ref[...], bias2_ref[...]).astype(BF16)
        mid_ref[t] = mid
        att_ref[t] = att
        rows = dot(wb_ref[...], att, ((1,), (1,)))
        for h in range(H):
            pay_ref[h * T + t : h * T + t + 1, :] = rows[h : h + 1].astype(BF16)
    pay_ref[H * T : PAY, :] = jnp.zeros((PAY - H * T, N), BF16)


def qkvg_kernel(att_ref, wqvg_ref, wk_ref, q_ref, k_ref, v_ref, g_ref):
    for t in range(T):
        att = att_ref[t]
        qvg = dot(att, wqvg_ref[...], ((1,), (0,)))
        q_ref[t] = (qvg[:, :C] * DH ** (-0.5)).astype(BF16)
        v_ref[t] = jnp.concatenate(
            [qvg[:, C : 2 * C].astype(BF16), jnp.ones((N, C), BF16)], axis=1
        )
        g_ref[t] = sigmoid(qvg[:, 2 * C :])
        k_ref[t] = dot(wk_ref[...], att, ((1,), (1,))).astype(BF16)


def merge_kernel(me_ref, spread_ref, *refs):
    parts, out_ref, all_rows = refs[:ROWS], refs[ROWS], refs[ROWS + 1]
    for d in range(ROWS):
        all_rows[me_ref[0] ^ d] = parts[d][...].astype(F32)
    rows = all_rows[...].reshape(ROWS * PAY, N).astype(BF16)
    out_ref[...] = dot(spread_ref[...], rows, ((1,), (0,))).astype(BF16)


def attend_kernel(
    me_ref, inter_ref, q_ref, k_ref, v_ref, g_ref, mid_ref, cross_ref, key_ref, valid_ref, valid_t_ref, wo_ref,
    *refs,
):
    parts, out_ref, extra = refs[:COLS], refs[COLS], refs[COLS + 1]
    for d in range(COLS):
        first = (me_ref[0] ^ d) * CJ
        for h in range(H):
            for s in range(CJ // 8):
                at = pl.multiple_of(first + 8 * s, 8)
                crossing = cross_ref[pl.ds(at // MB, 1), :]
                extra[h, pl.ds(at, 8), :] = (
                    parts[d][h * CJ + 8 * s : h * CJ + 8 * s + 8, :].astype(F32)
                    + inter_ref[h] * crossing
                    + key_ref[...]
                )
    lane_head = lax.broadcasted_iota(jnp.int32, (CHUNK, C), 1) // DH

    def one_column(t, carry):
        keys, vals = k_ref[t], v_ref[t]
        for n in range(N // CHUNK):
            rows = slice(n * CHUNK, (n + 1) * CHUNK)
            queries = q_ref[t, rows, :]
            total = jnp.zeros((CHUNK, C), F32)
            for h in range(H):
                own = jnp.where(lane_head == h, queries, jnp.zeros_like(queries))
                scores = dot(own, keys, ((1,), (0,))) + extra[h, rows, :]
                powers = jnp.exp(scores - jnp.max(scores, axis=1, keepdims=True)).astype(BF16)
                sums = dot(powers, vals, ((1,), (0,)))
                total = jnp.where(lane_head == h, sums[:, :C] / sums[:, C:], total)
            gated = (g_ref[t, rows, :] * total).astype(BF16)
            update = dot(gated, wo_ref[...], ((1,), (0,)))
            mask = valid_ref[rows, :] * valid_t_ref[t]
            out_ref[n * T + t] = (mid_ref[t, rows, :].astype(F32) + mask * update).astype(BF16)
        return carry

    lax.fori_loop(0, T, one_column, 0)


def on_device(
    pair,
    block_chain,
    block_valid,
    tri_norm_gain,
    tri_norm_bias,
    tri_in_weight,
    tri_gate_weight,
    out_norm_gain,
    out_norm_bias,
    tri_out_weight,
    att_norm_gain,
    att_norm_bias,
    qkvg_weight,
    bias_weight,
    inter_chain,
    att_out_weight,
):
    row_at, col_at = lax.axis_index("row"), lax.axis_index("col")
    residue_valid = jnp.repeat(block_valid, MB).astype(F32)
    residue_chain = jnp.repeat(block_chain, MB)
    valid_t = lax.dynamic_slice_in_dim(residue_valid, (col_at * ROWS + row_at) * T, T)
    valid_lanes = residue_valid[None, :]
    valid_rows = jnp.broadcast_to(residue_valid[:, None], (N, C))
    cross = (block_chain[:, None] != residue_chain[None, :]).astype(F32)
    key_mask = (MASK_NEG * (residue_valid - 1.0))[None, :]
    gain1, bias1 = tri_norm_gain[None, :], tri_norm_bias[None, :]

    turned = call(turn_kernel, struct((CJ, RI, C)), [pltpu.VMEM((RI * CJ, C), F32)], [VMEM])(pair)
    x = lax.all_to_all(turned, "row", 0, 0, tiled=True)

    parcels = call(
        project_kernel,
        struct((C, SEND, C)),
        [pltpu.VMEM((C * SEND, C), F32)],
        [VMEM, SMEM, VMEM, VMEM, VMEM, VMEM],
    )(x, valid_t, valid_lanes, gain1, bias1, tri_in_weight.T)
    gate = call(gate_kernel, struct((T, N, C), F32), [], [VMEM] * 4)(
        x, gain1, bias1, tri_gate_weight
    )
    channel = lax.all_to_all(parcels, ("col", "row"), 0, 0, tiled=True)
    product = call(
        product_kernel,
        struct((C, BACK, C)),
        [
            pltpu.VMEM((C * SEND, C), F32),
            pltpu.VMEM((N, N), BF16),
            pltpu.VMEM((N, N), BF16),
            pltpu.VMEM((L, N, C), F32),
            pltpu.VMEM((C * BACK, C), F32),
        ],
        [VMEM],
    )(channel)
    returned = lax.all_to_all(product, ("col", "row"), 0, 0, tiled=True)

    wb = jnp.zeros((8, C), BF16).at[:H].set(bias_weight.T)
    mid, att, pay = call(
        middle_kernel,
        [struct((T, N, C)), struct((T, N, C)), struct((PAY, N))],
        [pltpu.VMEM((C * BACK, C), F32)],
        [VMEM] * 9,
    )(
        returned, x, gate, out_norm_gain[:, None], out_norm_bias[:, None], tri_out_weight,
        att_norm_gain[None, :], att_norm_bias[None, :], wb,
    )

    both = ("row", "col")

    def swap(values, row_xor, col_xor):
        pairs = [
            (r * COLS + c, (r ^ row_xor) * COLS + (c ^ col_xor))
            for r in range(ROWS)
            for c in range(COLS)
        ]
        return lax.ppermute(values, both, pairs)

    pays = [pay] + [swap(pay, d, 0) for d in range(1, ROWS)]
    wanted = jnp.arange(H * CJ)
    head, part, t = wanted // CJ, wanted % CJ // T, wanted % T
    spread = (
        (part * PAY + head * T + t)[:, None] == jnp.arange(ROWS * PAY)[None, :]
    ).astype(BF16)
    merged = call(
        merge_kernel,
        struct((H * CJ, N)),
        [pltpu.VMEM((ROWS, PAY, N), F32)],
        [SMEM] + [VMEM] * (ROWS + 1),
    )(row_at[None], spread, *pays)
    even = [merged] + [swap(merged, 0, d) for d in range(2, COLS, 2)]
    odd = [swap(one, 0, 1) for one in even]
    biases = [one for two in zip(even, odd) for one in two]

    wqvg = jnp.concatenate([qkvg_weight[:, :C], qkvg_weight[:, 2 * C :]], axis=1)
    q, k, v, g = call(
        qkvg_kernel,
        [struct((T, N, C)), struct((T, C, N)), struct((T, N, 2 * C)), struct((T, N, C), F32)],
        [],
        [VMEM] * 3,
    )(att, wqvg, qkvg_weight[:, C : 2 * C].T)

    out = call(
        attend_kernel,
        struct((CJ, RI, C)),
        [pltpu.VMEM((H, N, N), F32)],
        [SMEM, SMEM] + [VMEM] * 8 + [SMEM, VMEM] + [VMEM] * COLS,
    )(
        col_at[None], inter_chain, q, k, v, g, mid, cross, key_mask, valid_rows, valid_t, att_out_weight,
        *biases,
    )
    home = lax.all_to_all(out, "row", 0, 0, tiled=True)
    return call(turn_back_kernel, struct((RI, CJ, C)), [pltpu.VMEM((RI * CJ, C), F32)], [VMEM])(home)


def solution(mesh):
    placed = (P("row", "col", None),) + (P(),) * 15
    return jax.shard_map(
        on_device, mesh=mesh, in_specs=placed, out_specs=P("row", "col", None), check_vma=False
    )
```

time: 740 us -> 207 us (0.28)
  waiting for transfers between devices: 507 us -> 36.9 us
  local copies, waits for them, and re-layouts: 124 us -> 11.4 us
  blocking collectives: 0 us -> 55.7 us
  Pallas kernels: 0 us -> 55.4 us
  matrix products: 50.8 us -> 0 us
  starting transfers between devices: 6.05 us -> 46.6 us
  other arithmetic: 32.5 us -> 0.2 us
  between operations: 13.5 us -> 0.28 us
    all_gather x4 -> x0, waiting for transfers between devices: 380 us -> none  [the longest x1 157 us: whole_bias(): bias_pieces = lax.all_gather(bias_block, ('row', 'col'), axis=0, tiled=True)]
    all_to_all x1 -> x2, waiting for transfers between devices: 127 us -> 27.1 us  [the longest x1 15.8 us: on_device(): returned = lax.all_to_all(product, ('col', 'row'), 0, 0, tiled=True)]
    all_to_all x0 -> x2, blocking collectives: none -> 55.7 us  [the longest x1 36.3 us: on_device(): channel = lax.all_to_all(parcels, ('col', 'row'), 0, 0, tiled=True)]
    pallas_call x0 -> x9, Pallas kernels: none -> 55.4 us  [the longest x1 40 us: on_device(): call(attend_kernel, struct((CJ, RI, C)), [pltpu.VMEM((H, N, N), F32)], [S...]
    dot_general x17 -> x0, matrix products: 50.8 us -> none  [the longest x5 12.3 us: attend(): jnp.einsum('khd,ihd->hki', keys, queries, preferred_element_type=jnp.floa...]
    ppermute x0 -> x22, starting transfers between devices: none -> 33.8 us  [swap(): return lax.ppermute(values, both, pairs)]
    dynamic_slice x18 -> x1, local copies, waits for them, and re-layouts: 30.2 us -> 0.08 us  [on_device(): lax.dynamic_slice_in_dim(residue_valid, (col_at * ROWS + row_at) * T, T)]
    all_gather x1 -> x0, local copies, waits for them, and re-layouts: 27.2 us -> none  [on_device(): lax.all_gather(left_side, 'col', axis=1, tiled=True)]
  transfers between devices with their start and end apart: 5 -> 24, of which waited for: 4 -> 5; matrix products, arithmetic and copies ran while one was open for 11% -> 1% of each run, Pallas kernels for 0% -> 1%
where the time goes in v1:
time: 207 us
  blocking collectives  55.7 us (27%)
  Pallas kernels  55.4 us (27%)
  starting transfers between devices  46.6 us (23%)
  waiting for transfers between devices  36.9 us (18%)
  local copies, waits for them, and re-layouts  11.4 us (6%)
    pallas_call x1, Pallas kernels, on_device(): call(attend_kernel, struct((CJ, RI, C)), [pltpu.VMEM((H, N, N), F32)], [S...  40 us
    all_to_all x1, blocking collectives, on_device(): channel = lax.all_to_all(parcels, ('col', 'row'), 0, 0, tiled=True)  36.3 us
    ppermute x22, starting transfers between devices, swap(): return lax.ppermute(values, both, pairs)  33.8 us
    all_to_all x1, blocking collectives, on_device(): home = lax.all_to_all(out, 'row', 0, 0, tiled=True)  19.4 us
    all_to_all x1, waiting for transfers between devices, on_device(): returned = lax.all_to_all(product, ('col', 'row'), 0, 0, tiled=True)  15.8 us
    all_to_all x1, waiting for transfers between devices, on_device(): x = lax.all_to_all(turned, 'row', 0, 0, tiled=True)  11.3 us
    ppermute x22, waiting for transfers between devices, swap(): return lax.ppermute(values, both, pairs)  9.81 us
    unnamed x56, local copies, waits for them, and re-layouts  9.32 us
  transfers between devices with their start and end apart: 24, of which 5 were waited for; matrix products, arithmetic and copies ran while one was open for 1% of the time, Pallas kernels for 1%

profile of v1, /device:TPU:1, one launch (start us, length us, event | category | flops | bytes accessed | tf_op | source)
XLA Modules:
  0.0 206.5 jit_solution(15833649090912221301)
XLA Ops:
  1.2 1.2 shard_map.154
  2.4 7.5 %all-to-all-start = ((bf16[40,80,128]{2,1,0:T(8,128)(2,1)}), bf16[40,80,128]{2,1,0:T(8,128)(2,1)S(1)}, u32[]{:S(2)}, u32[]{:S(2)}) async-start(bf16[40,80,128]{2,1,0:T(8,128)(2,1)} %shard_map.154), calls=%async_computation | async-start | bytes 1638400 | tf_op jit(solution)/shard_map/all_to_all | solution.py:235
  10.3 11.3 %all-to-all-done.x_ref = bf16[40,80,128]{2,1,0:T(8,128)(2,1)S(1)} async-done(((bf16[40,80,128]{2,1,0:T(8,128)(2,1)}), bf16[40,80,128]{2,1,0:T(8,128)(2,1)S(1)}, u32[]{:S(2)}, u32[]{:S(2)}) %all-to-all-start) | async-done | bytes 819232 | tf_op jit(solution)/shard_map/all_to_all | solution.py:235
  21.6 3.0 %shard_map.155 = bf16[128,56,128]{2,1,0:T(8,128)(2,1)S(1)} custom-call(bf16[40,80,128]{2,1,0:T(8,128)(2,1)S(1)} %all-to-all-done.x_ref, f32[5]{0:T(128)S(1)} %dynamic_slice.3.valid_t_ref, f32[1,640]{1,0:T(1,128)S(1)} %convert_element_type.34.valid_ref, f32[1,128]{1,0:T(1,128)S(1)} %bitcast.13, f32[1,128]{1,0:T(1,128)S(1)} %bitcast.15, ...), custom_call_target="tpu_custom_call" | custom-call | tf_op jit(solution)/shard_map/pallas_call | solution.py:237
  24.6 36.3 %all_to_all.20.in_ref = bf16[128,56,128]{2,1,0:T(8,128)(2,1)S(1)} all-to-all(bf16[128,56,128]{2,1,0:T(8,128)(2,1)S(1)} %shard_map.155), channel_id=1, replica_groups=mesh['row'=8,'col'=16] {'col','row'}, dimensions={0} | all-to-all | bytes 3670016 | tf_op jit(solution)/shard_map/all_to_all | solution.py:246
  60.9 4.1 %shard_map.156 = bf16[128,32,128]{2,1,0:T(8,128)(2,1)} custom-call(bf16[128,56,128]{2,1,0:T(8,128)(2,1)S(1)} %all_to_all.20.in_ref), custom_call_target="tpu_custom_call" | custom-call | tf_op jit(solution)/shard_map/pallas_call | solution.py:247
  65.0 5.3 %all-to-all-start.2 = ((bf16[128,32,128]{2,1,0:T(8,128)(2,1)}), bf16[128,32,128]{2,1,0:T(8,128)(2,1)S(1)}, u32[]{:S(2)}, u32[]{:S(2)}) async-start(bf16[128,32,128]{2,1,0:T(8,128)(2,1)} %shard_map.156), calls=%async_computation.2 | async-start | bytes 2097152 | tf_op jit(solution)/shard_map/all_to_all | solution.py:259
  73.0 15.8 %all-to-all-done.2.in_ref = bf16[128,32,128]{2,1,0:T(8,128)(2,1)S(1)} async-done(((bf16[128,32,128]{2,1,0:T(8,128)(2,1)}), bf16[128,32,128]{2,1,0:T(8,128)(2,1)S(1)}, u32[]{:S(2)}, u32[]{:S(2)}) %all-to-all-start.2) | async-done | bytes 1048608 | tf_op jit(solution)/shard_map/all_to_all | solution.py:259
  92.5 3.4 %shard_map.158 = (bf16[5,640,128]{2,1,0:T(8,128)(2,1)S(1)}, bf16[5,640,128]{2,1,0:T(8,128)(2,1)S(1)}, bf16[24,640]{1,0:T(8,128)(2,1)S(1)}) custom-call(bf16[128,32,128]{2,1,0:T(8,128)(2,1)S(1)} %all-to-all-done.2.in_ref, bf16[40,80,128]{2,1,0:T(8,128)(2,1)S(1)} %all-to-all-done.x_ref, f32[5,640,128]{2,1,0:T(8,128)S(1)} %shard_map.157.gate_ref, ...), custom_call_target="tpu_custom_call" | custom-call | tf_op jit(solution)/shard_map/pallas_call | solution.py:262
  98.6 1.9 collective-permute-start.1
  101.8 1.8 collective-permute-start.3
  104.1 3.8 %collective-permute-start.5 = (bf16[24,640]{1,0:T(8,128)(2,1)S(1)}, bf16[24,640]{1,0:T(8,128)(2,1)S(1)}, u32[]{:S(2)}, u32[]{:S(2)}) collective-permute-start(bf16[24,640]{1,0:T(8,128)(2,1)S(1)} %get-tuple-element.30.refs_0_), channel_id=1, source_target_pairs={{0,96},{1,97},{2,98},{3,99},{4,100},{5,101},{6,102},{7,103},{8,104... | collective-permute-start | bytes 92168 | tf_op jit(solution)/shard_map/ppermute | solution.py:280
  107.9 2.9 %collective-permute-start.6 = (bf16[24,640]{1,0:T(8,128)(2,1)S(1)}, bf16[24,640]{1,0:T(8,128)(2,1)S(1)}, u32[]{:S(2)}, u32[]{:S(2)}) collective-permute-start(bf16[24,640]{1,0:T(8,128)(2,1)S(1)} %get-tuple-element.30.refs_0_), channel_id=1, source_target_pairs={{0,112},{1,113},{2,114},{3,115},{4,116},{5,117},{6,118},{7,119},{8... | collective-permute-start | bytes 92168 | tf_op jit(solution)/shard_map/ppermute | solution.py:280
  110.9 3.3 %collective-permute-done.6.refs_7_ = bf16[24,640]{1,0:T(8,128)(2,1)S(1)} collective-permute-done((bf16[24,640]{1,0:T(8,128)(2,1)S(1)}, bf16[24,640]{1,0:T(8,128)(2,1)S(1)}, u32[]{:S(2)}, u32[]{:S(2)}) %collective-permute-start.6) | collective-permute-done | bytes 30752 | tf_op jit(solution)/shard_map/ppermute | solution.py:280
  115.0 1.3 collective-permute-start.12
  116.9 3.0 %collective-permute-start.16 = (bf16[160,640]{1,0:T(8,128)(2,1)S(1)}, bf16[160,640]{1,0:T(8,128)(2,1)S(1)}, u32[]{:S(2)}, u32[]{:S(2)}) collective-permute-start(bf16[160,640]{1,0:T(8,128)(2,1)S(1)} %shard_map.160.refs_0_), channel_id=1, source_target_pairs={{0,10},{1,11},{2,8},{3,9},{4,14},{5,15},{6,12},{7,13},{8,2},{9,3},... | collective-permute-start | bytes 614408 | tf_op jit(solution)/shard_map/ppermute | solution.py:280
  121.8 6.2 %collective-permute-start.20 = (bf16[160,640]{1,0:T(8,128)(2,1)S(1)}, bf16[160,640]{1,0:T(8,128)(2,1)S(1)}, u32[]{:S(2)}, u32[]{:S(2)}) collective-permute-start(bf16[160,640]{1,0:T(8,128)(2,1)S(1)} %shard_map.160.refs_0_), channel_id=1, source_target_pairs={{0,14},{1,15},{2,12},{3,13},{4,10},{5,11},{6,8},{7,9},{8,6},{9,7},... | collective-permute-start | bytes 614408 | tf_op jit(solution)/shard_map/ppermute | solution.py:280
  128.0 5.4 %collective-permute-done.14.refs_8_ = bf16[160,640]{1,0:T(8,128)(2,1)S(1)} collective-permute-done((bf16[160,640]{1,0:T(8,128)(2,1)S(1)}, bf16[160,640]{1,0:T(8,128)(2,1)S(1)}, u32[]{:S(2)}, u32[]{:S(2)}) %collective-permute-start.14) | collective-permute-done | bytes 204832 | tf_op jit(solution)/shard_map/ppermute | solution.py:280
  133.4 2.8 %collective-permute-start.7 = (bf16[160,640]{1,0:T(8,128)(2,1)S(1)}, bf16[160,640]{1,0:T(8,128)(2,1)S(1)}, u32[]{:S(2)}, u32[]{:S(2)}) collective-permute-start(bf16[160,640]{1,0:T(8,128)(2,1)S(1)} %shard_map.160.refs_0_), channel_id=1, source_target_pairs={{0,1},{1,0},{2,3},{3,2},{4,5},{5,4},{6,7},{7,6},{8,9},{9,8},{10,11... | collective-permute-start | bytes 614408 | tf_op jit(solution)/shard_map/ppermute | solution.py:280
  136.3 2.6 %collective-permute-start.13 = (bf16[160,640]{1,0:T(8,128)(2,1)S(1)}, bf16[160,640]{1,0:T(8,128)(2,1)S(1)}, u32[]{:S(2)}, u32[]{:S(2)}) collective-permute-start(bf16[160,640]{1,0:T(8,128)(2,1)S(1)} %collective-permute-done.12.refs_6_), channel_id=1, source_target_pairs={{0,1},{1,0},{2,3},{3,2},{4,5},{5,4},{6,7},{7,6},{8,9},{9,8},{10,11... | collective-permute-start | bytes 614408 | tf_op jit(solution)/shard_map/ppermute | solution.py:280
  139.0 2.2 %collective-permute-start.15 = (bf16[160,640]{1,0:T(8,128)(2,1)S(1)}, bf16[160,640]{1,0:T(8,128)(2,1)S(1)}, u32[]{:S(2)}, u32[]{:S(2)}) collective-permute-start(bf16[160,640]{1,0:T(8,128)(2,1)S(1)} %collective-permute-done.14.refs_8_), channel_id=1, source_target_pairs={{0,1},{1,0},{2,3},{3,2},{4,5},{5,4},{6,7},{7,6},{8,9},{9,8},{10,11... | collective-permute-start | bytes 614408 | tf_op jit(solution)/shard_map/ppermute | solution.py:280
  145.7 40.0 %shard_map.161 = bf16[40,80,128]{2,1,0:T(8,128)(2,1)S(1)} custom-call(s32[1]{0:T(128)} %bitcast.me_ref, f32[4]{0:T(128)S(1)} %copy-done.15, bf16[5,640,128]{2,1,0:T(8,128)(2,1)S(1)} %get-tuple-element.25.q_ref, bf16[5,128,640]{2,1,0:T(8,128)(2,1)S(1)} %get-tuple-element.26.k_ref, bf16[5,640,256]{2,1,0:T(8,128)(2,1)} %copy-done, f32[5,640,128]{2,1,0:T(8,128)} %copy-done.1, ...), custom_call_target="tpu_custom_call" | custom-call | tf_op jit(solution)/shard_map/pallas_call | solution.py:306
  185.7 19.4 %all_to_all.21.in_ref = bf16[40,80,128]{2,1,0:T(8,128)(2,1)S(1)} all-to-all(bf16[40,80,128]{2,1,0:T(8,128)(2,1)S(1)} %shard_map.161), channel_id=1, replica_groups=mesh['row'=8,'col'=16] {'row'}, dimensions={0} | all-to-all | bytes 1638400 | tf_op jit(solution)/shard_map/all_to_all | solution.py:315
  205.2 1.3 shard_map.162
  (109 shorter events, 20.3 us)
Async XLA Ops:
  2.4 19.2 %all-to-all-start = ((bf16[40,80,128]{2,1,0:T(8,128)(2,1)}), bf16[40,80,128]{2,1,0:T(8,128)(2,1)S(1)}, u32[]{:S(2)}, u32[]{:S(2)}) async-start(bf16[40,80,128]{2,1,0:T(8,128)(2,1)} %shard_map.154), calls=%async_computation | async-start | bytes 1638400 | tf_op jit(solution)/shard_map/all_to_all | solution.py:235
  65.0 23.8 %all-to-all-start.2 = ((bf16[128,32,128]{2,1,0:T(8,128)(2,1)}), bf16[128,32,128]{2,1,0:T(8,128)(2,1)S(1)}, u32[]{:S(2)}, u32[]{:S(2)}) async-start(bf16[128,32,128]{2,1,0:T(8,128)(2,1)} %shard_map.156), calls=%async_computation.2 | async-start | bytes 2097152 | tf_op jit(solution)/shard_map/all_to_all | solution.py:259
  97.8 6.3 %collective-permute-start = (bf16[24,640]{1,0:T(8,128)(2,1)S(1)}, bf16[24,640]{1,0:T(8,128)(2,1)S(1)}, u32[]{:S(2)}, u32[]{:S(2)}) collective-permute-start(bf16[24,640]{1,0:T(8,128)(2,1)S(1)} %get-tuple-element.30.refs_0_), channel_id=1, source_target_pairs={{0,16},{1,17},{2,18},{3,19},{4,20},{5,21},{6,22},{7,23},{8,24},{9,... | collective-permute-start | bytes 92168 | tf_op jit(solution)/shard_map/ppermute | solution.py:280
  98.6 9.3 %collective-permute-start.1 = (bf16[24,640]{1,0:T(8,128)(2,1)S(1)}, bf16[24,640]{1,0:T(8,128)(2,1)S(1)}, u32[]{:S(2)}, u32[]{:S(2)}) collective-permute-start(bf16[24,640]{1,0:T(8,128)(2,1)S(1)} %get-tuple-element.30.refs_0_), channel_id=1, source_target_pairs={{0,32},{1,33},{2,34},{3,35},{4,36},{5,37},{6,38},{7,39},{8,40},{9,... | collective-permute-start | bytes 92168 | tf_op jit(solution)/shard_map/ppermute | solution.py:280
  100.6 10.3 %collective-permute-start.2 = (bf16[24,640]{1,0:T(8,128)(2,1)S(1)}, bf16[24,640]{1,0:T(8,128)(2,1)S(1)}, u32[]{:S(2)}, u32[]{:S(2)}) collective-permute-start(bf16[24,640]{1,0:T(8,128)(2,1)S(1)} %get-tuple-element.30.refs_0_), channel_id=1, source_target_pairs={{0,48},{1,49},{2,50},{3,51},{4,52},{5,53},{6,54},{7,55},{8,56},{9,... | collective-permute-start | bytes 92168 | tf_op jit(solution)/shard_map/ppermute | solution.py:280
  101.8 9.1 %collective-permute-start.3 = (bf16[24,640]{1,0:T(8,128)(2,1)S(1)}, bf16[24,640]{1,0:T(8,128)(2,1)S(1)}, u32[]{:S(2)}, u32[]{:S(2)}) collective-permute-start(bf16[24,640]{1,0:T(8,128)(2,1)S(1)} %get-tuple-element.30.refs_0_), channel_id=1, source_target_pairs={{0,64},{1,65},{2,66},{3,67},{4,68},{5,69},{6,70},{7,71},{8,72},{9,... | collective-permute-start | bytes 92168 | tf_op jit(solution)/shard_map/ppermute | solution.py:280
  103.6 7.3 %collective-permute-start.4 = (bf16[24,640]{1,0:T(8,128)(2,1)S(1)}, bf16[24,640]{1,0:T(8,128)(2,1)S(1)}, u32[]{:S(2)}, u32[]{:S(2)}) collective-permute-start(bf16[24,640]{1,0:T(8,128)(2,1)S(1)} %get-tuple-element.30.refs_0_), channel_id=1, source_target_pairs={{0,80},{1,81},{2,82},{3,83},{4,84},{5,85},{6,86},{7,87},{8,88},{9,... | collective-permute-start | bytes 92168 | tf_op jit(solution)/shard_map/ppermute | solution.py:280
  104.1 6.8 %collective-permute-start.5 = (bf16[24,640]{1,0:T(8,128)(2,1)S(1)}, bf16[24,640]{1,0:T(8,128)(2,1)S(1)}, u32[]{:S(2)}, u32[]{:S(2)}) collective-permute-start(bf16[24,640]{1,0:T(8,128)(2,1)S(1)} %get-tuple-element.30.refs_0_), channel_id=1, source_target_pairs={{0,96},{1,97},{2,98},{3,99},{4,100},{5,101},{6,102},{7,103},{8,104... | collective-permute-start | bytes 92168 | tf_op jit(solution)/shard_map/ppermute | solution.py:280
  107.9 6.4 %collective-permute-start.6 = (bf16[24,640]{1,0:T(8,128)(2,1)S(1)}, bf16[24,640]{1,0:T(8,128)(2,1)S(1)}, u32[]{:S(2)}, u32[]{:S(2)}) collective-permute-start(bf16[24,640]{1,0:T(8,128)(2,1)S(1)} %get-tuple-element.30.refs_0_), channel_id=1, source_target_pairs={{0,112},{1,113},{2,114},{3,115},{4,116},{5,117},{6,118},{7,119},{8... | collective-permute-start | bytes 92168 | tf_op jit(solution)/shard_map/ppermute | solution.py:280
  114.5 7.3 %collective-permute-start.10 = (bf16[160,640]{1,0:T(8,128)(2,1)S(1)}, bf16[160,640]{1,0:T(8,128)(2,1)S(1)}, u32[]{:S(2)}, u32[]{:S(2)}) collective-permute-start(bf16[160,640]{1,0:T(8,128)(2,1)S(1)} %shard_map.160.refs_0_), channel_id=1, source_target_pairs={{0,4},{1,5},{2,6},{3,7},{4,0},{5,1},{6,2},{7,3},{8,12},{9,13},{10,... | collective-permute-start | bytes 614408 | tf_op jit(solution)/shard_map/ppermute | solution.py:280
  115.0 13.0 %collective-permute-start.12 = (bf16[160,640]{1,0:T(8,128)(2,1)S(1)}, bf16[160,640]{1,0:T(8,128)(2,1)S(1)}, u32[]{:S(2)}, u32[]{:S(2)}) collective-permute-start(bf16[160,640]{1,0:T(8,128)(2,1)S(1)} %shard_map.160.refs_0_), channel_id=1, source_target_pairs={{0,6},{1,7},{2,4},{3,5},{4,2},{5,3},{6,0},{7,1},{8,14},{9,15},{10,... | collective-permute-start | bytes 614408 | tf_op jit(solution)/shard_map/ppermute | solution.py:280
  116.3 17.2 %collective-permute-start.14 = (bf16[160,640]{1,0:T(8,128)(2,1)S(1)}, bf16[160,640]{1,0:T(8,128)(2,1)S(1)}, u32[]{:S(2)}, u32[]{:S(2)}) collective-permute-start(bf16[160,640]{1,0:T(8,128)(2,1)S(1)} %shard_map.160.refs_0_), channel_id=1, source_target_pairs={{0,8},{1,9},{2,10},{3,11},{4,12},{5,13},{6,14},{7,15},{8,0},{9,1},... | collective-permute-start | bytes 614408 | tf_op jit(solution)/shard_map/ppermute | solution.py:280
  116.9 19.4 %collective-permute-start.16 = (bf16[160,640]{1,0:T(8,128)(2,1)S(1)}, bf16[160,640]{1,0:T(8,128)(2,1)S(1)}, u32[]{:S(2)}, u32[]{:S(2)}) collective-permute-start(bf16[160,640]{1,0:T(8,128)(2,1)S(1)} %shard_map.160.refs_0_), channel_id=1, source_target_pairs={{0,10},{1,11},{2,8},{3,9},{4,14},{5,15},{6,12},{7,13},{8,2},{9,3},... | collective-permute-start | bytes 614408 | tf_op jit(solution)/shard_map/ppermute | solution.py:280
  119.9 16.3 %collective-permute-start.18 = (bf16[160,640]{1,0:T(8,128)(2,1)S(1)}, bf16[160,640]{1,0:T(8,128)(2,1)S(1)}, u32[]{:S(2)}, u32[]{:S(2)}) collective-permute-start(bf16[160,640]{1,0:T(8,128)(2,1)S(1)} %shard_map.160.refs_0_), channel_id=1, source_target_pairs={{0,12},{1,13},{2,14},{3,15},{4,8},{5,9},{6,10},{7,11},{8,4},{9,5},... | collective-permute-start | bytes 614408 | tf_op jit(solution)/shard_map/ppermute | solution.py:280
  121.8 17.1 %collective-permute-start.20 = (bf16[160,640]{1,0:T(8,128)(2,1)S(1)}, bf16[160,640]{1,0:T(8,128)(2,1)S(1)}, u32[]{:S(2)}, u32[]{:S(2)}) collective-permute-start(bf16[160,640]{1,0:T(8,128)(2,1)S(1)} %shard_map.160.refs_0_), channel_id=1, source_target_pairs={{0,14},{1,15},{2,12},{3,13},{4,10},{5,11},{6,8},{7,9},{8,6},{9,7},... | collective-permute-start | bytes 614408 | tf_op jit(solution)/shard_map/ppermute | solution.py:280
  128.0 13.1 %collective-permute-start.8 = (bf16[160,640]{1,0:T(8,128)(2,1)S(1)}, bf16[160,640]{1,0:T(8,128)(2,1)S(1)}, u32[]{:S(2)}, u32[]{:S(2)}) collective-permute-start(bf16[160,640]{1,0:T(8,128)(2,1)S(1)} %shard_map.160.refs_0_), channel_id=1, source_target_pairs={{0,2},{1,3},{2,0},{3,1},{4,6},{5,7},{6,4},{7,5},{8,10},{9,11},{10,... | collective-permute-start | bytes 614408 | tf_op jit(solution)/shard_map/ppermute | solution.py:280
  133.4 7.9 %collective-permute-start.7 = (bf16[160,640]{1,0:T(8,128)(2,1)S(1)}, bf16[160,640]{1,0:T(8,128)(2,1)S(1)}, u32[]{:S(2)}, u32[]{:S(2)}) collective-permute-start(bf16[160,640]{1,0:T(8,128)(2,1)S(1)} %shard_map.160.refs_0_), channel_id=1, source_target_pairs={{0,1},{1,0},{2,3},{3,2},{4,5},{5,4},{6,7},{7,6},{8,9},{9,8},{10,11... | collective-permute-start | bytes 614408 | tf_op jit(solution)/shard_map/ppermute | solution.py:280
  136.3 5.4 %collective-permute-start.11 = (bf16[160,640]{1,0:T(8,128)(2,1)S(1)}, bf16[160,640]{1,0:T(8,128)(2,1)S(1)}, u32[]{:S(2)}, u32[]{:S(2)}) collective-permute-start(bf16[160,640]{1,0:T(8,128)(2,1)S(1)} %collective-permute-done.10.refs_4_), channel_id=1, source_target_pairs={{0,1},{1,0},{2,3},{3,2},{4,5},{5,4},{6,7},{7,6},{8,9},{9,8},{10,11... | collective-permute-start | bytes 614408 | tf_op jit(solution)/shard_map/ppermute | solution.py:280
  136.3 5.5 %collective-permute-start.13 = (bf16[160,640]{1,0:T(8,128)(2,1)S(1)}, bf16[160,640]{1,0:T(8,128)(2,1)S(1)}, u32[]{:S(2)}, u32[]{:S(2)}) collective-permute-start(bf16[160,640]{1,0:T(8,128)(2,1)S(1)} %collective-permute-done.12.refs_6_), channel_id=1, source_target_pairs={{0,1},{1,0},{2,3},{3,2},{4,5},{5,4},{6,7},{7,6},{8,9},{9,8},{10,11... | collective-permute-start | bytes 614408 | tf_op jit(solution)/shard_map/ppermute | solution.py:280
  139.0 6.6 %collective-permute-start.15 = (bf16[160,640]{1,0:T(8,128)(2,1)S(1)}, bf16[160,640]{1,0:T(8,128)(2,1)S(1)}, u32[]{:S(2)}, u32[]{:S(2)}) collective-permute-start(bf16[160,640]{1,0:T(8,128)(2,1)S(1)} %collective-permute-done.14.refs_8_), channel_id=1, source_target_pairs={{0,1},{1,0},{2,3},{3,2},{4,5},{5,4},{6,7},{7,6},{8,9},{9,8},{10,11... | collective-permute-start | bytes 614408 | tf_op jit(solution)/shard_map/ppermute | solution.py:280
  141.1 4.4 %collective-permute-start.17 = (bf16[160,640]{1,0:T(8,128)(2,1)S(1)}, bf16[160,640]{1,0:T(8,128)(2,1)S(1)}, u32[]{:S(2)}, u32[]{:S(2)}) collective-permute-start(bf16[160,640]{1,0:T(8,128)(2,1)S(1)} %collective-permute-done.16.refs_10_), channel_id=1, source_target_pairs={{0,1},{1,0},{2,3},{3,2},{4,5},{5,4},{6,7},{7,6},{8,9},{9,8},{10,11... | collective-permute-start | bytes 614408 | tf_op jit(solution)/shard_map/ppermute | solution.py:280
  141.3 4.3 %collective-permute-start.19 = (bf16[160,640]{1,0:T(8,128)(2,1)S(1)}, bf16[160,640]{1,0:T(8,128)(2,1)S(1)}, u32[]{:S(2)}, u32[]{:S(2)}) collective-permute-start(bf16[160,640]{1,0:T(8,128)(2,1)S(1)} %collective-permute-done.18.refs_12_), channel_id=1, source_target_pairs={{0,1},{1,0},{2,3},{3,2},{4,5},{5,4},{6,7},{7,6},{8,9},{9,8},{10,11... | collective-permute-start | bytes 614408 | tf_op jit(solution)/shard_map/ppermute | solution.py:280
  141.6 3.9 %collective-permute-start.21 = (bf16[160,640]{1,0:T(8,128)(2,1)S(1)}, bf16[160,640]{1,0:T(8,128)(2,1)S(1)}, u32[]{:S(2)}, u32[]{:S(2)}) collective-permute-start(bf16[160,640]{1,0:T(8,128)(2,1)S(1)} %collective-permute-done.20.refs_14_), channel_id=1, source_target_pairs={{0,1},{1,0},{2,3},{3,2},{4,5},{5,4},{6,7},{7,6},{8,9},{9,8},{10,11... | collective-permute-start | bytes 614408 | tf_op jit(solution)/shard_map/ppermute | solution.py:280
  141.8 3.8 %collective-permute-start.9 = (bf16[160,640]{1,0:T(8,128)(2,1)S(1)}, bf16[160,640]{1,0:T(8,128)(2,1)S(1)}, u32[]{:S(2)}, u32[]{:S(2)}) collective-permute-start(bf16[160,640]{1,0:T(8,128)(2,1)S(1)} %collective-permute-done.8.refs_2_), channel_id=1, source_target_pairs={{0,1},{1,0},{2,3},{3,2},{4,5},{5,4},{6,7},{7,6},{8,9},{9,8},{10,11... | collective-permute-start | bytes 614408 | tf_op jit(solution)/shard_map/ppermute | solution.py:280
  (27 other events, 486.4 us)

commit v2 on v1

v2 whole, which is shorter than its diff:
```python
import functools

import jax
import jax.numpy as jnp
from jax import lax
from jax.experimental import pallas as pl
from jax.experimental.pallas import tpu as pltpu
from jax.sharding import PartitionSpec as P

H = 4
DH = 32
MB = 64
C = 128
N = 640
ROWS = 8
COLS = 16
RI = N // ROWS
CJ = N // COLS
T = CJ // ROWS
L = N // C
SEND = 56
BACK = 32
PAY = 24
GROUP = 4
CHUNK = GROUP * RI

MASK_NEG = 10000.0
EPS = 1e-05

F32 = jnp.float32
BF16 = jnp.bfloat16
VMEM = pl.BlockSpec(memory_space=pltpu.VMEM)
SMEM = pl.BlockSpec(memory_space=pltpu.SMEM)


def dot(a, b, over):
    return lax.dot_general(a, b, (over, ((), ())), preferred_element_type=F32)


def layer_norm(values, gain, shift, axis=-1):
    middle = jnp.mean(values, axis=axis, keepdims=True)
    centred = values - middle
    spread = jnp.mean(centred * centred, axis=axis, keepdims=True)
    return centred * lax.rsqrt(spread + EPS) * gain + shift


def sigmoid(x):
    return 0.5 * jnp.tanh(0.5 * x) + 0.5


def call(kernel, out_shape, scratch, specs, cost=None, mib=24):
    return pl.pallas_call(
        kernel,
        out_shape=out_shape,
        in_specs=specs,
        out_specs=jax.tree.map(lambda _: VMEM, out_shape),
        scratch_shapes=scratch,
        compiler_params=pltpu.CompilerParams(vmem_limit_bytes=mib * 1024 * 1024),
        cost_estimate=cost,
    )


def struct(shape, dtype=BF16):
    return jax.ShapeDtypeStruct(shape, dtype)


def turn_kernel(pair_ref, out_ref, wide):
    wide[...] = pair_ref[...].astype(F32).reshape(RI * CJ, C)
    for j in range(CJ):
        out_ref[j] = wide[pl.ds(j, RI, stride=CJ), :].astype(BF16)


def turn_back_kernel(in_ref, out_ref, wide):
    for j in range(CJ):
        wide[pl.ds(j, RI, stride=CJ), :] = in_ref[j].astype(F32)
    out_ref[...] = wide[...].reshape(RI, CJ, C).astype(BF16)


def column(ref, t):
    return jnp.concatenate([ref[r * T + t] for r in range(ROWS)], axis=0)


def project_kernel(x_ref, valid_t_ref, valid_ref, norms_ref, w_ref, out_ref, wide):
    wide[...] = jnp.zeros_like(wide)
    for t in range(T):
        x = column(x_ref, t).astype(F32)
        normed = layer_norm(x, norms_ref[0:1], norms_ref[1:2]).astype(BF16)
        proj = dot(w_ref[...], normed, ((1,), (1,)))
        mask = valid_ref[...] * valid_t_ref[t]
        for side in range(2):
            gate = proj[2 * side * C : (2 * side + 1) * C]
            value = proj[(2 * side + 1) * C : (2 * side + 2) * C]
            part = mask * sigmoid(gate) * value
            for l in range(L):
                wide[pl.ds(side * T * L + t * L + l, C, stride=SEND), :] = part[
                    :, l * C : (l + 1) * C
                ]
    out_ref[...] = wide[...].reshape(C, SEND, C).astype(BF16)


def gate_kernel(x_ref, norms_ref, w_ref, out_ref):
    for t in range(T):
        x = column(x_ref, t).astype(F32)
        normed = layer_norm(x, norms_ref[0:1], norms_ref[1:2]).astype(BF16)
        out_ref[t] = sigmoid(dot(normed, w_ref[...], ((1,), (0,))))


def product_kernel(in_ref, out_ref, wide, left, right, prod, back):
    wide[...] = in_ref[...].astype(F32).reshape(C * SEND, C)
    for t in range(T):
        for l in range(L):
            left[t * C : (t + 1) * C, l * C : (l + 1) * C] = wide[
                pl.ds(t * L + l, C, stride=SEND), :
            ].astype(BF16)
            right[t * C : (t + 1) * C, l * C : (l + 1) * C] = wide[
                pl.ds(T * L + t * L + l, C, stride=SEND), :
            ].astype(BF16)
    back[...] = jnp.zeros_like(back)
    for l in range(L):
        prod[l] = dot(right[...], left[:, l * C : (l + 1) * C], ((0,), (0,)))
        for t in range(T):
            back[pl.ds(t * L + l, C, stride=BACK), :] = prod[l, pl.ds(t, C, stride=T), :]
    out_ref[...] = back[...].reshape(C, BACK, C).astype(BF16)


def middle_kernel(
    in_ref, x_ref, gate_ref, norms_ref, w_ref,
    mid_ref, att_ref, pay_ref, wide, pay,
):
    wide[...] = in_ref[...].astype(F32).reshape(C * BACK, C)
    gain = jnp.broadcast_to(norms_ref[2:3], (C, C)).T[:, :1]
    bias = jnp.broadcast_to(norms_ref[3:4], (C, C)).T[:, :1]
    for t in range(T):
        prod = jnp.concatenate(
            [wide[pl.ds(t * L + l, C, stride=BACK), :] for l in range(L)], axis=1
        )
        normed = layer_norm(prod, gain, bias, 0).astype(BF16)
        update = dot(normed, w_ref[:C], ((0,), (0,)))
        mid = (column(x_ref, t).astype(F32) + gate_ref[t] * update).astype(BF16)
        att = layer_norm(mid.astype(F32), norms_ref[4:5], norms_ref[5:6]).astype(BF16)
        mid_ref[t] = mid
        att_ref[t] = att
        rows = dot(w_ref[C:], att, ((1,), (1,)))
        for h in range(H):
            pay[h * T + t : h * T + t + 1, :] = rows[h : h + 1]
    pay[H * T : PAY, :] = jnp.zeros((PAY - H * T, N), F32)
    for r in range(ROWS):
        pay_ref[r] = pay[...].astype(BF16)


def qkvg_kernel(att_ref, wqvg_ref, wk_ref, q_ref, k_ref, v_ref, g_ref):
    for t in range(T):
        att = att_ref[t]
        qvg = dot(att, wqvg_ref[...], ((1,), (0,)))
        q_ref[t] = (qvg[:, :C] * DH ** (-0.5)).astype(BF16)
        v_ref[t] = jnp.concatenate(
            [qvg[:, C : 2 * C].astype(BF16), jnp.ones((N, C), BF16)], axis=1
        )
        g_ref[t] = sigmoid(qvg[:, 2 * C :])
        k_ref[t] = dot(wk_ref[...], att, ((1,), (1,))).astype(BF16)


def merge_kernel(spread_ref, in_ref, out_ref):
    rows = in_ref[...].astype(F32).reshape(ROWS * PAY, N).astype(BF16)
    out_ref[...] = dot(spread_ref[...], rows, ((1,), (0,))).astype(BF16)


def attend_kernel(
    steps, me_ref, inter_ref, q_ref, k_ref, v_ref, g_ref, mid_ref, cross_ref, key_ref, valid_ref, valid_t_ref, wo_ref,
    *refs,
):
    parts, (out_ref, extra, score_a, score_b, power_a, power_b) = refs[:4], refs[4:]
    score, power = (score_a, score_b), (power_a, power_b)
    me = me_ref[0]
    chips = [(me // 2) ^ step for step in steps]
    for n in range(GROUP):
        for other in range(2):
            core = (me % 2) ^ other
            first = chips[n] * RI + core * CJ
            part = parts[2 * other] if n == 0 else parts[2 * other + 1].at[n - 1]
            for s in range(CJ // 8):
                to = pl.multiple_of(n * RI + core * CJ + 8 * s, 8)
                crossing = cross_ref[pl.ds((first + 8 * s) // MB, 1), :]
                for h in range(H):
                    extra[h, pl.ds(to, 8), :] = (
                        part[h * CJ + 8 * s : h * CJ + 8 * s + 8, :].astype(F32)
                        + inter_ref[h] * crossing
                        + key_ref[...]
                    )
    lane_head = lax.broadcasted_iota(jnp.int32, (CHUNK, C), 1) // DH

    def rows_of(take):
        return jnp.concatenate([take(pl.ds(pl.multiple_of(chip * RI, RI), RI)) for chip in chips], axis=0)

    valid = rows_of(lambda rows: valid_ref[rows, :])

    def one_column(t, carry):
        queries = rows_of(lambda rows: q_ref[t, rows, :])

        def set_score(h):
            own = jnp.where(lane_head == h, queries, jnp.zeros_like(queries))
            score[h % 2][...] = dot(own, k_ref[t], ((1,), (0,))) + extra[h]

        total = jnp.zeros((CHUNK, C), F32)
        set_score(0)
        for h in range(H):
            if h + 1 < H:
                set_score(h + 1)
            now = score[h % 2][...]
            highest = jnp.max(now, axis=1, keepdims=True)
            power[h % 2][...] = jnp.exp(now - highest).astype(BF16)
            sums = dot(power[h % 2][...], v_ref[t], ((1,), (0,)))
            total = jnp.where(lane_head == h, sums[:, :C] / sums[:, C:], total)
        gated = (rows_of(lambda rows: g_ref[t, rows, :]) * total).astype(BF16)
        update = dot(gated, wo_ref[...], ((1,), (0,)))
        mid = rows_of(lambda rows: mid_ref[t, rows, :]).astype(F32)
        out = (mid + valid * valid_t_ref[t] * update).astype(BF16)
        for n in range(GROUP):
            out_ref[n * T + t] = out[n * RI : (n + 1) * RI]
        return carry

    lax.fori_loop(0, T, one_column, 0)


def order_kernel(me_ref, *refs):
    out_ref = refs[-1]
    for step in range(ROWS):
        chip = (me_ref[0] // 2) ^ step
        for t in range(T):
            out_ref[chip * T + t] = refs[step % 2][step // 2 * T + t]


def on_device(
    pair,
    block_chain,
    block_valid,
    tri_norm_gain,
    tri_norm_bias,
    tri_in_weight,
    tri_gate_weight,
    out_norm_gain,
    out_norm_bias,
    tri_out_weight,
    att_norm_gain,
    att_norm_bias,
    qkvg_weight,
    bias_weight,
    inter_chain,
    att_out_weight,
):
    row_at, col_at = lax.axis_index("row"), lax.axis_index("col")
    residue_valid = jnp.repeat(block_valid, MB).astype(F32)
    residue_chain = jnp.repeat(block_chain, MB)
    valid_t = lax.dynamic_slice_in_dim(residue_valid, (col_at * ROWS + row_at) * T, T)
    valid_lanes = residue_valid[None, :]
    valid_rows = jnp.broadcast_to(residue_valid[:, None], (N, C))
    cross = (block_chain[:, None] != residue_chain[None, :]).astype(F32)
    key_mask = (MASK_NEG * (residue_valid - 1.0))[None, :]
    norms = jnp.stack(
        [tri_norm_gain, tri_norm_bias, out_norm_gain, out_norm_bias, att_norm_gain, att_norm_bias]
    )

    turned = call(turn_kernel, struct((CJ, RI, C)), [pltpu.VMEM((RI * CJ, C), F32)], [VMEM])(pair)
    x = lax.all_to_all(turned, "row", 0, 0, tiled=True)

    parcels = call(
        project_kernel,
        struct((C, SEND, C)),
        [pltpu.VMEM((C * SEND, C), F32)],
        [VMEM, SMEM, VMEM, VMEM, VMEM],
    )(x, valid_t, valid_lanes, norms, tri_in_weight.T)
    gate = call(gate_kernel, struct((T, N, C), F32), [], [VMEM] * 3)(
        x, norms, tri_gate_weight
    )
    channel = lax.all_to_all(parcels, ("col", "row"), 0, 0, tiled=True)
    product = call(
        product_kernel,
        struct((C, BACK, C)),
        [
            pltpu.VMEM((C * SEND, C), F32),
            pltpu.VMEM((N, N), BF16),
            pltpu.VMEM((N, N), BF16),
            pltpu.VMEM((L, N, C), F32),
            pltpu.VMEM((C * BACK, C), F32),
        ],
        [VMEM],
    )(channel)
    returned = lax.all_to_all(product, ("col", "row"), 0, 0, tiled=True)

    w_mid = jnp.concatenate([tri_out_weight, jnp.pad(bias_weight.T, ((0, 8 - H), (0, 0)))])
    mid, att, pay = call(
        middle_kernel,
        [struct((T, N, C)), struct((T, N, C)), struct((ROWS, PAY, N))],
        [pltpu.VMEM((C * BACK, C), F32), pltpu.VMEM((PAY, N), F32)],
        [VMEM] * 5,
    )(
        returned, x, gate, norms, w_mid
    )

    both = ("row", "col")

    def swap(values, row_xor, col_xor):
        pairs = [
            (r * COLS + c, (r ^ row_xor) * COLS + (c ^ col_xor))
            for r in range(ROWS)
            for c in range(COLS)
        ]
        return lax.ppermute(values, both, pairs)

    wanted = jnp.arange(H * CJ)
    head, part, t = wanted // CJ, wanted % CJ // T, wanted % T
    spread = (
        (part * PAY + head * T + t)[:, None] == jnp.arange(ROWS * PAY)[None, :]
    ).astype(BF16)
    merged = call(merge_kernel, struct((H * CJ, N)), [], [VMEM] * 2)(
        spread, lax.all_to_all(pay, "row", 0, 0, tiled=True)
    )
    hold = lax.optimization_barrier
    *column, beside = hold([swap(merged, 0, 4 * d) for d in range(1, GROUP)] + [swap(merged, 0, 2)])
    along = jnp.stack(column)
    across = swap(along, 0, 2)
    wqvg = jnp.concatenate([qkvg_weight[:, :C], qkvg_weight[:, 2 * C :]], axis=1)
    q, k, v, g = call(
        qkvg_kernel,
        [struct((T, N, C)), struct((T, C, N)), struct((T, N, 2 * C)), struct((T, N, C), F32)],
        [],
        [VMEM] * 3,
    )(att, wqvg, qkvg_weight[:, C : 2 * C].T)


    def attend(first, *parts):
        steps = [2 * d + first for d in range(GROUP)]
        return call(
            functools.partial(attend_kernel, tuple(steps)),
            struct((GROUP * T, RI, C)),
            [pltpu.VMEM((H, CHUNK, N), F32)]
            + [pltpu.VMEM((CHUNK, N), F32)] * 2
            + [pltpu.VMEM((CHUNK, N), BF16)] * 2,
            [SMEM, SMEM] + [VMEM] * 8 + [SMEM, VMEM] + [VMEM] * 4,
            pl.CostEstimate(
                flops=2 * T * H * CHUNK * N * 3 * C,
                bytes_accessed=8 * 1024 * 1024,
                transcendentals=T * H * CHUNK * N,
            ),
        )(
            col_at[None], inter_chain, q, k, v, g, mid, cross, key_mask, valid_rows, valid_t, att_out_weight,
            *parts,
        )

    merged2, along2, beside2, q, k, v, g = hold(
        (swap(merged, 0, 1), swap(along, 0, 1), swap(beside, 0, 1), q, k, v, g)
    )
    near = attend(0, merged, along, merged2, along2)
    near, across = hold((near, across))
    far = attend(1, beside, across, beside2, swap(across, 0, 1))
    out = call(order_kernel, struct((CJ, RI, C)), [], [SMEM] + [VMEM] * 2)(col_at[None], near, far)
    home = lax.all_to_all(out, "row", 0, 0, tiled=True)
    return call(turn_back_kernel, struct((RI, CJ, C)), [pltpu.VMEM((RI * CJ, C), F32)], [VMEM])(home)


def solution(mesh):
    placed = (P("row", "col", None),) + (P(),) * 15
    return jax.shard_map(
        on_device, mesh=mesh, in_specs=placed, out_specs=P("row", "col", None), check_vma=False
    )
```

time: 207 us -> 169 us (0.82)
  starting transfers between devices: 46.6 us -> 25.8 us
  Pallas kernels: 55.4 us -> 36.6 us
  waiting for transfers between devices: 36.9 us -> 43.3 us
  local copies, waits for them, and re-layouts: 11.4 us -> 7.19 us
  blocking collectives: 55.7 us -> 53.4 us
    ppermute x22 -> x9, starting transfers between devices: 33.8 us -> 9.36 us  [swap(): return lax.ppermute(values, both, pairs)]
    pallas_call x4 -> x6, Pallas kernels: 44.8 us -> 26 us  [the longest x2 21.1 us: attend(): call(functools.partial(attend_kernel, tuple(steps)), struct((GROUP * T, R...]
    all_to_all x0 -> x1, waiting for transfers between devices: none -> 6.77 us  [on_device(): lax.all_to_all(pay, 'row', 0, 0, tiled=True)]
    all_to_all x0 -> x1, starting transfers between devices: none -> 3.62 us  [on_device(): lax.all_to_all(pay, 'row', 0, 0, tiled=True)]
    unnamed x56 -> x50, local copies, waits for them, and re-layouts: 9.32 us -> 6.58 us
    all_to_all x1, blocking collectives: 19.4 us -> 17.1 us  [on_device(): home = lax.all_to_all(out, 'row', 0, 0, tiled=True)]
    ppermute x22 -> x9, waiting for transfers between devices: 9.81 us -> 9.36 us  [swap(): return lax.ppermute(values, both, pairs)]
  transfers between devices with their start and end apart: 24 -> 12, of which waited for: 5 -> 9; matrix products, arithmetic and copies ran while one was open for 1% -> 1% of each run, Pallas kernels for 1% -> 8%
where the time goes in v2:
time: 169 us; the launch traced here: 168 us
  blocking collectives  53.4 us (32%)
  waiting for transfers between devices  43.3 us (26%)
  Pallas kernels  36.6 us (22%)
  starting transfers between devices  25.8 us (15%)
  local copies, waits for them, and re-layouts  7.19 us (4%)
    all_to_all x1, blocking collectives, on_device(): channel = lax.all_to_all(parcels, ('col', 'row'), 0, 0, tiled=True)  36.3 us
    pallas_call x2, Pallas kernels, attend(): call(functools.partial(attend_kernel, tuple(steps)), struct((GROUP * T, R...  21.1 us
    all_to_all x1, blocking collectives, on_device(): home = lax.all_to_all(out, 'row', 0, 0, tiled=True)  17.1 us
    all_to_all x1, waiting for transfers between devices, on_device(): returned = lax.all_to_all(product, ('col', 'row'), 0, 0, tiled=True)  16 us
    all_to_all x1, waiting for transfers between devices, on_device(): x = lax.all_to_all(turned, 'row', 0, 0, tiled=True)  11.2 us
    ppermute x9, waiting for transfers between devices, swap(): return lax.ppermute(values, both, pairs)  9.36 us
    ppermute x9, starting transfers between devices, swap(): return lax.ppermute(values, both, pairs)  9.36 us
    all_to_all x1, starting transfers between devices, on_device(): x = lax.all_to_all(turned, 'row', 0, 0, tiled=True)  7.48 us
  transfers between devices with their start and end apart: 12, of which 9 were waited for; matrix products, arithmetic and copies ran while one was open for 1% of the time, Pallas kernels for 8%

profile of v2, /device:TPU:1, one launch (start us, length us, event | category | flops | bytes accessed | tf_op | source)
XLA Modules:
  0.0 168.1 jit_solution(12663498004420800860)
XLA Ops:
  0.0 1.1 copy-done
  1.2 1.2 shard_map.154
  2.4 7.5 %all-to-all-start = ((bf16[40,80,128]{2,1,0:T(8,128)(2,1)}), bf16[40,80,128]{2,1,0:T(8,128)(2,1)S(1)}, u32[]{:S(2)}, u32[]{:S(2)}) async-start(bf16[40,80,128]{2,1,0:T(8,128)(2,1)} %shard_map.154), calls=%async_computation | async-start | bytes 1638400 | tf_op jit(solution)/shard_map/all_to_all | solution.py:264
  10.4 11.2 %all-to-all-done.x_ref = bf16[40,80,128]{2,1,0:T(8,128)(2,1)S(1)} async-done(((bf16[40,80,128]{2,1,0:T(8,128)(2,1)}), bf16[40,80,128]{2,1,0:T(8,128)(2,1)S(1)}, u32[]{:S(2)}, u32[]{:S(2)}) %all-to-all-start) | async-done | bytes 819232 | tf_op jit(solution)/shard_map/all_to_all | solution.py:264
  21.6 3.0 %shard_map.155 = bf16[128,56,128]{2,1,0:T(8,128)(2,1)S(1)} custom-call(bf16[40,80,128]{2,1,0:T(8,128)(2,1)S(1)} %all-to-all-done.x_ref, f32[5]{0:T(128)S(1)} %dynamic_slice.3.valid_t_ref, f32[1,640]{1,0:T(1,128)S(1)} %convert_element_type.37.valid_ref, f32[6,128]{1,0:T(8,128)S(1)} %stack.39.norms_ref, bf16[512,128]{1,0:T(8,128)(2,1)S(1)} %bitcast.13), custom_call_target="tpu_custom_call" | custom-call | tf_op jit(solution)/shard_map/pallas_call | solution.py:266
  24.7 36.3 %all_to_all.25.in_ref = bf16[128,56,128]{2,1,0:T(8,128)(2,1)S(1)} all-to-all(bf16[128,56,128]{2,1,0:T(8,128)(2,1)S(1)} %shard_map.155), channel_id=1, replica_groups=mesh['row'=8,'col'=16] {'col','row'}, dimensions={0} | all-to-all | bytes 3670016 | tf_op jit(solution)/shard_map/all_to_all | solution.py:275
  60.9 4.0 %shard_map.156 = bf16[128,32,128]{2,1,0:T(8,128)(2,1)} custom-call(bf16[128,56,128]{2,1,0:T(8,128)(2,1)S(1)} %all_to_all.25.in_ref), custom_call_target="tpu_custom_call" | custom-call | tf_op jit(solution)/shard_map/pallas_call | solution.py:276
  65.0 5.3 %all-to-all-start.2 = ((bf16[128,32,128]{2,1,0:T(8,128)(2,1)}), bf16[128,32,128]{2,1,0:T(8,128)(2,1)S(1)}, u32[]{:S(2)}, u32[]{:S(2)}) async-start(bf16[128,32,128]{2,1,0:T(8,128)(2,1)} %shard_map.156), calls=%async_computation.2 | async-start | bytes 2097152 | tf_op jit(solution)/shard_map/all_to_all | solution.py:288
  71.7 1.1 shard_map.157.gate_ref
  72.8 16.0 %all-to-all-done.2.in_ref = bf16[128,32,128]{2,1,0:T(8,128)(2,1)S(1)} async-done(((bf16[128,32,128]{2,1,0:T(8,128)(2,1)}), bf16[128,32,128]{2,1,0:T(8,128)(2,1)S(1)}, u32[]{:S(2)}, u32[]{:S(2)}) %all-to-all-start.2) | async-done | bytes 1048608 | tf_op jit(solution)/shard_map/all_to_all | solution.py:288
  88.8 3.5 %shard_map.158 = (bf16[5,640,128]{2,1,0:T(8,128)(2,1)S(1)}, bf16[5,640,128]{2,1,0:T(8,128)(2,1)S(1)}, bf16[8,24,640]{2,1,0:T(8,128)(2,1)S(1)}) custom-call(bf16[128,32,128]{2,1,0:T(8,128)(2,1)S(1)} %all-to-all-done.2.in_ref, bf16[40,80,128]{2,1,0:T(8,128)(2,1)S(1)} %all-to-all-done.x_ref, f32[5,640,128]{2,1,0:T(8,128)S(1)} %shard_map.157.gate_ref, ...), custom_call_target="tpu_custom_call" | custom-call | tf_op jit(solution)/shard_map/pallas_call | solution.py:291
  94.8 3.6 %all-to-all-start.3 = ((bf16[8,24,640]{2,1,0:T(8,128)(2,1)}), bf16[8,24,640]{2,1,0:T(8,128)(2,1)S(1)}, u32[]{:S(2)}, u32[]{:S(2)}) async-start(bf16[8,24,640]{2,1,0:T(8,128)(2,1)} %copy-done.3), calls=%async_computation.3 | async-start | bytes 491520 | tf_op jit(solution)/shard_map/all_to_all | solution.py:316
  99.1 6.8 %all-to-all-done.3.in_ref = bf16[8,24,640]{2,1,0:T(8,128)(2,1)S(1)} async-done(((bf16[8,24,640]{2,1,0:T(8,128)(2,1)}), bf16[8,24,640]{2,1,0:T(8,128)(2,1)S(1)}, u32[]{:S(2)}, u32[]{:S(2)}) %all-to-all-start.3) | async-done | bytes 245792 | tf_op jit(solution)/shard_map/all_to_all | solution.py:316
  106.9 1.2 collective-permute-start.2
  108.1 2.1 %collective-permute-start.3 = (bf16[160,640]{1,0:T(8,128)(2,1)S(1)}, bf16[160,640]{1,0:T(8,128)(2,1)S(1)}, u32[]{:S(2)}, u32[]{:S(2)}) collective-permute-start(bf16[160,640]{1,0:T(8,128)(2,1)S(1)} %shard_map.159.refs_0_), channel_id=1, source_target_pairs={{0,12},{1,13},{2,14},{3,15},{4,8},{5,9},{6,10},{7,11},{8,4},{9,5},... | collective-permute-start | bytes 614408 | tf_op jit(solution)/shard_map/ppermute | solution.py:308
  111.0 3.7 %collective-permute-done.2 = bf16[160,640]{1,0:T(8,128)(2,1)S(1)} collective-permute-done((bf16[160,640]{1,0:T(8,128)(2,1)S(1)}, bf16[160,640]{1,0:T(8,128)(2,1)S(1)}, u32[]{:S(2)}, u32[]{:S(2)}) %collective-permute-start.2) | collective-permute-done | bytes 204832 | tf_op jit(solution)/shard_map/ppermute | solution.py:308
  114.7 3.6 %collective-permute-done.3 = bf16[160,640]{1,0:T(8,128)(2,1)S(1)} collective-permute-done((bf16[160,640]{1,0:T(8,128)(2,1)S(1)}, bf16[160,640]{1,0:T(8,128)(2,1)S(1)}, u32[]{:S(2)}, u32[]{:S(2)}) %collective-permute-start.3) | collective-permute-done | bytes 204832 | tf_op jit(solution)/shard_map/ppermute | solution.py:308
  118.4 2.5 %collective-permute-start.5 = (bf16[3,160,640]{2,1,0:T(8,128)(2,1)S(1)}, bf16[3,160,640]{2,1,0:T(8,128)(2,1)}, u32[]{:S(2)}, u32[]{:S(2)}) collective-permute-start(bf16[3,160,640]{2,1,0:T(8,128)(2,1)S(1)} %pad_maximum_fusion.refs_1_), channel_id=1, source_target_pairs={{0,1},{1,0},{2,3},{3,2},{4,5},{5,4},{6,7},{7,6},{8,9},{9,8},{10,11... | collective-permute-start | bytes 1843208 | tf_op jit(solution)/shard_map/ppermute | solution.py:308
  124.0 1.1 copy-done.6
  125.8 10.8 %shard_map.161.refs_0_ = bf16[20,80,128]{2,1,0:T(8,128)(2,1)S(1)} custom-call(s32[1]{0:T(128)} %bitcast.me_ref, f32[4]{0:T(128)S(1)} %copy-done.9, bf16[5,640,128]{2,1,0:T(8,128)(2,1)S(1)} %get-tuple-element.35.q_ref, bf16[5,128,640]{2,1,0:T(8,128)(2,1)S(1)} %get-tuple-element.36.k_ref, bf16[5,640,256]{2,1,0:T(8,128)(2,1)S(1)} %get-tuple-element.37.v_ref, ...), custom_call_target="tpu_custom_call" | custom-call | flops 3145728000 | bytes 8388608 | tf_op jit(solution)/shard_map/pallas_call | solution.py:333
  137.6 1.7 collective-permute-done.8.refs_3_
  139.2 10.3 %shard_map.162.refs_1_ = bf16[20,80,128]{2,1,0:T(8,128)(2,1)S(1)} custom-call(s32[1]{0:T(128)} %bitcast.me_ref, f32[4]{0:T(128)S(1)} %copy-done.9, bf16[5,640,128]{2,1,0:T(8,128)(2,1)S(1)} %get-tuple-element.35.q_ref, bf16[5,128,640]{2,1,0:T(8,128)(2,1)S(1)} %get-tuple-element.36.k_ref, bf16[5,640,256]{2,1,0:T(8,128)(2,1)S(1)} %get-tuple-element.37.v_ref, ...), custom_call_target="tpu_custom_call" | custom-call | flops 3145728000 | bytes 8388608 | tf_op jit(solution)/shard_map/pallas_call | solution.py:333
  149.6 17.1 %all_to_all.26.in_ref = bf16[40,80,128]{2,1,0:T(8,128)(2,1)S(1)} all-to-all(bf16[40,80,128]{2,1,0:T(8,128)(2,1)S(1)} %shard_map.163), channel_id=1, replica_groups=mesh['row'=8,'col'=16] {'row'}, dimensions={0} | all-to-all | bytes 1638400 | tf_op jit(solution)/shard_map/all_to_all | solution.py:357
  166.7 1.3 shard_map.164
  (82 shorter events, 11.5 us)
Async XLA Ops:
  1.1 9.2 %copy-start.17 = (f32[128]{0:T(128)S(1)}, f32[128]{0:T(128)}, u32[]{:S(2)}) copy-start(f32[128]{0:T(128)} %param.19) | copy-start | bytes 1540
  1.2 9.2 %copy-start.18 = (f32[128]{0:T(128)S(1)}, f32[128]{0:T(128)}, u32[]{:S(2)}) copy-start(f32[128]{0:T(128)} %param.20) | copy-start | bytes 1540
  1.2 9.2 %copy-start.19 = (f32[128]{0:T(128)S(1)}, f32[128]{0:T(128)}, u32[]{:S(2)}) copy-start(f32[128]{0:T(128)} %param.23) | copy-start | bytes 1540
  1.2 9.2 %copy-start.20 = (f32[128]{0:T(128)S(1)}, f32[128]{0:T(128)}, u32[]{:S(2)}) copy-start(f32[128]{0:T(128)} %param.24) | copy-start | bytes 1540
  2.4 19.2 %all-to-all-start = ((bf16[40,80,128]{2,1,0:T(8,128)(2,1)}), bf16[40,80,128]{2,1,0:T(8,128)(2,1)S(1)}, u32[]{:S(2)}, u32[]{:S(2)}) async-start(bf16[40,80,128]{2,1,0:T(8,128)(2,1)} %shard_map.154), calls=%async_computation | async-start | bytes 1638400 | tf_op jit(solution)/shard_map/all_to_all | solution.py:264
  10.1 50.8 %copy-start.13 = (f32[640]{0:T(1024)}, f32[640]{0:T(1024)S(1)}, u32[]{:S(2)}) copy-start(f32[640]{0:T(1024)S(1)} %convert_element_type.36) | copy-start | bytes 7684
  65.0 23.8 %all-to-all-start.2 = ((bf16[128,32,128]{2,1,0:T(8,128)(2,1)}), bf16[128,32,128]{2,1,0:T(8,128)(2,1)S(1)}, u32[]{:S(2)}, u32[]{:S(2)}) async-start(bf16[128,32,128]{2,1,0:T(8,128)(2,1)} %shard_map.156), calls=%async_computation.2 | async-start | bytes 2097152 | tf_op jit(solution)/shard_map/all_to_all | solution.py:288
  94.8 26.2 %copy-start.10 = (bf16[128,512]{1,0:T(8,128)(2,1)S(1)}, bf16[128,512]{1,0:T(8,128)(2,1)}, u32[]{:S(2)}) copy-start(bf16[128,512]{1,0:T(8,128)(2,1)} %param.28) | copy-start | bytes 393220
  94.8 26.3 %copy-start.15 = (s32[10]{0:T(128)S(1)}, s32[10]{0:T(128)}, u32[]{:S(2)}) copy-start(s32[10]{0:T(128)} %param.17) | copy-start | bytes 124
  94.8 27.2 %slice-start = ((bf16[128,512]{1,0:T(8,128)(2,1)}), bf16[128,256]{1,0:T(8,128)(2,1)S(1)}, s32[]{:S(2)}) async-start(bf16[128,512]{1,0:T(8,128)(2,1)} %param.28), calls=%async_computation.5 | async-start | bytes 131072 | tf_op jit(solution)/shard_map/slice | solution.py:322
  94.8 27.8 %copy-start.2 = (bf16[5,640,128]{2,1,0:T(8,128)(2,1)S(1)}, bf16[5,640,128]{2,1,0:T(8,128)(2,1)}, u32[]{:S(2)}) copy-start(bf16[5,640,128]{2,1,0:T(8,128)(2,1)} %copy-done.1) | copy-start | bytes 2457604
  94.8 11.1 %all-to-all-start.3 = ((bf16[8,24,640]{2,1,0:T(8,128)(2,1)}), bf16[8,24,640]{2,1,0:T(8,128)(2,1)S(1)}, u32[]{:S(2)}, u32[]{:S(2)}) async-start(bf16[8,24,640]{2,1,0:T(8,128)(2,1)} %copy-done.3), calls=%async_computation.3 | async-start | bytes 491520 | tf_op jit(solution)/shard_map/all_to_all | solution.py:316
  99.1 24.7 %copy-start.14 = (f32[640]{0:T(1024)S(1)}, f32[640]{0:T(1024)}, u32[]{:S(2)}) copy-start(f32[640]{0:T(1024)} %copy-done.13) | copy-start | bytes 7684
  106.1 17.8 %copy-start.9 = (f32[4]{0:T(128)S(1)}, f32[4]{0:T(128)}, u32[]{:S(2)}) copy-start(f32[4]{0:T(128)} %inter_ref.3) | copy-start | bytes 52
  106.1 4.9 %collective-permute-start.1 = (bf16[160,640]{1,0:T(8,128)(2,1)S(1)}, bf16[160,640]{1,0:T(8,128)(2,1)S(1)}, u32[]{:S(2)}, u32[]{:S(2)}) collective-permute-start(bf16[160,640]{1,0:T(8,128)(2,1)S(1)} %shard_map.159.refs_0_), channel_id=1, source_target_pairs={{0,4},{1,5},{2,6},{3,7},{4,0},{5,1},{6,2},{7,3},{8,12},{9,13},{10,... | collective-permute-start | bytes 614408 | tf_op jit(solution)/shard_map/ppermute | solution.py:308
  106.9 7.8 %collective-permute-start.2 = (bf16[160,640]{1,0:T(8,128)(2,1)S(1)}, bf16[160,640]{1,0:T(8,128)(2,1)S(1)}, u32[]{:S(2)}, u32[]{:S(2)}) collective-permute-start(bf16[160,640]{1,0:T(8,128)(2,1)S(1)} %shard_map.159.refs_0_), channel_id=1, source_target_pairs={{0,8},{1,9},{2,10},{3,11},{4,12},{5,13},{6,14},{7,15},{8,0},{9,1},... | collective-permute-start | bytes 614408 | tf_op jit(solution)/shard_map/ppermute | solution.py:308
  108.1 10.2 %collective-permute-start.3 = (bf16[160,640]{1,0:T(8,128)(2,1)S(1)}, bf16[160,640]{1,0:T(8,128)(2,1)S(1)}, u32[]{:S(2)}, u32[]{:S(2)}) collective-permute-start(bf16[160,640]{1,0:T(8,128)(2,1)S(1)} %shard_map.159.refs_0_), channel_id=1, source_target_pairs={{0,12},{1,13},{2,14},{3,15},{4,8},{5,9},{6,10},{7,11},{8,4},{9,5},... | collective-permute-start | bytes 614408 | tf_op jit(solution)/shard_map/ppermute | solution.py:308
  110.3 8.1 %collective-permute-start.4 = (bf16[160,640]{1,0:T(8,128)(2,1)S(1)}, bf16[160,640]{1,0:T(8,128)(2,1)S(1)}, u32[]{:S(2)}, u32[]{:S(2)}) collective-permute-start(bf16[160,640]{1,0:T(8,128)(2,1)S(1)} %shard_map.159.refs_0_), channel_id=1, source_target_pairs={{0,2},{1,3},{2,0},{3,1},{4,6},{5,7},{6,4},{7,5},{8,10},{9,11},{10,... | collective-permute-start | bytes 614408 | tf_op jit(solution)/shard_map/ppermute | solution.py:308
  118.4 5.4 %collective-permute-start.5 = (bf16[3,160,640]{2,1,0:T(8,128)(2,1)S(1)}, bf16[3,160,640]{2,1,0:T(8,128)(2,1)}, u32[]{:S(2)}, u32[]{:S(2)}) collective-permute-start(bf16[3,160,640]{2,1,0:T(8,128)(2,1)S(1)} %pad_maximum_fusion.refs_1_), channel_id=1, source_target_pairs={{0,1},{1,0},{2,3},{3,2},{4,5},{5,4},{6,7},{7,6},{8,9},{9,8},{10,11... | collective-permute-start | bytes 1843208 | tf_op jit(solution)/shard_map/ppermute | solution.py:308
  121.3 15.5 %collective-permute-start.7 = (bf16[3,160,640]{2,1,0:T(8,128)(2,1)S(1)}, bf16[3,160,640]{2,1,0:T(8,128)(2,1)S(1)}, u32[]{:S(2)}, u32[]{:S(2)}) collective-permute-start(bf16[3,160,640]{2,1,0:T(8,128)(2,1)S(1)} %pad_maximum_fusion.refs_1_), channel_id=1, source_target_pairs={{0,2},{1,3},{2,0},{3,1},{4,6},{5,7},{6,4},{7,5},{8,10},{9,11},{10,... | collective-permute-start | bytes 1843208 | tf_op jit(solution)/shard_map/ppermute | solution.py:308
  121.9 1.6 collective-permute-start
  122.3 1.5 collective-permute-start.6
  125.8 13.4 %copy-start.7 = (bf16[5,640,128]{2,1,0:T(8,128)(2,1)S(1)}, bf16[5,640,128]{2,1,0:T(8,128)(2,1)}, u32[]{:S(2)}) copy-start(bf16[5,640,128]{2,1,0:T(8,128)(2,1)} %copy-done.5) | copy-start | bytes 2457604
  136.8 2.5 %collective-permute-start.8 = (bf16[3,160,640]{2,1,0:T(8,128)(2,1)S(1)}, bf16[3,160,640]{2,1,0:T(8,128)(2,1)S(1)}, u32[]{:S(2)}, u32[]{:S(2)}) collective-permute-start(bf16[3,160,640]{2,1,0:T(8,128)(2,1)S(1)} %collective-permute-done.7.refs_1_), channel_id=1, source_target_pairs={{0,1},{1,0},{2,3},{3,2},{4,5},{5,4},{6,7},{7,6},{8,9},{9,8},{10,11... | collective-permute-start | bytes 1843208 | tf_op jit(solution)/shard_map/ppermute | solution.py:308
  (13 other events, 54.3 us)

commit v3 on v2

v3 whole, which is shorter than its diff:
```python
import functools

import jax
import jax.numpy as jnp
from jax import lax
from jax.experimental import pallas as pl
from jax.experimental.pallas import tpu as pltpu
from jax.sharding import PartitionSpec as P

H = 4
DH = 32
MB = 64
C = 128
N = 640
ROWS = 8
COLS = 16
RI = N // ROWS
CJ = N // COLS
T = CJ // ROWS
SEND = 56
BACK = 32
G = RI // 16
A = CJ // 8
TURN = T * RI
PAY = 112
GROUP = 2
CHUNK = GROUP * RI

MASK_NEG = 10000.0
EPS = 1e-05

F32 = jnp.float32
BF16 = jnp.bfloat16
VMEM = pl.BlockSpec(memory_space=pltpu.VMEM)
SMEM = pl.BlockSpec(memory_space=pltpu.SMEM)


def dot(a, b, over):
    return lax.dot_general(a, b, (over, ((), ())), preferred_element_type=F32)


def layer_norm(values, gain, shift, axis=-1):
    middle = jnp.mean(values, axis=axis, keepdims=True)
    centred = values - middle
    spread = jnp.mean(centred * centred, axis=axis, keepdims=True)
    return centred * lax.rsqrt(spread + EPS) * gain + shift


def sigmoid(x):
    return 0.5 * jnp.tanh(0.5 * x) + 0.5


def call(kernel, out_shape, scratch, specs, cost=None, mib=24):
    return pl.pallas_call(
        kernel,
        out_shape=out_shape,
        in_specs=specs,
        out_specs=jax.tree.map(lambda _: VMEM, out_shape),
        scratch_shapes=scratch,
        compiler_params=pltpu.CompilerParams(vmem_limit_bytes=mib * 1024 * 1024),
        cost_estimate=cost,
    )


def struct(shape, dtype=BF16):
    return jax.ShapeDtypeStruct(shape, dtype)


def swap_groups(arrays):
    arrays = list(arrays)
    group = lax.broadcasted_iota(jnp.int32, arrays[0].shape, 1) // 16
    for bit in (1, 2, 4):
        high = (group & bit) != 0
        for p in range(8):
            if not p & bit:
                one, two = arrays[p], arrays[p | bit]
                arrays[p] = jnp.where(high, pltpu.roll(two, 16 * bit, 1), one)
                arrays[p | bit] = jnp.where(high, two, pltpu.roll(one, C - 16 * bit, 1))
    return arrays


def turn_back_kernel(in_ref, out_ref, wide):
    for j in range(CJ):
        wide[pl.ds(j, RI, stride=CJ), :] = in_ref[j].astype(F32)
    out_ref[...] = wide[...].reshape(RI, CJ, C).astype(BF16)


def project_kernel(
    pair_hbm, valid_hbm, gain_hbm, bias_hbm, w_hbm, out_ref, x_ref,
    pair_ref, valid_ref, gain_ref, bias_ref, w_ref, pairs, wide, sems,
):
    copies = [
        pltpu.make_async_copy(source, target, sems.at[n])
        for n, (source, target) in enumerate(
            (
                (pair_hbm, pair_ref),
                (valid_hbm, valid_ref),
                (gain_hbm, gain_ref),
                (bias_hbm, bias_ref),
                (w_hbm, w_ref),
            )
        )
    ]
    for copy in copies:
        copy.start()
    wide[...] = jnp.zeros_like(wide)
    for copy in copies:
        copy.wait()
    pairs[...] = pair_ref[...].astype(F32).reshape(RI * CJ, C)
    weight = w_ref[...].T
    for a in range(A):
        x = jnp.concatenate(
            [
                pairs[pl.ds(16 * g * CJ + 8 * a + b, 16, stride=CJ), :]
                for g in range(G)
                for b in range(8)
            ],
            axis=0,
        )
        x_ref[a] = x.astype(BF16)
        normed = layer_norm(x, gain_ref[...][None, :], bias_ref[...][None, :]).astype(BF16)
        proj = dot(weight, normed, ((1,), (1,)))
        valid_j = valid_ref[(lax.axis_index("col") * A + a) // (MB // 8)]
        for g in range(G):
            lanes = slice(g * C, (g + 1) * C)
            mask = (valid_ref[(lax.axis_index("row") * G + g) // (MB // 16)] * valid_j).astype(F32)
            for side in range(2):
                gate = proj[2 * side * C : (2 * side + 1) * C, lanes]
                value = proj[(2 * side + 1) * C : (2 * side + 2) * C, lanes]
                wide[pl.ds((side * A + a) * G + g, C, stride=SEND), :] = mask * sigmoid(gate) * value
    out_ref[...] = wide[...].reshape(C, SEND, C).astype(BF16)


def gate_kernel(x_ref, norms_ref, w_ref, out_ref):
    for a in range(A):
        x = x_ref[a].astype(F32)
        normed = layer_norm(x, norms_ref[0:1], norms_ref[1:2]).astype(BF16)
        out_ref[a] = sigmoid(dot(normed, w_ref[...], ((1,), (0,))))


def product_kernel(in_ref, out_ref, wide, left, right, prod, back):
    wide[...] = in_ref[...].astype(F32).reshape(C * SEND, C)
    for side, matrix in enumerate((left, right)):
        for a in range(A):
            rows = [
                wide[pl.ds((side * A + a) * G + g, C, stride=SEND), :].astype(BF16) for g in range(G)
            ]
            parts = swap_groups(
                [
                    jnp.concatenate([row[r * COLS : (r + 1) * COLS] for row in rows], axis=0)
                    for r in range(ROWS)
                ]
            )
            for b in range(8):
                first = (a * 8 + b) * COLS
                for g in range(G):
                    matrix[first : first + COLS, g * C : (g + 1) * C] = parts[b][
                        g * COLS : (g + 1) * COLS
                    ]
    back[...] = jnp.zeros_like(back)
    for g in range(G):
        prod[g] = dot(right[...], left[:, g * C : (g + 1) * C], ((0,), (0,)))
    for g in range(G):
        for half in range(2):
            firsts = [s // 2 * C + s % 2 * 8 for s in range(half * A, half * A + A)]
            parts = swap_groups(
                [
                    jnp.concatenate(
                        [prod[g, pl.ds(first + b, ROWS, stride=16), :] for first in firsts], axis=0
                    )
                    for b in range(8)
                ]
            )
            for r in range(ROWS):
                for a in range(A):
                    row = (r * COLS + half) * BACK + a * G + g
                    back[pl.ds(row, ROWS, stride=2 * BACK), :] = parts[r][a * ROWS : (a + 1) * ROWS]
    out_ref[...] = back[...].reshape(C, BACK, C).astype(BF16)


def middle_kernel(in_ref, x_ref, gate_ref, norms_ref, w_ref, out_ref, wide, pay):
    wide[...] = in_ref[...].astype(F32).reshape(C * BACK, C)
    pay[...] = jnp.zeros_like(pay)
    gain = jnp.broadcast_to(norms_ref[2:3], (C, C)).T[:, :1]
    bias = jnp.broadcast_to(norms_ref[3:4], (C, C)).T[:, :1]
    for a in range(A):
        prod = jnp.concatenate(
            [wide[pl.ds(a * G + g, C, stride=BACK), :] for g in range(G)], axis=1
        )
        normed = layer_norm(prod, gain, bias, 0).astype(BF16)
        update = dot(normed, w_ref[:C], ((0,), (0,)))
        mid = (x_ref[a].astype(F32) + gate_ref[a] * update).astype(BF16)
        for g in range(G):
            for b in range(8):
                r, t = divmod(8 * a + b, T)
                out_ref[r, t * RI + 16 * g : t * RI + 16 * g + 16, :] = mid[
                    (g * 8 + b) * 16 : (g * 8 + b + 1) * 16
                ]
        att = layer_norm(mid.astype(F32), norms_ref[4:5], norms_ref[5:6]).astype(BF16)
        rows = dot(w_ref[C:], att, ((1,), (1,)))
        for g in range(G):
            first = (a * G + g) * H
            pay[first : first + H, :] = rows[:H, g * C : (g + 1) * C]
    for r in range(ROWS):
        out_ref[r, TURN:, :] = pay[...].astype(BF16)


def qkvg_kernel(in_ref, norms_ref, wqg_ref, wv_ref, wk_ref, q_ref, k_ref, v_ref, g_ref):
    for t in range(T):
        mid = jnp.concatenate([in_ref[r, t * RI : (t + 1) * RI, :] for r in range(ROWS)], axis=0)
        att = layer_norm(mid.astype(F32), norms_ref[4:5], norms_ref[5:6]).astype(BF16)
        keyed = jnp.concatenate(
            [att[r * RI + 16 * g : r * RI + 16 * g + 16] for g in range(G) for r in range(ROWS)], axis=0
        )
        qg = dot(att, wqg_ref[...], ((1,), (0,)))
        q_ref[t] = (qg[:, :C] * DH ** (-0.5)).astype(BF16)
        g_ref[t] = sigmoid(qg[:, C:])
        vals = dot(keyed, wv_ref[...], ((1,), (0,))).astype(BF16)
        v_ref[t] = jnp.concatenate([vals, jnp.ones((N, C), BF16)], axis=1)
        k_ref[t] = dot(wk_ref[...], keyed, ((1,), (1,))).astype(BF16)


def merge_kernel(in_ref, out_ref, parts, rows):
    for b, part in enumerate(swap_groups([in_ref[r, TURN:, :].astype(F32) for r in range(ROWS)])):
        parts[b] = part
    for b in range(8):
        for g in range(G):
            for h in range(H):
                rows[g, pl.ds(h * CJ + b, A, stride=8), :] = parts[b, pl.ds(g * H + h, A, stride=G * H), :]
    out_ref[...] = jnp.concatenate([rows[g] for g in range(G)], axis=1).astype(BF16)


def attend_kernel(
    steps, me_ref, inter_ref, q_ref, k_ref, v_ref, g_ref, mid_ref, cross_ref, key_ref, valid_ref, valid_t_ref, wo_ref,
    *refs,
):
    parts, (out_ref, extra, score_a, score_b, power_a, power_b) = refs[: 2 * GROUP], refs[2 * GROUP :]
    score, power = (score_a, score_b), (power_a, power_b)
    me = me_ref[0]
    chips = [(me // 2) ^ step for step in steps]
    for n in range(GROUP):
        for other in range(2):
            core = (me % 2) ^ other
            first = chips[n] * RI + core * CJ
            part = parts[other * GROUP + n]
            for s in range(CJ // 8):
                to = pl.multiple_of(n * RI + core * CJ + 8 * s, 8)
                crossing = cross_ref[pl.ds((first + 8 * s) // MB, 1), :]
                for h in range(H):
                    extra[h, pl.ds(to, 8), :] = (
                        part[h * CJ + 8 * s : h * CJ + 8 * s + 8, :].astype(F32)
                        + inter_ref[h] * crossing
                        + key_ref[...]
                    )
    lane_head = lax.broadcasted_iota(jnp.int32, (CHUNK, C), 1) // DH

    def rows_of(take):
        return jnp.concatenate([take(pl.ds(pl.multiple_of(chip * RI, RI), RI)) for chip in chips], axis=0)

    valid = rows_of(lambda rows: valid_ref[rows, :])

    def one_column(t, carry):
        queries = rows_of(lambda rows: q_ref[t, rows, :])

        def set_score(h):
            own = jnp.where(lane_head == h, queries, jnp.zeros_like(queries))
            score[h % 2][...] = dot(own, k_ref[t], ((1,), (0,))) + extra[h]

        total = jnp.zeros((CHUNK, C), F32)
        set_score(0)
        for h in range(H + 1):
            if h + 1 < H:
                set_score(h + 1)
            if h > 0:
                sums = dot(power[(h - 1) % 2][...], v_ref[t], ((1,), (0,)))
                total = jnp.where(lane_head == h - 1, sums[:, :C] / sums[:, C:], total)
            if h < H:
                now = score[h % 2][...]
                highest = jnp.max(now, axis=1, keepdims=True)
                power[h % 2][...] = jnp.exp(now - highest).astype(BF16)
        gated = (rows_of(lambda rows: g_ref[t, rows, :]) * total).astype(BF16)
        update = dot(gated, wo_ref[...], ((1,), (0,)))
        own = pl.ds(pl.multiple_of(t * RI, RI), RI)
        mid = jnp.concatenate([mid_ref[chip, own, :] for chip in chips], axis=0).astype(F32)
        out = (mid + valid * valid_t_ref[t] * update).astype(BF16)
        for n in range(GROUP):
            out_ref[n * T + t] = out[n * RI : (n + 1) * RI]
        return carry

    lax.fori_loop(0, T, one_column, 0)


def order_kernel(me_ref, *refs):
    out_ref = refs[-1]
    for step in range(ROWS):
        chip = (me_ref[0] // 2) ^ step
        for t in range(T):
            out_ref[chip * T + t] = refs[step % 2 * 2 + step // 4][step % 4 // 2 * T + t]


def on_device(
    pair,
    block_chain,
    block_valid,
    tri_norm_gain,
    tri_norm_bias,
    tri_in_weight,
    tri_gate_weight,
    out_norm_gain,
    out_norm_bias,
    tri_out_weight,
    att_norm_gain,
    att_norm_bias,
    qkvg_weight,
    bias_weight,
    inter_chain,
    att_out_weight,
):
    row_at, col_at = lax.axis_index("row"), lax.axis_index("col")
    both = ("row", "col")
    residue_valid = jnp.repeat(block_valid, MB).astype(F32)
    norms = jnp.stack(
        [tri_norm_gain, tri_norm_bias, out_norm_gain, out_norm_bias, att_norm_gain, att_norm_bias]
    )

    parcels, x = call(
        project_kernel,
        [struct((C, SEND, C)), struct((A, N, C))],
        [
            pltpu.VMEM((RI, CJ, C), BF16),
            pltpu.SMEM((N // MB,), jnp.int32),
            pltpu.VMEM((C,), F32),
            pltpu.VMEM((C,), F32),
            pltpu.VMEM((C, 4 * C), BF16),
            pltpu.VMEM((RI * CJ, C), F32),
            pltpu.VMEM((C * SEND, C), F32),
            pltpu.SemaphoreType.DMA((5,)),
        ],
        [pl.BlockSpec(memory_space=pl.ANY)] * 5,
        mib=60,
    )(pair, block_valid, tri_norm_gain, tri_norm_bias, tri_in_weight)
    gate = call(gate_kernel, struct((A, N, C), F32), [], [VMEM] * 3)(x, norms, tri_gate_weight)
    channel = lax.all_to_all(parcels, both, 0, 0, tiled=True)
    product = call(
        product_kernel,
        struct((C, BACK, C)),
        [
            pltpu.VMEM((C * SEND, C), F32),
            pltpu.VMEM((N, N), BF16),
            pltpu.VMEM((N, N), BF16),
            pltpu.VMEM((G, N, C), F32),
            pltpu.VMEM((C * BACK, C), F32),
        ],
        [VMEM],
    )(channel)
    returned = lax.all_to_all(product, both, 0, 0, tiled=True)

    w_mid = jnp.concatenate([tri_out_weight, jnp.pad(bias_weight.T, ((0, 8 - H), (0, 0)))])
    turned = call(
        middle_kernel,
        struct((ROWS, TURN + PAY, C)),
        [pltpu.VMEM((C * BACK, C), F32), pltpu.VMEM((PAY, C), F32)],
        [VMEM] * 5,
    )(returned, x, gate, norms, w_mid)
    mid = lax.all_to_all(turned, "row", 0, 0, tiled=True)

    valid_t = lax.dynamic_slice_in_dim(residue_valid, (col_at * ROWS + row_at) * T, T)
    valid_rows = jnp.broadcast_to(residue_valid[:, None], (N, C))

    def keyed(values):
        return values.reshape(ROWS, G, 16).transpose(1, 0, 2).reshape(N)

    cross = (block_chain[:, None] != keyed(jnp.repeat(block_chain, MB))[None, :]).astype(F32)
    key_mask = (MASK_NEG * (keyed(residue_valid) - 1.0))[None, :]

    def swap(values, row_xor, col_xor):
        pairs = [
            (r * COLS + c, (r ^ row_xor) * COLS + (c ^ col_xor))
            for r in range(ROWS)
            for c in range(COLS)
        ]
        return lax.ppermute(values, both, pairs)

    merged = call(
        merge_kernel,
        struct((H * CJ, N)),
        [pltpu.VMEM((ROWS, PAY, C), F32), pltpu.VMEM((G, H * CJ, C), F32)],
        [VMEM],
    )(mid)
    hold = lax.optimization_barrier
    one, two, three, beside = [swap(merged, 0, step) for step in (4, 8, 12, 2)]

    wqg = jnp.concatenate([qkvg_weight[:, :C], qkvg_weight[:, 3 * C :]], axis=1)
    q, k, v, g = call(
        qkvg_kernel,
        [struct((T, N, C)), struct((T, C, N)), struct((T, N, 2 * C)), struct((T, N, C), F32)],
        [],
        [VMEM] * 5,
    )(mid, norms, wqg, qkvg_weight[:, 2 * C : 3 * C], qkvg_weight[:, C : 2 * C].T)

    def attend(steps, *parts):
        return call(
            functools.partial(attend_kernel, tuple(steps)),
            struct((GROUP * T, RI, C)),
            [pltpu.VMEM((H, CHUNK, N), F32)]
            + [pltpu.VMEM((CHUNK, N), F32)] * 2
            + [pltpu.VMEM((CHUNK, N), BF16)] * 2,
            [SMEM, SMEM] + [VMEM] * 8 + [SMEM, VMEM] + [VMEM] * (2 * GROUP),
            pl.CostEstimate(flops=1 << 20, bytes_accessed=1 << 16, transcendentals=0),
        )(
            col_at[None], inter_chain, q, k, v, g, mid, cross, key_mask, valid_rows, valid_t, att_out_weight,
            *parts,
        )

    def core(values):
        return swap(values, 0, 1)

    one_across = swap(one, 0, 2)
    merged, near, merged2, near2, q, k, v, g = hold((merged, one, core(merged), core(one), q, k, v, g))
    outs = [attend((0, 2), merged, near, merged2, near2)]
    outs[0], two, three, beside, one_across = hold((outs[0], two, three, beside, one_across))
    two_across, three_across = swap(two, 0, 2), swap(three, 0, 2)
    two, three, two2, three2, beside2, one_across2 = hold(
        (two, three, core(two), core(three), core(beside), core(one_across))
    )
    outs.append(attend((4, 6), two, three, two2, three2))
    outs[1], two_across = hold((outs[1], two_across))
    two_across2 = core(two_across)
    outs.append(attend((1, 3), beside, one_across, beside2, one_across2))
    outs[2], three_across, two_across2 = hold((outs[2], three_across, two_across2))
    outs.append(attend((5, 7), two_across, three_across, two_across2, core(three_across)))
    out = call(order_kernel, struct((CJ, RI, C)), [], [SMEM] + [VMEM] * 4)(col_at[None], *outs)
    home = lax.all_to_all(out, "row", 0, 0, tiled=True)
    return call(turn_back_kernel, struct((RI, CJ, C)), [pltpu.VMEM((RI * CJ, C), F32)], [VMEM])(home)


def solution(mesh):
    placed = (P("row", "col", None),) + (P(),) * 15
    return jax.shard_map(
        on_device, mesh=mesh, in_specs=placed, out_specs=P("row", "col", None), check_vma=False
    )
```

time: 169 us -> 160 us (0.947)
  waiting for transfers between devices: 43.3 us -> 32.3 us
  Pallas kernels: 36.6 us -> 45.2 us
  local copies, waits for them, and re-layouts: 7.19 us -> 1.36 us
  blocking collectives: 53.4 us -> 57.6 us
  starting transfers between devices: 25.8 us -> 22.4 us
    all_to_all x3 -> x2, starting transfers between devices: 16.4 us -> 8.51 us  [the longest x1 4.82 us: on_device(): returned = lax.all_to_all(product, both, 0, 0, tiled=True)]
    ppermute x9 -> x15, waiting for transfers between devices: 9.36 us -> 1.92 us  [swap(): return lax.ppermute(values, both, pairs)]
    unnamed x50 -> x29, local copies, waits for them, and re-layouts: 6.58 us -> 0.18 us
    ppermute x9 -> x15, starting transfers between devices: 9.36 us -> 13.9 us  [swap(): return lax.ppermute(values, both, pairs)]
    all_to_all x3 -> x2, waiting for transfers between devices: 34 us -> 30.4 us  [the longest x1 17.1 us: on_device(): returned = lax.all_to_all(product, both, 0, 0, tiled=True)]
    pallas_call x1, Pallas kernels: 4.05 us -> 7.16 us  [on_device(): call(product_kernel, struct((C, BACK, C)), [pltpu.VMEM((C * SEND, C), F32...]
    pallas_call x2 -> x4, Pallas kernels: 21.1 us -> 24.2 us  [attend(): call(functools.partial(attend_kernel, tuple(steps)), struct((GROUP * T, R...]
    all_to_all x1, blocking collectives: 36.3 us -> 39 us  [on_device(): channel = lax.all_to_all(parcels, both, 0, 0, tiled=True)]
  transfers between devices with their start and end apart: 12 -> 17, of which waited for: 9 -> 5; matrix products, arithmetic and copies ran while one was open for 1% -> 1% of each run, Pallas kernels for 8% -> 13%
where the time goes in v3:
time: 160 us
  blocking collectives  57.6 us (36%)
  Pallas kernels  45.2 us (28%)
  waiting for transfers between devices  32.3 us (20%)
  starting transfers between devices  22.4 us (14%)
    all_to_all x1, blocking collectives, on_device(): channel = lax.all_to_all(parcels, both, 0, 0, tiled=True)  39 us
    pallas_call x4, Pallas kernels, attend(): call(functools.partial(attend_kernel, tuple(steps)), struct((GROUP * T, R...  24.2 us
    all_to_all x1, blocking collectives, on_device(): home = lax.all_to_all(out, 'row', 0, 0, tiled=True)  18.6 us
    all_to_all x1, waiting for transfers between devices, on_device(): returned = lax.all_to_all(product, both, 0, 0, tiled=True)  17.1 us
    ppermute x15, starting transfers between devices, swap(): return lax.ppermute(values, both, pairs)  13.9 us
    all_to_all x1, waiting for transfers between devices, on_device(): mid = lax.all_to_all(turned, 'row', 0, 0, tiled=True)  13.2 us
    pallas_call x1, Pallas kernels, on_device(): call(product_kernel, struct((C, BACK, C)), [pltpu.VMEM((C * SEND, C), F32...  7.16 us
    pallas_call x1, Pallas kernels, on_device(): call(project_kernel, [struct((C, SEND, C)), struct((A, N, C))], [pltpu.VM...  4.86 us
  transfers between devices with their start and end apart: 17, of which 5 were waited for; matrix products, arithmetic and copies ran while one was open for 1% of the time, Pallas kernels for 13%

profile of v3, /device:TPU:1, one launch (start us, length us, event | category | flops | bytes accessed | tf_op | source)
XLA Modules:
  0.0 160.1 jit_solution(11396238200112013880)
XLA Ops:
  0.0 4.9 %shard_map.154 = (bf16[128,56,128]{2,1,0:T(8,128)(2,1)}, bf16[5,640,128]{2,1,0:T(8,128)(2,1)}) custom-call(bf16[80,40,128]{2,1,0:T(8,128)(2,1)} %pair_hbm.1, s32[10]{0:T(128)} %valid_hbm.1, f32[128]{0:T(128)} %gain_hbm.1, f32[128]{0:T(128)} %bias_hbm.1, bf16[128,512]{1,0:T(8,128)(2,1)} %w_hbm.1), custom_call_target="tpu_custom_call" | custom-call | tf_op jit(solution)/shard_map/pallas_call | solution.py:326
  4.9 39.0 %all_to_all.20.in_ref = bf16[128,56,128]{2,1,0:T(8,128)(2,1)S(1)} all-to-all(bf16[128,56,128]{2,1,0:T(8,128)(2,1)} %get-tuple-element.35), channel_id=1, replica_groups=mesh['row'=8,'col'=16] {'row','col'}, dimensions={0} | all-to-all | bytes 3670016 | tf_op jit(solution)/shard_map/all_to_all | solution.py:343
  43.9 7.2 %shard_map.155 = bf16[128,32,128]{2,1,0:T(8,128)(2,1)} custom-call(bf16[128,56,128]{2,1,0:T(8,128)(2,1)S(1)} %all_to_all.20.in_ref), custom_call_target="tpu_custom_call" | custom-call | tf_op jit(solution)/shard_map/pallas_call | solution.py:344
  51.1 4.8 %all-to-all-start.1 = ((bf16[128,32,128]{2,1,0:T(8,128)(2,1)}), bf16[128,32,128]{2,1,0:T(8,128)(2,1)S(1)}, u32[]{:S(2)}, u32[]{:S(2)}) async-start(bf16[128,32,128]{2,1,0:T(8,128)(2,1)} %shard_map.155), calls=%async_computation.1 | async-start | bytes 2097152 | tf_op jit(solution)/shard_map/all_to_all | solution.py:356
  56.0 1.1 shard_map.156.gate_ref
  57.9 17.1 %all-to-all-done.1.in_ref = bf16[128,32,128]{2,1,0:T(8,128)(2,1)S(1)} async-done(((bf16[128,32,128]{2,1,0:T(8,128)(2,1)}), bf16[128,32,128]{2,1,0:T(8,128)(2,1)S(1)}, u32[]{:S(2)}, u32[]{:S(2)}) %all-to-all-start.1) | async-done | bytes 1048608 | tf_op jit(solution)/shard_map/all_to_all | solution.py:356
  75.1 4.4 %shard_map.157 = bf16[8,512,128]{2,1,0:T(8,128)(2,1)} custom-call(bf16[128,32,128]{2,1,0:T(8,128)(2,1)S(1)} %all-to-all-done.1.in_ref, bf16[5,640,128]{2,1,0:T(8,128)(2,1)S(1)} %copy-done, f32[5,640,128]{2,1,0:T(8,128)S(1)} %shard_map.156.gate_ref, f32[6,128]{1,0:T(8,128)S(1)} %stack.27.norms_ref, bf16[136,128]{1,0:T(8,128)(2,1)S(1)} %fusion.1.w_ref), custom_call_target="tpu_custom_call" | custom-call | tf_op jit(solution)/shard_map/pallas_call | solution.py:359
  79.5 3.7 %all-to-all-start.2 = ((bf16[8,512,128]{2,1,0:T(8,128)(2,1)}), bf16[8,512,128]{2,1,0:T(8,128)(2,1)S(1)}, u32[]{:S(2)}, u32[]{:S(2)}) async-start(bf16[8,512,128]{2,1,0:T(8,128)(2,1)} %shard_map.157), calls=%async_computation.2 | async-start | bytes 2097152 | tf_op jit(solution)/shard_map/all_to_all | solution.py:365
  83.8 13.2 %all-to-all-done.2.in_ref.mid_ref = bf16[8,512,128]{2,1,0:T(8,128)(2,1)S(1)} async-done(((bf16[8,512,128]{2,1,0:T(8,128)(2,1)}), bf16[8,512,128]{2,1,0:T(8,128)(2,1)S(1)}, u32[]{:S(2)}, u32[]{:S(2)}) %all-to-all-start.2) | async-done | bytes 1048608 | tf_op jit(solution)/shard_map/all_to_all | solution.py:365
  97.5 0.9 collective-permute-start
  98.4 2.3 %collective-permute-start.1 = (bf16[160,640]{1,0:T(8,128)(2,1)S(1)}, bf16[160,640]{1,0:T(8,128)(2,1)S(1)}, u32[]{:S(2)}, u32[]{:S(2)}) collective-permute-start(bf16[160,640]{1,0:T(8,128)(2,1)S(1)} %shard_map.158.refs_0_), channel_id=1, source_target_pairs={{0,1},{1,0},{2,3},{3,2},{4,5},{5,4},{6,7},{7,6},{8,9},{9,8},{10,11... | collective-permute-start | bytes 614408 | tf_op jit(solution)/shard_map/ppermute | solution.py:382
  101.3 2.0 %collective-permute-start.3 = (bf16[160,640]{1,0:T(8,128)(2,1)S(1)}, bf16[160,640]{1,0:T(8,128)(2,1)S(1)}, u32[]{:S(2)}, u32[]{:S(2)}) collective-permute-start(bf16[160,640]{1,0:T(8,128)(2,1)S(1)} %shard_map.158.refs_0_), channel_id=1, source_target_pairs={{0,8},{1,9},{2,10},{3,11},{4,12},{5,13},{6,14},{7,15},{8,0},{9,1},... | collective-permute-start | bytes 614408 | tf_op jit(solution)/shard_map/ppermute | solution.py:382
  103.3 1.9 %collective-permute-start.4 = (bf16[160,640]{1,0:T(8,128)(2,1)S(1)}, bf16[160,640]{1,0:T(8,128)(2,1)S(1)}, u32[]{:S(2)}, u32[]{:S(2)}) collective-permute-start(bf16[160,640]{1,0:T(8,128)(2,1)S(1)} %shard_map.158.refs_0_), channel_id=1, source_target_pairs={{0,12},{1,13},{2,14},{3,15},{4,8},{5,9},{6,10},{7,11},{8,4},{9,5},... | collective-permute-start | bytes 614408 | tf_op jit(solution)/shard_map/ppermute | solution.py:382
  105.6 1.7 %collective-permute-start.2 = (bf16[160,640]{1,0:T(8,128)(2,1)S(1)}, bf16[160,640]{1,0:T(8,128)(2,1)S(1)}, u32[]{:S(2)}, u32[]{:S(2)}) collective-permute-start(bf16[160,640]{1,0:T(8,128)(2,1)S(1)} %collective-permute-done.refs_1_), channel_id=1, source_target_pairs={{0,1},{1,0},{2,3},{3,2},{4,5},{5,4},{6,7},{7,6},{8,9},{9,8},{10,11... | collective-permute-start | bytes 614408 | tf_op jit(solution)/shard_map/ppermute | solution.py:382
  107.7 1.6 %shard_map.159 = (bf16[5,640,128]{2,1,0:T(8,128)(2,1)S(1)}, bf16[5,128,640]{2,1,0:T(8,128)(2,1)S(1)}, bf16[5,640,256]{2,1,0:T(8,128)(2,1)S(1)}, f32[5,640,128]{2,1,0:T(8,128)S(1)}) custom-call(bf16[8,512,128]{2,1,0:T(8,128)(2,1)S(1)} %all-to-all-done.2.in_ref.mid_ref, f32[6,128]{1,0:T(8,128)S(1)} %stack.27.norms_ref, ...), custom_call_target="tpu_custom_call" | custom-call | tf_op jit(solution)/shard_map/pallas_call | solution.py:394
  109.5 6.1 %shard_map.160.refs_0_ = bf16[10,80,128]{2,1,0:T(8,128)(2,1)S(1)} custom-call(s32[1]{0:T(128)} %bitcast.me_ref, f32[4]{0:T(128)S(1)} %copy-done.3, bf16[5,640,128]{2,1,0:T(8,128)(2,1)S(1)} %get-tuple-element.41.q_ref, bf16[5,128,640]{2,1,0:T(8,128)(2,1)S(1)} %get-tuple-element.42.k_ref, bf16[5,640,256]{2,1,0:T(8,128)(2,1)S(1)} %get-tuple-element.43.v_ref, ...), custom_call_target="tpu_custom_call" | custom-call | flops 1048576 | bytes 65536 | tf_op jit(solution)/shard_map/pallas_call | solution.py:402
  115.7 1.4 collective-permute-start.7
  119.2 6.1 %shard_map.161.refs_1_ = bf16[10,80,128]{2,1,0:T(8,128)(2,1)S(1)} custom-call(s32[1]{0:T(128)} %bitcast.me_ref, f32[4]{0:T(128)S(1)} %copy-done.3, bf16[5,640,128]{2,1,0:T(8,128)(2,1)S(1)} %get-tuple-element.41.q_ref, bf16[5,128,640]{2,1,0:T(8,128)(2,1)S(1)} %get-tuple-element.42.k_ref, bf16[5,640,256]{2,1,0:T(8,128)(2,1)S(1)} %get-tuple-element.43.v_ref, ...), custom_call_target="tpu_custom_call" | custom-call | flops 1048576 | bytes 65536 | tf_op jit(solution)/shard_map/pallas_call | solution.py:402
  125.3 1.1 collective-permute-start.13
  126.4 6.0 %shard_map.162.refs_2_ = bf16[10,80,128]{2,1,0:T(8,128)(2,1)S(1)} custom-call(s32[1]{0:T(128)} %bitcast.me_ref, f32[4]{0:T(128)S(1)} %copy-done.3, bf16[5,640,128]{2,1,0:T(8,128)(2,1)S(1)} %get-tuple-element.41.q_ref, bf16[5,128,640]{2,1,0:T(8,128)(2,1)S(1)} %get-tuple-element.42.k_ref, bf16[5,640,256]{2,1,0:T(8,128)(2,1)S(1)} %get-tuple-element.43.v_ref, ...), custom_call_target="tpu_custom_call" | custom-call | flops 1048576 | bytes 65536 | tf_op jit(solution)/shard_map/pallas_call | solution.py:402
  132.6 1.4 collective-permute-done.14.refs_3_
  134.0 6.0 %shard_map.163.refs_3_ = bf16[10,80,128]{2,1,0:T(8,128)(2,1)S(1)} custom-call(s32[1]{0:T(128)} %bitcast.me_ref, f32[4]{0:T(128)S(1)} %copy-done.3, bf16[5,640,128]{2,1,0:T(8,128)(2,1)S(1)} %get-tuple-element.41.q_ref, bf16[5,128,640]{2,1,0:T(8,128)(2,1)S(1)} %get-tuple-element.42.k_ref, bf16[5,640,256]{2,1,0:T(8,128)(2,1)S(1)} %get-tuple-element.43.v_ref, ...), custom_call_target="tpu_custom_call" | custom-call | flops 1048576 | bytes 65536 | tf_op jit(solution)/shard_map/pallas_call | solution.py:402
  140.1 18.6 %all_to_all.21.in_ref = bf16[40,80,128]{2,1,0:T(8,128)(2,1)S(1)} all-to-all(bf16[40,80,128]{2,1,0:T(8,128)(2,1)S(1)} %shard_map.164), channel_id=1, replica_groups=mesh['row'=8,'col'=16] {'row'}, dimensions={0} | all-to-all | bytes 1638400 | tf_op jit(solution)/shard_map/all_to_all | solution.py:433
  158.7 1.3 shard_map.165
  (74 shorter events, 5.7 us)
Async XLA Ops:
  51.0 4.9 %copy-start.11 = (f32[128]{0:T(128)S(1)}, f32[128]{0:T(128)}, u32[]{:S(2)}) copy-start(f32[128]{0:T(128)} %param.24) | copy-start | bytes 1540
  51.0 4.9 %copy-start.12 = (f32[128]{0:T(128)S(1)}, f32[128]{0:T(128)}, u32[]{:S(2)}) copy-start(f32[128]{0:T(128)} %param.26) | copy-start | bytes 1540
  51.0 4.9 %copy-start.13 = (f32[128]{0:T(128)S(1)}, f32[128]{0:T(128)}, u32[]{:S(2)}) copy-start(f32[128]{0:T(128)} %param.27) | copy-start | bytes 1540
  51.0 4.9 %copy-start = (bf16[5,640,128]{2,1,0:T(8,128)(2,1)S(1)}, bf16[5,640,128]{2,1,0:T(8,128)(2,1)}, u32[]{:S(2)}) copy-start(bf16[5,640,128]{2,1,0:T(8,128)(2,1)} %get-tuple-element.36.x_ref) | copy-start | bytes 2457604
  51.1 4.9 %copy-start.2 = (bf16[128,128]{1,0:T(8,128)(2,1)S(1)}, bf16[128,128]{1,0:T(8,128)(2,1)}, u32[]{:S(2)}) copy-start(bf16[128,128]{1,0:T(8,128)(2,1)} %w_ref.1) | copy-start | bytes 98308
  51.1 24.0 %all-to-all-start.1 = ((bf16[128,32,128]{2,1,0:T(8,128)(2,1)}), bf16[128,32,128]{2,1,0:T(8,128)(2,1)S(1)}, u32[]{:S(2)}, u32[]{:S(2)}) async-start(bf16[128,32,128]{2,1,0:T(8,128)(2,1)} %shard_map.155), calls=%async_computation.1 | async-start | bytes 2097152 | tf_op jit(solution)/shard_map/all_to_all | solution.py:356
  79.5 17.5 %all-to-all-start.2 = ((bf16[8,512,128]{2,1,0:T(8,128)(2,1)}), bf16[8,512,128]{2,1,0:T(8,128)(2,1)S(1)}, u32[]{:S(2)}, u32[]{:S(2)}) async-start(bf16[8,512,128]{2,1,0:T(8,128)(2,1)} %shard_map.157), calls=%async_computation.2 | async-start | bytes 2097152 | tf_op jit(solution)/shard_map/all_to_all | solution.py:365
  83.8 25.7 %copy-start.1 = (bf16[128,128]{1,0:T(8,128)(2,1)S(1)}, bf16[128,128]{1,0:T(8,128)(2,1)}, u32[]{:S(2)}) copy-start(bf16[128,128]{1,0:T(8,128)(2,1)} %wo_ref.7) | copy-start | bytes 98308
  83.8 25.7 %copy-start.3 = (f32[4]{0:T(128)S(1)}, f32[4]{0:T(128)}, u32[]{:S(2)}) copy-start(f32[4]{0:T(128)} %inter_ref.7) | copy-start | bytes 52
  97.5 8.1 %collective-permute-start = (bf16[160,640]{1,0:T(8,128)(2,1)S(1)}, bf16[160,640]{1,0:T(8,128)(2,1)S(1)}, u32[]{:S(2)}, u32[]{:S(2)}) collective-permute-start(bf16[160,640]{1,0:T(8,128)(2,1)S(1)} %shard_map.158.refs_0_), channel_id=1, source_target_pairs={{0,4},{1,5},{2,6},{3,7},{4,0},{5,1},{6,2},{7,3},{8,12},{9,13},{10,... | collective-permute-start | bytes 614408 | tf_op jit(solution)/shard_map/ppermute | solution.py:382
  98.4 8.9 %collective-permute-start.1 = (bf16[160,640]{1,0:T(8,128)(2,1)S(1)}, bf16[160,640]{1,0:T(8,128)(2,1)S(1)}, u32[]{:S(2)}, u32[]{:S(2)}) collective-permute-start(bf16[160,640]{1,0:T(8,128)(2,1)S(1)} %shard_map.158.refs_0_), channel_id=1, source_target_pairs={{0,1},{1,0},{2,3},{3,2},{4,5},{5,4},{6,7},{7,6},{8,9},{9,8},{10,11... | collective-permute-start | bytes 614408 | tf_op jit(solution)/shard_map/ppermute | solution.py:382
  101.3 14.3 %collective-permute-start.3 = (bf16[160,640]{1,0:T(8,128)(2,1)S(1)}, bf16[160,640]{1,0:T(8,128)(2,1)S(1)}, u32[]{:S(2)}, u32[]{:S(2)}) collective-permute-start(bf16[160,640]{1,0:T(8,128)(2,1)S(1)} %shard_map.158.refs_0_), channel_id=1, source_target_pairs={{0,8},{1,9},{2,10},{3,11},{4,12},{5,13},{6,14},{7,15},{8,0},{9,1},... | collective-permute-start | bytes 614408 | tf_op jit(solution)/shard_map/ppermute | solution.py:382
  103.3 12.2 %collective-permute-start.4 = (bf16[160,640]{1,0:T(8,128)(2,1)S(1)}, bf16[160,640]{1,0:T(8,128)(2,1)S(1)}, u32[]{:S(2)}, u32[]{:S(2)}) collective-permute-start(bf16[160,640]{1,0:T(8,128)(2,1)S(1)} %shard_map.158.refs_0_), channel_id=1, source_target_pairs={{0,12},{1,13},{2,14},{3,15},{4,8},{5,9},{6,10},{7,11},{8,4},{9,5},... | collective-permute-start | bytes 614408 | tf_op jit(solution)/shard_map/ppermute | solution.py:382
  105.3 10.3 %collective-permute-start.5 = (bf16[160,640]{1,0:T(8,128)(2,1)S(1)}, bf16[160,640]{1,0:T(8,128)(2,1)S(1)}, u32[]{:S(2)}, u32[]{:S(2)}) collective-permute-start(bf16[160,640]{1,0:T(8,128)(2,1)S(1)} %shard_map.158.refs_0_), channel_id=1, source_target_pairs={{0,2},{1,3},{2,0},{3,1},{4,6},{5,7},{6,4},{7,5},{8,10},{9,11},{10,... | collective-permute-start | bytes 614408 | tf_op jit(solution)/shard_map/ppermute | solution.py:382
  105.6 3.7 %collective-permute-start.2 = (bf16[160,640]{1,0:T(8,128)(2,1)S(1)}, bf16[160,640]{1,0:T(8,128)(2,1)S(1)}, u32[]{:S(2)}, u32[]{:S(2)}) collective-permute-start(bf16[160,640]{1,0:T(8,128)(2,1)S(1)} %collective-permute-done.refs_1_), channel_id=1, source_target_pairs={{0,1},{1,0},{2,3},{3,2},{4,5},{5,4},{6,7},{7,6},{8,9},{9,8},{10,11... | collective-permute-start | bytes 614408 | tf_op jit(solution)/shard_map/ppermute | solution.py:382
  107.3 8.4 %collective-permute-start.6 = (bf16[160,640]{1,0:T(8,128)(2,1)S(1)}, bf16[160,640]{1,0:T(8,128)(2,1)S(1)}, u32[]{:S(2)}, u32[]{:S(2)}) collective-permute-start(bf16[160,640]{1,0:T(8,128)(2,1)S(1)} %collective-permute-done.refs_1_), channel_id=1, source_target_pairs={{0,2},{1,3},{2,0},{3,1},{4,6},{5,7},{6,4},{7,5},{8,10},{9,11},{10,... | collective-permute-start | bytes 614408 | tf_op jit(solution)/shard_map/ppermute | solution.py:382
  115.7 2.5 %collective-permute-start.7 = (bf16[160,640]{1,0:T(8,128)(2,1)S(1)}, bf16[160,640]{1,0:T(8,128)(2,1)S(1)}, u32[]{:S(2)}, u32[]{:S(2)}) collective-permute-start(bf16[160,640]{1,0:T(8,128)(2,1)S(1)} %collective-permute-done.3.refs_0_), channel_id=1, source_target_pairs={{0,1},{1,0},{2,3},{3,2},{4,5},{5,4},{6,7},{7,6},{8,9},{9,8},{10,11... | collective-permute-start | bytes 614408 | tf_op jit(solution)/shard_map/ppermute | solution.py:382
  117.2 2.0 %collective-permute-start.8 = (bf16[160,640]{1,0:T(8,128)(2,1)S(1)}, bf16[160,640]{1,0:T(8,128)(2,1)S(1)}, u32[]{:S(2)}, u32[]{:S(2)}) collective-permute-start(bf16[160,640]{1,0:T(8,128)(2,1)S(1)} %collective-permute-done.4.refs_1_), channel_id=1, source_target_pairs={{0,1},{1,0},{2,3},{3,2},{4,5},{5,4},{6,7},{7,6},{8,9},{9,8},{10,11... | collective-permute-start | bytes 614408 | tf_op jit(solution)/shard_map/ppermute | solution.py:382
  117.2 2.0 %collective-permute-start.9 = (bf16[160,640]{1,0:T(8,128)(2,1)S(1)}, bf16[160,640]{1,0:T(8,128)(2,1)S(1)}, u32[]{:S(2)}, u32[]{:S(2)}) collective-permute-start(bf16[160,640]{1,0:T(8,128)(2,1)S(1)} %collective-permute-done.5.refs_0_), channel_id=1, source_target_pairs={{0,1},{1,0},{2,3},{3,2},{4,5},{5,4},{6,7},{7,6},{8,9},{9,8},{10,11... | collective-permute-start | bytes 614408 | tf_op jit(solution)/shard_map/ppermute | solution.py:382
  117.7 1.5 collective-permute-start.10
  117.7 7.6 %collective-permute-start.11 = (bf16[160,640]{1,0:T(8,128)(2,1)S(1)}, bf16[160,640]{1,0:T(8,128)(2,1)S(1)}, u32[]{:S(2)}, u32[]{:S(2)}) collective-permute-start(bf16[160,640]{1,0:T(8,128)(2,1)S(1)} %collective-permute-done.3.refs_0_), channel_id=1, source_target_pairs={{0,2},{1,3},{2,0},{3,1},{4,6},{5,7},{6,4},{7,5},{8,10},{9,11},{10,... | collective-permute-start | bytes 614408 | tf_op jit(solution)/shard_map/ppermute | solution.py:382
  118.2 14.2 %collective-permute-start.12 = (bf16[160,640]{1,0:T(8,128)(2,1)S(1)}, bf16[160,640]{1,0:T(8,128)(2,1)S(1)}, u32[]{:S(2)}, u32[]{:S(2)}) collective-permute-start(bf16[160,640]{1,0:T(8,128)(2,1)S(1)} %collective-permute-done.4.refs_1_), channel_id=1, source_target_pairs={{0,2},{1,3},{2,0},{3,1},{4,6},{5,7},{6,4},{7,5},{8,10},{9,11},{10,... | collective-permute-start | bytes 614408 | tf_op jit(solution)/shard_map/ppermute | solution.py:382
  125.3 7.2 %collective-permute-start.13 = (bf16[160,640]{1,0:T(8,128)(2,1)S(1)}, bf16[160,640]{1,0:T(8,128)(2,1)S(1)}, u32[]{:S(2)}, u32[]{:S(2)}) collective-permute-start(bf16[160,640]{1,0:T(8,128)(2,1)S(1)} %collective-permute-done.11.refs_0_), channel_id=1, source_target_pairs={{0,1},{1,0},{2,3},{3,2},{4,5},{5,4},{6,7},{7,6},{8,9},{9,8},{10,11... | collective-permute-start | bytes 614408 | tf_op jit(solution)/shard_map/ppermute | solution.py:382
  132.5 1.5 collective-permute-start.14
  (7 other events, 27.9 us)

commit v4 on v3

--- a/solution.py
+++ b/solution.py
@@ -1,4 +1,5 @@
 import functools
+import math
 
 import jax
 import jax.numpy as jnp
@@ -18,6 +19,7 @@
 CJ = N // COLS
 T = CJ // ROWS
 SEND = 56
+PITCH = 40
 BACK = 32
 G = RI // 16
 A = CJ // 8
@@ -28,6 +30,7 @@
 
 MASK_NEG = 10000.0
 EPS = 1e-05
+LOG2E = math.log2(math.e)
 
 F32 = jnp.float32
 BF16 = jnp.bfloat16
@@ -173,9 +176,9 @@
             )
             for r in range(ROWS):
                 for a in range(A):
-                    row = (r * COLS + half) * BACK + a * G + g
-                    back[pl.ds(row, ROWS, stride=2 * BACK), :] = parts[r][a * ROWS : (a + 1) * ROWS]
-    out_ref[...] = back[...].reshape(C, BACK, C).astype(BF16)
+                    row = (r * COLS + half) * PITCH + a * G + g
+                    back[pl.ds(row, ROWS, stride=2 * PITCH), :] = parts[r][a * ROWS : (a + 1) * ROWS]
+    out_ref[...] = back[...].reshape(C, PITCH, C)[:, :BACK].astype(BF16)
 
 
 def middle_kernel(in_ref, x_ref, gate_ref, norms_ref, w_ref, out_ref, wide, pay):
@@ -206,6 +209,7 @@
 
 
 def qkvg_kernel(in_ref, norms_ref, wqg_ref, wv_ref, wk_ref, q_ref, k_ref, v_ref, g_ref):
+    lane_head = lax.broadcasted_iota(jnp.int32, (N, C), 1) // DH
     for t in range(T):
         mid = jnp.concatenate([in_ref[r, t * RI : (t + 1) * RI, :] for r in range(ROWS)], axis=0)
         att = layer_norm(mid.astype(F32), norms_ref[4:5], norms_ref[5:6]).astype(BF16)
@@ -213,10 +217,11 @@
             [att[r * RI + 16 * g : r * RI + 16 * g + 16] for g in range(G) for r in range(ROWS)], axis=0
         )
         qg = dot(att, wqg_ref[...], ((1,), (0,)))
-        q_ref[t] = (qg[:, :C] * DH ** (-0.5)).astype(BF16)
+        q_ref[t] = (qg[:, :C] * (LOG2E * DH ** (-0.5))).astype(BF16)
         g_ref[t] = sigmoid(qg[:, C:])
         vals = dot(keyed, wv_ref[...], ((1,), (0,))).astype(BF16)
-        v_ref[t] = jnp.concatenate([vals, jnp.ones((N, C), BF16)], axis=1)
+        for h in range(H):
+            v_ref[t * H + h] = jnp.where(lane_head == h, vals, jnp.ones_like(vals))
         k_ref[t] = dot(wk_ref[...], keyed, ((1,), (1,))).astype(BF16)
 
 
@@ -247,7 +252,7 @@
                 to = pl.multiple_of(n * RI + core * CJ + 8 * s, 8)
                 crossing = cross_ref[pl.ds((first + 8 * s) // MB, 1), :]
                 for h in range(H):
-                    extra[h, pl.ds(to, 8), :] = (
+                    extra[h, pl.ds(to, 8), :] = LOG2E * (
                         part[h * CJ + 8 * s : h * CJ + 8 * s + 8, :].astype(F32)
                         + inter_ref[h] * crossing
                         + key_ref[...]
@@ -259,25 +264,16 @@
 
     valid = rows_of(lambda rows: valid_ref[rows, :])
 
-    def one_column(t, carry):
+    def set_score(t, h):
         queries = rows_of(lambda rows: q_ref[t, rows, :])
-
-        def set_score(h):
-            own = jnp.where(lane_head == h, queries, jnp.zeros_like(queries))
-            score[h % 2][...] = dot(own, k_ref[t], ((1,), (0,))) + extra[h]
-
-        total = jnp.zeros((CHUNK, C), F32)
-        set_score(0)
-        for h in range(H + 1):
-            if h + 1 < H:
-                set_score(h + 1)
-            if h > 0:
-                sums = dot(power[(h - 1) % 2][...], v_ref[t], ((1,), (0,)))
-                total = jnp.where(lane_head == h - 1, sums[:, :C] / sums[:, C:], total)
-            if h < H:
-                now = score[h % 2][...]
-                highest = jnp.max(now, axis=1, keepdims=True)
-                power[h % 2][...] = jnp.exp(now - highest).astype(BF16)
+        own = jnp.where(lane_head == h, queries, jnp.zeros_like(queries))
+        score[h % 2][...] = dot(own, k_ref[t], ((1,), (0,))) + extra[h]
+
+    def weigh(t, h, total):
+        sums = dot(power[h % 2][...], v_ref[t * H + h], ((1,), (0,)))
+        return jnp.where(lane_head == h, sums / pltpu.roll(sums, C // 2, 1), total)
+
+    def finish(t, total):
         gated = (rows_of(lambda rows: g_ref[t, rows, :]) * total).astype(BF16)
         update = dot(gated, wo_ref[...], ((1,), (0,)))
         own = pl.ds(pl.multiple_of(t * RI, RI), RI)
@@ -285,9 +281,27 @@
         out = (mid + valid * valid_t_ref[t] * update).astype(BF16)
         for n in range(GROUP):
             out_ref[n * T + t] = out[n * RI : (n + 1) * RI]
-        return carry
-
-    lax.fori_loop(0, T, one_column, 0)
+
+    def one_column(t, total):
+        for h in range(H):
+            if h + 1 < H:
+                set_score(t, h + 1)
+            else:
+                set_score(jnp.minimum(t + 1, T - 1), 0)
+            if h > 0:
+                total = weigh(t, h - 1, total)
+            else:
+                before = jnp.maximum(t - 1, 0)
+                finish(before, weigh(before, H - 1, total))
+            now = score[h % 2][...]
+            highest = jnp.max(now, axis=1, keepdims=True)
+            power[h % 2][...] = jnp.exp2(now - highest).astype(BF16)
+        return total
+
+    power[(H - 1) % 2][...] = jnp.ones((CHUNK, N), BF16)
+    set_score(0, 0)
+    total = lax.fori_loop(0, T, one_column, jnp.zeros((CHUNK, C), F32))
+    finish(T - 1, weigh(T - 1, H - 1, total))
 
 
 def order_kernel(me_ref, *refs):
@@ -349,7 +363,7 @@
             pltpu.VMEM((N, N), BF16),
             pltpu.VMEM((N, N), BF16),
             pltpu.VMEM((G, N, C), F32),
-            pltpu.VMEM((C * BACK, C), F32),
+            pltpu.VMEM((C * PITCH, C), F32),
         ],
         [VMEM],
     )(channel)
@@ -388,15 +402,21 @@
         [VMEM],
     )(mid)
     hold = lax.optimization_barrier
-    one, two, three, beside = [swap(merged, 0, step) for step in (4, 8, 12, 2)]
-
+
+    def core(values):
+        return swap(values, 0, 1)
+
+    one, merged2 = swap(merged, 0, 4), core(merged)
     wqg = jnp.concatenate([qkvg_weight[:, :C], qkvg_weight[:, 3 * C :]], axis=1)
     q, k, v, g = call(
         qkvg_kernel,
-        [struct((T, N, C)), struct((T, C, N)), struct((T, N, 2 * C)), struct((T, N, C), F32)],
+        [struct((T, N, C)), struct((T, C, N)), struct((T * H, N, C)), struct((T, N, C), F32)],
         [],
         [VMEM] * 5,
     )(mid, norms, wqg, qkvg_weight[:, 2 * C : 3 * C], qkvg_weight[:, C : 2 * C].T)
+
+    merged, q, k, v, g = hold((merged, q, k, v, g))
+    two, three, beside = [swap(merged, 0, step) for step in (8, 12, 2)]
 
     def attend(steps, *parts):
         return call(
@@ -412,21 +432,16 @@
             *parts,
         )
 
-    def core(values):
-        return swap(values, 0, 1)
-
     one_across = swap(one, 0, 2)
-    merged, near, merged2, near2, q, k, v, g = hold((merged, one, core(merged), core(one), q, k, v, g))
-    outs = [attend((0, 2), merged, near, merged2, near2)]
-    outs[0], two, three, beside, one_across = hold((outs[0], two, three, beside, one_across))
+    near = hold((merged, one, merged2, core(one)))
+    outs = [attend((0, 2), *near)]
+    outs[0], two, three, beside = hold((outs[0], two, three, beside))
     two_across, three_across = swap(two, 0, 2), swap(three, 0, 2)
-    two, three, two2, three2, beside2, one_across2 = hold(
-        (two, three, core(two), core(three), core(beside), core(one_across))
-    )
+    two, three, two2, three2, beside2 = hold((two, three, core(two), core(three), core(beside)))
     outs.append(attend((4, 6), two, three, two2, three2))
-    outs[1], two_across = hold((outs[1], two_across))
+    outs[1], one_across, two_across = hold((outs[1], one_across, two_across))
     two_across2 = core(two_across)
-    outs.append(attend((1, 3), beside, one_across, beside2, one_across2))
+    outs.append(attend((1, 3), beside, one_across, beside2, core(one_across)))
     outs[2], three_across, two_across2 = hold((outs[2], three_across, two_across2))
     outs.append(attend((5, 7), two_across, three_across, two_across2, core(three_across)))
     out = call(order_kernel, struct((CJ, RI, C)), [], [SMEM] + [VMEM] * 4)(col_at[None], *outs)

time: 160 us -> 164 us (1.025)
  waiting for transfers between devices: 32.3 us -> 36.8 us
    ppermute x15, waiting for transfers between devices: 1.92 us -> 6.46 us  [swap(): return lax.ppermute(values, both, pairs)]
  transfers between devices with their start and end apart: 17 -> 17, of which waited for: 5 -> 7; matrix products, arithmetic and copies ran while one was open for 1% -> 1% of each run, Pallas kernels for 13% -> 13%
where the time goes in v4:
time: 164 us; the launch traced here: 163 us
  blocking collectives  57.7 us (35%)
  Pallas kernels  44.7 us (27%)
  waiting for transfers between devices  36.8 us (22%)
  starting transfers between devices  21.5 us (13%)
    all_to_all x1, blocking collectives, on_device(): channel = lax.all_to_all(parcels, both, 0, 0, tiled=True)  39 us
    pallas_call x4, Pallas kernels, attend(): call(functools.partial(attend_kernel, tuple(steps)), struct((GROUP * T, R...  24 us
    all_to_all x1, blocking collectives, on_device(): home = lax.all_to_all(out, 'row', 0, 0, tiled=True)  18.7 us
    all_to_all x1, waiting for transfers between devices, on_device(): returned = lax.all_to_all(product, both, 0, 0, tiled=True)  17.2 us
    all_to_all x1, waiting for transfers between devices, on_device(): mid = lax.all_to_all(turned, 'row', 0, 0, tiled=True)  13.2 us
    ppermute x15, starting transfers between devices, swap(): return lax.ppermute(values, both, pairs)  13 us
    pallas_call x1, Pallas kernels, on_device(): call(product_kernel, struct((C, BACK, C)), [pltpu.VMEM((C * SEND, C), F32...  6.73 us
    ppermute x15, waiting for transfers between devices, swap(): return lax.ppermute(values, both, pairs)  6.46 us
  transfers between devices with their start and end apart: 17, of which 7 were waited for; matrix products, arithmetic and copies ran while one was open for 1% of the time, Pallas kernels for 13%

profile of v4, /device:TPU:1, one launch (start us, length us, event | category | flops | bytes accessed | tf_op | source)
XLA Modules:
  0.0 163.3 jit_solution(9209851922897959183)
XLA Ops:
  0.0 4.9 %shard_map.154 = (bf16[128,56,128]{2,1,0:T(8,128)(2,1)}, bf16[5,640,128]{2,1,0:T(8,128)(2,1)}) custom-call(bf16[80,40,128]{2,1,0:T(8,128)(2,1)} %pair_hbm.1, s32[10]{0:T(128)} %valid_hbm.1, f32[128]{0:T(128)} %gain_hbm.1, f32[128]{0:T(128)} %bias_hbm.1, bf16[128,512]{1,0:T(8,128)(2,1)} %w_hbm.1), custom_call_target="tpu_custom_call" | custom-call | tf_op jit(solution)/shard_map/pallas_call | solution.py:340
  4.9 39.0 %all_to_all.20.in_ref = bf16[128,56,128]{2,1,0:T(8,128)(2,1)S(1)} all-to-all(bf16[128,56,128]{2,1,0:T(8,128)(2,1)} %get-tuple-element.35), channel_id=1, replica_groups=mesh['row'=8,'col'=16] {'row','col'}, dimensions={0} | all-to-all | bytes 3670016 | tf_op jit(solution)/shard_map/all_to_all | solution.py:357
  43.9 6.7 %shard_map.155 = bf16[128,32,128]{2,1,0:T(8,128)(2,1)} custom-call(bf16[128,56,128]{2,1,0:T(8,128)(2,1)S(1)} %all_to_all.20.in_ref), custom_call_target="tpu_custom_call" | custom-call | tf_op jit(solution)/shard_map/pallas_call | solution.py:358
  50.6 4.8 %all-to-all-start.1 = ((bf16[128,32,128]{2,1,0:T(8,128)(2,1)}), bf16[128,32,128]{2,1,0:T(8,128)(2,1)S(1)}, u32[]{:S(2)}, u32[]{:S(2)}) async-start(bf16[128,32,128]{2,1,0:T(8,128)(2,1)} %shard_map.155), calls=%async_computation.1 | async-start | bytes 2097152 | tf_op jit(solution)/shard_map/all_to_all | solution.py:370
  55.6 1.1 shard_map.156.gate_ref
  57.5 17.2 %all-to-all-done.1.in_ref = bf16[128,32,128]{2,1,0:T(8,128)(2,1)S(1)} async-done(((bf16[128,32,128]{2,1,0:T(8,128)(2,1)}), bf16[128,32,128]{2,1,0:T(8,128)(2,1)S(1)}, u32[]{:S(2)}, u32[]{:S(2)}) %all-to-all-start.1) | async-done | bytes 1048608 | tf_op jit(solution)/shard_map/all_to_all | solution.py:370
  74.6 4.4 %shard_map.157 = bf16[8,512,128]{2,1,0:T(8,128)(2,1)} custom-call(bf16[128,32,128]{2,1,0:T(8,128)(2,1)S(1)} %all-to-all-done.1.in_ref, bf16[5,640,128]{2,1,0:T(8,128)(2,1)S(1)} %copy-done, f32[5,640,128]{2,1,0:T(8,128)S(1)} %shard_map.156.gate_ref, f32[6,128]{1,0:T(8,128)S(1)} %stack.27.norms_ref, bf16[136,128]{1,0:T(8,128)(2,1)S(1)} %fusion.1.w_ref), custom_call_target="tpu_custom_call" | custom-call | tf_op jit(solution)/shard_map/pallas_call | solution.py:373
  79.1 3.7 %all-to-all-start.2 = ((bf16[8,512,128]{2,1,0:T(8,128)(2,1)}), bf16[8,512,128]{2,1,0:T(8,128)(2,1)S(1)}, u32[]{:S(2)}, u32[]{:S(2)}) async-start(bf16[8,512,128]{2,1,0:T(8,128)(2,1)} %shard_map.157), calls=%async_computation.2 | async-start | bytes 2097152 | tf_op jit(solution)/shard_map/all_to_all | solution.py:379
  83.4 13.2 %all-to-all-done.2.in_ref.mid_ref = bf16[8,512,128]{2,1,0:T(8,128)(2,1)S(1)} async-done(((bf16[8,512,128]{2,1,0:T(8,128)(2,1)}), bf16[8,512,128]{2,1,0:T(8,128)(2,1)S(1)}, u32[]{:S(2)}, u32[]{:S(2)}) %all-to-all-start.2) | async-done | bytes 1048608 | tf_op jit(solution)/shard_map/all_to_all | solution.py:379
  97.1 0.9 collective-permute-start
  98.6 2.4 %collective-permute-start.1 = (bf16[160,640]{1,0:T(8,128)(2,1)S(1)}, bf16[160,640]{1,0:T(8,128)(2,1)S(1)}, u32[]{:S(2)}, u32[]{:S(2)}) collective-permute-start(bf16[160,640]{1,0:T(8,128)(2,1)S(1)} %shard_map.158.refs_0_), channel_id=1, source_target_pairs={{0,1},{1,0},{2,3},{3,2},{4,5},{5,4},{6,7},{7,6},{8,9},{9,8},{10,11... | collective-permute-start | bytes 614408 | tf_op jit(solution)/shard_map/ppermute | solution.py:396
  101.0 1.8 %shard_map.159 = (bf16[5,640,128]{2,1,0:T(8,128)(2,1)S(1)}, bf16[5,128,640]{2,1,0:T(8,128)(2,1)S(1)}, bf16[20,640,128]{2,1,0:T(8,128)(2,1)S(1)}, f32[5,640,128]{2,1,0:T(8,128)S(1)}) custom-call(bf16[8,512,128]{2,1,0:T(8,128)(2,1)S(1)} %all-to-all-done.2.in_ref.mid_ref, f32[6,128]{1,0:T(8,128)S(1)} %stack.27.norms_ref, ...), custom_call_target="tpu_custom_call" | custom-call | tf_op jit(solution)/shard_map/pallas_call | solution.py:411
  102.7 2.0 %collective-permute-start.3 = (bf16[160,640]{1,0:T(8,128)(2,1)S(1)}, bf16[160,640]{1,0:T(8,128)(2,1)S(1)}, u32[]{:S(2)}, u32[]{:S(2)}) collective-permute-start(bf16[160,640]{1,0:T(8,128)(2,1)S(1)} %shard_map.158.refs_0_), channel_id=1, source_target_pairs={{0,8},{1,9},{2,10},{3,11},{4,12},{5,13},{6,14},{7,15},{8,0},{9,1},... | collective-permute-start | bytes 614408 | tf_op jit(solution)/shard_map/ppermute | solution.py:396
  104.7 2.0 %collective-permute-start.4 = (bf16[160,640]{1,0:T(8,128)(2,1)S(1)}, bf16[160,640]{1,0:T(8,128)(2,1)S(1)}, u32[]{:S(2)}, u32[]{:S(2)}) collective-permute-start(bf16[160,640]{1,0:T(8,128)(2,1)S(1)} %shard_map.158.refs_0_), channel_id=1, source_target_pairs={{0,12},{1,13},{2,14},{3,15},{4,8},{5,9},{6,10},{7,11},{8,4},{9,5},... | collective-permute-start | bytes 614408 | tf_op jit(solution)/shard_map/ppermute | solution.py:396
  107.9 1.0 collective-permute-done.2.refs_3_
  109.1 6.0 %shard_map.160.refs_0_ = bf16[10,80,128]{2,1,0:T(8,128)(2,1)S(1)} custom-call(s32[1]{0:T(128)} %bitcast.me_ref, f32[4]{0:T(128)S(1)} %copy-done.3, bf16[5,640,128]{2,1,0:T(8,128)(2,1)S(1)} %get-tuple-element.41.q_ref, bf16[5,128,640]{2,1,0:T(8,128)(2,1)S(1)} %get-tuple-element.42.k_ref, bf16[20,640,128]{2,1,0:T(8,128)(2,1)S(1)} %get-tuple-element.43.v_ref, ...), custom_call_target="tpu_custom_call" | custom-call | flops 1048576 | bytes 65536 | tf_op jit(solution)/shard_map/pallas_call | solution.py:422
  117.3 0.9 collective-permute-start.10
  118.2 6.0 %shard_map.161.refs_1_ = bf16[10,80,128]{2,1,0:T(8,128)(2,1)S(1)} custom-call(s32[1]{0:T(128)} %bitcast.me_ref, f32[4]{0:T(128)S(1)} %copy-done.3, bf16[5,640,128]{2,1,0:T(8,128)(2,1)S(1)} %get-tuple-element.41.q_ref, bf16[5,128,640]{2,1,0:T(8,128)(2,1)S(1)} %get-tuple-element.42.k_ref, bf16[20,640,128]{2,1,0:T(8,128)(2,1)S(1)} %get-tuple-element.43.v_ref, ...), custom_call_target="tpu_custom_call" | custom-call | flops 1048576 | bytes 65536 | tf_op jit(solution)/shard_map/pallas_call | solution.py:422
  124.2 3.5 %collective-permute-done.10.refs_0_ = bf16[160,640]{1,0:T(8,128)(2,1)S(1)} collective-permute-done((bf16[160,640]{1,0:T(8,128)(2,1)S(1)}, bf16[160,640]{1,0:T(8,128)(2,1)S(1)}, u32[]{:S(2)}, u32[]{:S(2)}) %collective-permute-start.10) | collective-permute-done | bytes 204832 | tf_op jit(solution)/shard_map/ppermute | solution.py:396
  129.7 6.0 %shard_map.162.refs_2_ = bf16[10,80,128]{2,1,0:T(8,128)(2,1)S(1)} custom-call(s32[1]{0:T(128)} %bitcast.me_ref, f32[4]{0:T(128)S(1)} %copy-done.3, bf16[5,640,128]{2,1,0:T(8,128)(2,1)S(1)} %get-tuple-element.41.q_ref, bf16[5,128,640]{2,1,0:T(8,128)(2,1)S(1)} %get-tuple-element.42.k_ref, bf16[20,640,128]{2,1,0:T(8,128)(2,1)S(1)} %get-tuple-element.43.v_ref, ...), custom_call_target="tpu_custom_call" | custom-call | flops 1048576 | bytes 65536 | tf_op jit(solution)/shard_map/pallas_call | solution.py:422
  136.1 1.1 collective-permute-done.14.refs_3_
  137.2 6.0 %shard_map.163.refs_3_ = bf16[10,80,128]{2,1,0:T(8,128)(2,1)S(1)} custom-call(s32[1]{0:T(128)} %bitcast.me_ref, f32[4]{0:T(128)S(1)} %copy-done.3, bf16[5,640,128]{2,1,0:T(8,128)(2,1)S(1)} %get-tuple-element.41.q_ref, bf16[5,128,640]{2,1,0:T(8,128)(2,1)S(1)} %get-tuple-element.42.k_ref, bf16[20,640,128]{2,1,0:T(8,128)(2,1)S(1)} %get-tuple-element.43.v_ref, ...), custom_call_target="tpu_custom_call" | custom-call | flops 1048576 | bytes 65536 | tf_op jit(solution)/shard_map/pallas_call | solution.py:422
  143.2 18.7 %all_to_all.21.in_ref = bf16[40,80,128]{2,1,0:T(8,128)(2,1)S(1)} all-to-all(bf16[40,80,128]{2,1,0:T(8,128)(2,1)S(1)} %shard_map.164), channel_id=1, replica_groups=mesh['row'=8,'col'=16] {'row'}, dimensions={0} | all-to-all | bytes 1638400 | tf_op jit(solution)/shard_map/all_to_all | solution.py:448
  161.9 1.3 shard_map.165
  (74 shorter events, 8.4 us)
Async XLA Ops:
  43.9 11.6 %copy-start.11 = (f32[128]{0:T(128)S(1)}, f32[128]{0:T(128)}, u32[]{:S(2)}) copy-start(f32[128]{0:T(128)} %param.24) | copy-start | bytes 1540
  43.9 11.6 %copy-start.12 = (f32[128]{0:T(128)S(1)}, f32[128]{0:T(128)}, u32[]{:S(2)}) copy-start(f32[128]{0:T(128)} %param.26) | copy-start | bytes 1540
  43.9 11.6 %copy-start.13 = (f32[128]{0:T(128)S(1)}, f32[128]{0:T(128)}, u32[]{:S(2)}) copy-start(f32[128]{0:T(128)} %param.27) | copy-start | bytes 1540
  43.9 11.7 %copy-start = (bf16[5,640,128]{2,1,0:T(8,128)(2,1)S(1)}, bf16[5,640,128]{2,1,0:T(8,128)(2,1)}, u32[]{:S(2)}) copy-start(bf16[5,640,128]{2,1,0:T(8,128)(2,1)} %get-tuple-element.36.x_ref) | copy-start | bytes 2457604
  43.9 11.7 %copy-start.2 = (bf16[128,128]{1,0:T(8,128)(2,1)S(1)}, bf16[128,128]{1,0:T(8,128)(2,1)}, u32[]{:S(2)}) copy-start(bf16[128,128]{1,0:T(8,128)(2,1)} %w_ref.1) | copy-start | bytes 98308
  50.6 24.0 %all-to-all-start.1 = ((bf16[128,32,128]{2,1,0:T(8,128)(2,1)}), bf16[128,32,128]{2,1,0:T(8,128)(2,1)S(1)}, u32[]{:S(2)}, u32[]{:S(2)}) async-start(bf16[128,32,128]{2,1,0:T(8,128)(2,1)} %shard_map.155), calls=%async_computation.1 | async-start | bytes 2097152 | tf_op jit(solution)/shard_map/all_to_all | solution.py:370
  79.1 17.5 %all-to-all-start.2 = ((bf16[8,512,128]{2,1,0:T(8,128)(2,1)}), bf16[8,512,128]{2,1,0:T(8,128)(2,1)S(1)}, u32[]{:S(2)}, u32[]{:S(2)}) async-start(bf16[8,512,128]{2,1,0:T(8,128)(2,1)} %shard_map.157), calls=%async_computation.2 | async-start | bytes 2097152 | tf_op jit(solution)/shard_map/all_to_all | solution.py:379
  82.8 26.3 %copy-start.1 = (bf16[128,128]{1,0:T(8,128)(2,1)S(1)}, bf16[128,128]{1,0:T(8,128)(2,1)}, u32[]{:S(2)}) copy-start(bf16[128,128]{1,0:T(8,128)(2,1)} %wo_ref.7) | copy-start | bytes 98308
  82.8 26.3 %copy-start.3 = (f32[4]{0:T(128)S(1)}, f32[4]{0:T(128)}, u32[]{:S(2)}) copy-start(f32[4]{0:T(128)} %inter_ref.7) | copy-start | bytes 52
  97.1 9.9 %collective-permute-start = (bf16[160,640]{1,0:T(8,128)(2,1)S(1)}, bf16[160,640]{1,0:T(8,128)(2,1)S(1)}, u32[]{:S(2)}, u32[]{:S(2)}) collective-permute-start(bf16[160,640]{1,0:T(8,128)(2,1)S(1)} %shard_map.158.refs_0_), channel_id=1, source_target_pairs={{0,4},{1,5},{2,6},{3,7},{4,0},{5,1},{6,2},{7,3},{8,12},{9,13},{10,... | collective-permute-start | bytes 614408 | tf_op jit(solution)/shard_map/ppermute | solution.py:396
  98.6 9.3 %collective-permute-start.1 = (bf16[160,640]{1,0:T(8,128)(2,1)S(1)}, bf16[160,640]{1,0:T(8,128)(2,1)S(1)}, u32[]{:S(2)}, u32[]{:S(2)}) collective-permute-start(bf16[160,640]{1,0:T(8,128)(2,1)S(1)} %shard_map.158.refs_0_), channel_id=1, source_target_pairs={{0,1},{1,0},{2,3},{3,2},{4,5},{5,4},{6,7},{7,6},{8,9},{9,8},{10,11... | collective-permute-start | bytes 614408 | tf_op jit(solution)/shard_map/ppermute | solution.py:396
  102.7 12.4 %collective-permute-start.3 = (bf16[160,640]{1,0:T(8,128)(2,1)S(1)}, bf16[160,640]{1,0:T(8,128)(2,1)S(1)}, u32[]{:S(2)}, u32[]{:S(2)}) collective-permute-start(bf16[160,640]{1,0:T(8,128)(2,1)S(1)} %shard_map.158.refs_0_), channel_id=1, source_target_pairs={{0,8},{1,9},{2,10},{3,11},{4,12},{5,13},{6,14},{7,15},{8,0},{9,1},... | collective-permute-start | bytes 614408 | tf_op jit(solution)/shard_map/ppermute | solution.py:396
  104.7 11.0 %collective-permute-start.4 = (bf16[160,640]{1,0:T(8,128)(2,1)S(1)}, bf16[160,640]{1,0:T(8,128)(2,1)S(1)}, u32[]{:S(2)}, u32[]{:S(2)}) collective-permute-start(bf16[160,640]{1,0:T(8,128)(2,1)S(1)} %shard_map.158.refs_0_), channel_id=1, source_target_pairs={{0,12},{1,13},{2,14},{3,15},{4,8},{5,9},{6,10},{7,11},{8,4},{9,5},... | collective-permute-start | bytes 614408 | tf_op jit(solution)/shard_map/ppermute | solution.py:396
  106.7 9.0 %collective-permute-start.5 = (bf16[160,640]{1,0:T(8,128)(2,1)S(1)}, bf16[160,640]{1,0:T(8,128)(2,1)S(1)}, u32[]{:S(2)}, u32[]{:S(2)}) collective-permute-start(bf16[160,640]{1,0:T(8,128)(2,1)S(1)} %shard_map.158.refs_0_), channel_id=1, source_target_pairs={{0,2},{1,3},{2,0},{3,1},{4,6},{5,7},{6,4},{7,5},{8,10},{9,11},{10,... | collective-permute-start | bytes 614408 | tf_op jit(solution)/shard_map/ppermute | solution.py:396
  107.0 1.9 %collective-permute-start.2 = (bf16[160,640]{1,0:T(8,128)(2,1)S(1)}, bf16[160,640]{1,0:T(8,128)(2,1)S(1)}, u32[]{:S(2)}, u32[]{:S(2)}) collective-permute-start(bf16[160,640]{1,0:T(8,128)(2,1)S(1)} %collective-permute-done.refs_1_), channel_id=1, source_target_pairs={{0,1},{1,0},{2,3},{3,2},{4,5},{5,4},{6,7},{7,6},{8,9},{9,8},{10,11... | collective-permute-start | bytes 614408 | tf_op jit(solution)/shard_map/ppermute | solution.py:396
  115.7 2.4 %collective-permute-start.6 = (bf16[160,640]{1,0:T(8,128)(2,1)S(1)}, bf16[160,640]{1,0:T(8,128)(2,1)S(1)}, u32[]{:S(2)}, u32[]{:S(2)}) collective-permute-start(bf16[160,640]{1,0:T(8,128)(2,1)S(1)} %collective-permute-done.3.refs_0_), channel_id=1, source_target_pairs={{0,1},{1,0},{2,3},{3,2},{4,5},{5,4},{6,7},{7,6},{8,9},{9,8},{10,11... | collective-permute-start | bytes 614408 | tf_op jit(solution)/shard_map/ppermute | solution.py:396
  116.2 2.0 %collective-permute-start.7 = (bf16[160,640]{1,0:T(8,128)(2,1)S(1)}, bf16[160,640]{1,0:T(8,128)(2,1)S(1)}, u32[]{:S(2)}, u32[]{:S(2)}) collective-permute-start(bf16[160,640]{1,0:T(8,128)(2,1)S(1)} %collective-permute-done.4.refs_1_), channel_id=1, source_target_pairs={{0,1},{1,0},{2,3},{3,2},{4,5},{5,4},{6,7},{7,6},{8,9},{9,8},{10,11... | collective-permute-start | bytes 614408 | tf_op jit(solution)/shard_map/ppermute | solution.py:396
  116.2 1.9 %collective-permute-start.8 = (bf16[160,640]{1,0:T(8,128)(2,1)S(1)}, bf16[160,640]{1,0:T(8,128)(2,1)S(1)}, u32[]{:S(2)}, u32[]{:S(2)}) collective-permute-start(bf16[160,640]{1,0:T(8,128)(2,1)S(1)} %collective-permute-done.5.refs_0_), channel_id=1, source_target_pairs={{0,1},{1,0},{2,3},{3,2},{4,5},{5,4},{6,7},{7,6},{8,9},{9,8},{10,11... | collective-permute-start | bytes 614408 | tf_op jit(solution)/shard_map/ppermute | solution.py:396
  116.7 7.5 %collective-permute-start.9 = (bf16[160,640]{1,0:T(8,128)(2,1)S(1)}, bf16[160,640]{1,0:T(8,128)(2,1)S(1)}, u32[]{:S(2)}, u32[]{:S(2)}) collective-permute-start(bf16[160,640]{1,0:T(8,128)(2,1)S(1)} %collective-permute-done.refs_1_), channel_id=1, source_target_pairs={{0,2},{1,3},{2,0},{3,1},{4,6},{5,7},{6,4},{7,5},{8,10},{9,11},{10,... | collective-permute-start | bytes 614408 | tf_op jit(solution)/shard_map/ppermute | solution.py:396
  117.3 10.5 %collective-permute-start.10 = (bf16[160,640]{1,0:T(8,128)(2,1)S(1)}, bf16[160,640]{1,0:T(8,128)(2,1)S(1)}, u32[]{:S(2)}, u32[]{:S(2)}) collective-permute-start(bf16[160,640]{1,0:T(8,128)(2,1)S(1)} %collective-permute-done.3.refs_0_), channel_id=1, source_target_pairs={{0,2},{1,3},{2,0},{3,1},{4,6},{5,7},{6,4},{7,5},{8,10},{9,11},{10,... | collective-permute-start | bytes 614408 | tf_op jit(solution)/shard_map/ppermute | solution.py:396
  127.7 1.9 %collective-permute-start.11 = (bf16[160,640]{1,0:T(8,128)(2,1)S(1)}, bf16[160,640]{1,0:T(8,128)(2,1)S(1)}, u32[]{:S(2)}, u32[]{:S(2)}) collective-permute-start(bf16[160,640]{1,0:T(8,128)(2,1)S(1)} %collective-permute-done.9.refs_1_), channel_id=1, source_target_pairs={{0,1},{1,0},{2,3},{3,2},{4,5},{5,4},{6,7},{7,6},{8,9},{9,8},{10,11... | collective-permute-start | bytes 614408 | tf_op jit(solution)/shard_map/ppermute | solution.py:396
  128.6 7.1 %collective-permute-start.12 = (bf16[160,640]{1,0:T(8,128)(2,1)S(1)}, bf16[160,640]{1,0:T(8,128)(2,1)S(1)}, u32[]{:S(2)}, u32[]{:S(2)}) collective-permute-start(bf16[160,640]{1,0:T(8,128)(2,1)S(1)} %collective-permute-done.4.refs_1_), channel_id=1, source_target_pairs={{0,2},{1,3},{2,0},{3,1},{4,6},{5,7},{6,4},{7,5},{8,10},{9,11},{10,... | collective-permute-start | bytes 614408 | tf_op jit(solution)/shard_map/ppermute | solution.py:396
  129.1 6.5 %collective-permute-start.13 = (bf16[160,640]{1,0:T(8,128)(2,1)S(1)}, bf16[160,640]{1,0:T(8,128)(2,1)S(1)}, u32[]{:S(2)}, u32[]{:S(2)}) collective-permute-start(bf16[160,640]{1,0:T(8,128)(2,1)S(1)} %collective-permute-done.10.refs_0_), channel_id=1, source_target_pairs={{0,1},{1,0},{2,3},{3,2},{4,5},{5,4},{6,7},{7,6},{8,9},{9,8},{10,11... | collective-permute-start | bytes 614408 | tf_op jit(solution)/shard_map/ppermute | solution.py:396
  135.7 1.5 collective-permute-start.14
  (7 other events, 52.8 us)

commit v5 on v3

--- a/solution.py
+++ b/solution.py
@@ -234,7 +234,7 @@
     steps, me_ref, inter_ref, q_ref, k_ref, v_ref, g_ref, mid_ref, cross_ref, key_ref, valid_ref, valid_t_ref, wo_ref,
     *refs,
 ):
-    parts, (out_ref, extra, score_a, score_b, power_a, power_b) = refs[: 2 * GROUP], refs[2 * GROUP :]
+    parts, (out_ref, extra, score_a, score_b, power_a, power_b) = refs[:-6], refs[-6:]
     score, power = (score_a, score_b), (power_a, power_b)
     me = me_ref[0]
     chips = [(me // 2) ^ step for step in steps]
@@ -242,7 +242,7 @@
         for other in range(2):
             core = (me % 2) ^ other
             first = chips[n] * RI + core * CJ
-            part = parts[other * GROUP + n]
+            part = parts[other].at[n] if len(parts) == 2 else parts[other * GROUP + n]
             for s in range(CJ // 8):
                 to = pl.multiple_of(n * RI + core * CJ + 8 * s, 8)
                 crossing = cross_ref[pl.ds((first + 8 * s) // MB, 1), :]
@@ -388,8 +388,11 @@
         [VMEM],
     )(mid)
     hold = lax.optimization_barrier
-    one, two, three, beside = [swap(merged, 0, step) for step in (4, 8, 12, 2)]
-
+
+    def core(values):
+        return swap(values, 0, 1)
+
+    one, merged2 = swap(merged, 0, 4), core(merged)
     wqg = jnp.concatenate([qkvg_weight[:, :C], qkvg_weight[:, 3 * C :]], axis=1)
     q, k, v, g = call(
         qkvg_kernel,
@@ -398,6 +401,9 @@
         [VMEM] * 5,
     )(mid, norms, wqg, qkvg_weight[:, 2 * C : 3 * C], qkvg_weight[:, C : 2 * C].T)
 
+    merged, q, k, v, g = hold((merged, q, k, v, g))
+    two, three, beside = [swap(merged, 0, step) for step in (8, 12, 2)]
+
     def attend(steps, *parts):
         return call(
             functools.partial(attend_kernel, tuple(steps)),
@@ -405,30 +411,25 @@
             [pltpu.VMEM((H, CHUNK, N), F32)]
             + [pltpu.VMEM((CHUNK, N), F32)] * 2
             + [pltpu.VMEM((CHUNK, N), BF16)] * 2,
-            [SMEM, SMEM] + [VMEM] * 8 + [SMEM, VMEM] + [VMEM] * (2 * GROUP),
+            [SMEM, SMEM] + [VMEM] * 8 + [SMEM, VMEM] + [VMEM] * len(parts),
             pl.CostEstimate(flops=1 << 20, bytes_accessed=1 << 16, transcendentals=0),
         )(
             col_at[None], inter_chain, q, k, v, g, mid, cross, key_mask, valid_rows, valid_t, att_out_weight,
             *parts,
         )
 
-    def core(values):
-        return swap(values, 0, 1)
-
-    one_across = swap(one, 0, 2)
-    merged, near, merged2, near2, q, k, v, g = hold((merged, one, core(merged), core(one), q, k, v, g))
-    outs = [attend((0, 2), merged, near, merged2, near2)]
+    one_across = swap(one, ROWS // 2, 2)
+    near = hold((merged, one, merged2, core(one)))
+    outs = [attend((0, 2), *near)]
     outs[0], two, three, beside, one_across = hold((outs[0], two, three, beside, one_across))
-    two_across, three_across = swap(two, 0, 2), swap(three, 0, 2)
-    two, three, two2, three2, beside2, one_across2 = hold(
-        (two, three, core(two), core(three), core(beside), core(one_across))
-    )
-    outs.append(attend((4, 6), two, three, two2, three2))
-    outs[1], two_across = hold((outs[1], two_across))
-    two_across2 = core(two_across)
-    outs.append(attend((1, 3), beside, one_across, beside2, one_across2))
-    outs[2], three_across, two_across2 = hold((outs[2], three_across, two_across2))
-    outs.append(attend((5, 7), two_across, three_across, two_across2, core(three_across)))
+    column, across = jnp.stack([two, three]), jnp.stack([beside, one_across])
+    far = swap(column, ROWS // 2, 2)
+    column, across, column2, across2 = hold((column, across, core(column), core(across)))
+    outs.append(attend((4, 6), column, column2))
+    outs[1], across = hold((outs[1], across))
+    outs.append(attend((1, 3), across, across2))
+    outs[2], far = hold((outs[2], far))
+    outs.append(attend((5, 7), far, core(far)))
     out = call(order_kernel, struct((CJ, RI, C)), [], [SMEM] + [VMEM] * 4)(col_at[None], *outs)
     home = lax.all_to_all(out, "row", 0, 0, tiled=True)
     return call(turn_back_kernel, struct((RI, CJ, C)), [pltpu.VMEM((RI * CJ, C), F32)], [VMEM])(home)

time: 160 us -> 159 us (level)
    ppermute x15 -> x11, starting transfers between devices: 13.9 us -> 13.4 us  [swap(): return lax.ppermute(values, both, pairs)]
  transfers between devices with their start and end apart: 17 -> 13, of which waited for: 5 -> 3; matrix products, arithmetic and copies ran while one was open for 1% -> 1% of each run, Pallas kernels for 13% -> 13%
where the time goes in v5:
time: 159 us; the launch traced here: 158 us
  blocking collectives  56.9 us (36%)
  Pallas kernels  45.2 us (28%)
  waiting for transfers between devices  31.8 us (20%)
  starting transfers between devices  21.9 us (14%)
    all_to_all x1, blocking collectives, on_device(): channel = lax.all_to_all(parcels, both, 0, 0, tiled=True)  39 us
    pallas_call x4, Pallas kernels, attend(): call(functools.partial(attend_kernel, tuple(steps)), struct((GROUP * T, R...  24.2 us
    all_to_all x1, blocking collectives, on_device(): home = lax.all_to_all(out, 'row', 0, 0, tiled=True)  17.9 us
    all_to_all x1, waiting for transfers between devices, on_device(): returned = lax.all_to_all(product, both, 0, 0, tiled=True)  17.1 us
    ppermute x11, starting transfers between devices, swap(): return lax.ppermute(values, both, pairs)  13.4 us
    all_to_all x1, waiting for transfers between devices, on_device(): mid = lax.all_to_all(turned, 'row', 0, 0, tiled=True)  13.2 us
    pallas_call x1, Pallas kernels, on_device(): call(product_kernel, struct((C, BACK, C)), [pltpu.VMEM((C * SEND, C), F32...  7.16 us
    pallas_call x1, Pallas kernels, on_device(): call(project_kernel, [struct((C, SEND, C)), struct((A, N, C))], [pltpu.VM...  4.86 us
  transfers between devices with their start and end apart: 13, of which 3 were waited for; matrix products, arithmetic and copies ran while one was open for 1% of the time, Pallas kernels for 13%

profile of v5, /device:TPU:1, one launch (start us, length us, event | category | flops | bytes accessed | tf_op | source)
XLA Modules:
  0.0 158.4 jit_solution(16455103380273265033)
XLA Ops:
  0.0 4.9 %shard_map.154 = (bf16[128,56,128]{2,1,0:T(8,128)(2,1)}, bf16[5,640,128]{2,1,0:T(8,128)(2,1)}) custom-call(bf16[80,40,128]{2,1,0:T(8,128)(2,1)} %pair_hbm.1, s32[10]{0:T(128)} %valid_hbm.1, f32[128]{0:T(128)} %gain_hbm.1, f32[128]{0:T(128)} %bias_hbm.1, bf16[128,512]{1,0:T(8,128)(2,1)} %w_hbm.1), custom_call_target="tpu_custom_call" | custom-call | tf_op jit(solution)/shard_map/pallas_call | solution.py:326
  4.9 39.0 %all_to_all.20.in_ref = bf16[128,56,128]{2,1,0:T(8,128)(2,1)S(1)} all-to-all(bf16[128,56,128]{2,1,0:T(8,128)(2,1)} %get-tuple-element.33), channel_id=1, replica_groups=mesh['row'=8,'col'=16] {'row','col'}, dimensions={0} | all-to-all | bytes 3670016 | tf_op jit(solution)/shard_map/all_to_all | solution.py:343
  43.9 7.2 %shard_map.155 = bf16[128,32,128]{2,1,0:T(8,128)(2,1)} custom-call(bf16[128,56,128]{2,1,0:T(8,128)(2,1)S(1)} %all_to_all.20.in_ref), custom_call_target="tpu_custom_call" | custom-call | tf_op jit(solution)/shard_map/pallas_call | solution.py:344
  51.1 4.8 %all-to-all-start.1 = ((bf16[128,32,128]{2,1,0:T(8,128)(2,1)}), bf16[128,32,128]{2,1,0:T(8,128)(2,1)S(1)}, u32[]{:S(2)}, u32[]{:S(2)}) async-start(bf16[128,32,128]{2,1,0:T(8,128)(2,1)} %shard_map.155), calls=%async_computation.1 | async-start | bytes 2097152 | tf_op jit(solution)/shard_map/all_to_all | solution.py:356
  56.0 1.1 shard_map.156.gate_ref
  57.9 17.1 %all-to-all-done.1.in_ref = bf16[128,32,128]{2,1,0:T(8,128)(2,1)S(1)} async-done(((bf16[128,32,128]{2,1,0:T(8,128)(2,1)}), bf16[128,32,128]{2,1,0:T(8,128)(2,1)S(1)}, u32[]{:S(2)}, u32[]{:S(2)}) %all-to-all-start.1) | async-done | bytes 1048608 | tf_op jit(solution)/shard_map/all_to_all | solution.py:356
  75.1 4.4 %shard_map.157 = bf16[8,512,128]{2,1,0:T(8,128)(2,1)} custom-call(bf16[128,32,128]{2,1,0:T(8,128)(2,1)S(1)} %all-to-all-done.1.in_ref, bf16[5,640,128]{2,1,0:T(8,128)(2,1)S(1)} %copy-done, f32[5,640,128]{2,1,0:T(8,128)S(1)} %shard_map.156.gate_ref, f32[6,128]{1,0:T(8,128)S(1)} %stack.45.norms_ref, bf16[136,128]{1,0:T(8,128)(2,1)S(1)} %fusion.1.w_ref), custom_call_target="tpu_custom_call" | custom-call | tf_op jit(solution)/shard_map/pallas_call | solution.py:359
  79.5 3.7 %all-to-all-start.2 = ((bf16[8,512,128]{2,1,0:T(8,128)(2,1)}), bf16[8,512,128]{2,1,0:T(8,128)(2,1)S(1)}, u32[]{:S(2)}, u32[]{:S(2)}) async-start(bf16[8,512,128]{2,1,0:T(8,128)(2,1)} %shard_map.157), calls=%async_computation.2 | async-start | bytes 2097152 | tf_op jit(solution)/shard_map/all_to_all | solution.py:365
  83.8 13.2 %all-to-all-done.2.in_ref.mid_ref = bf16[8,512,128]{2,1,0:T(8,128)(2,1)S(1)} async-done(((bf16[8,512,128]{2,1,0:T(8,128)(2,1)}), bf16[8,512,128]{2,1,0:T(8,128)(2,1)S(1)}, u32[]{:S(2)}, u32[]{:S(2)}) %all-to-all-start.2) | async-done | bytes 1048608 | tf_op jit(solution)/shard_map/all_to_all | solution.py:365
  97.5 0.9 collective-permute-start
  98.4 2.3 %collective-permute-start.1 = (bf16[160,640]{1,0:T(8,128)(2,1)S(1)}, bf16[160,640]{1,0:T(8,128)(2,1)S(1)}, u32[]{:S(2)}, u32[]{:S(2)}) collective-permute-start(bf16[160,640]{1,0:T(8,128)(2,1)S(1)} %shard_map.158.refs_0_), channel_id=1, source_target_pairs={{0,1},{1,0},{2,3},{3,2},{4,5},{5,4},{6,7},{7,6},{8,9},{9,8},{10,11... | collective-permute-start | bytes 614408 | tf_op jit(solution)/shard_map/ppermute | solution.py:382
  101.3 1.6 %shard_map.159 = (bf16[5,640,128]{2,1,0:T(8,128)(2,1)S(1)}, bf16[5,128,640]{2,1,0:T(8,128)(2,1)S(1)}, bf16[5,640,256]{2,1,0:T(8,128)(2,1)S(1)}, f32[5,640,128]{2,1,0:T(8,128)S(1)}) custom-call(bf16[8,512,128]{2,1,0:T(8,128)(2,1)S(1)} %all-to-all-done.2.in_ref.mid_ref, f32[6,128]{1,0:T(8,128)S(1)} %stack.45.norms_ref, ...), custom_call_target="tpu_custom_call" | custom-call | tf_op jit(solution)/shard_map/pallas_call | solution.py:397
  103.0 2.0 %collective-permute-start.3 = (bf16[160,640]{1,0:T(8,128)(2,1)S(1)}, bf16[160,640]{1,0:T(8,128)(2,1)S(1)}, u32[]{:S(2)}, u32[]{:S(2)}) collective-permute-start(bf16[160,640]{1,0:T(8,128)(2,1)S(1)} %shard_map.158.refs_0_), channel_id=1, source_target_pairs={{0,8},{1,9},{2,10},{3,11},{4,12},{5,13},{6,14},{7,15},{8,0},{9,1},... | collective-permute-start | bytes 614408 | tf_op jit(solution)/shard_map/ppermute | solution.py:382
  105.0 2.0 %collective-permute-start.4 = (bf16[160,640]{1,0:T(8,128)(2,1)S(1)}, bf16[160,640]{1,0:T(8,128)(2,1)S(1)}, u32[]{:S(2)}, u32[]{:S(2)}) collective-permute-start(bf16[160,640]{1,0:T(8,128)(2,1)S(1)} %shard_map.158.refs_0_), channel_id=1, source_target_pairs={{0,12},{1,13},{2,14},{3,15},{4,8},{5,9},{6,10},{7,11},{8,4},{9,5},... | collective-permute-start | bytes 614408 | tf_op jit(solution)/shard_map/ppermute | solution.py:382
  107.2 0.8 collective-permute-start.2
  108.1 1.6 %collective-permute-start.6 = (bf16[160,640]{1,0:T(8,128)(2,1)S(1)}, bf16[160,640]{1,0:T(8,128)(2,1)S(1)}, u32[]{:S(2)}, u32[]{:S(2)}) collective-permute-start(bf16[160,640]{1,0:T(8,128)(2,1)S(1)} %collective-permute-done.refs_1_), channel_id=1, source_target_pairs={{0,66},{1,67},{2,64},{3,65},{4,70},{5,71},{6,68},{7,69},{8,74},{9,... | collective-permute-start | bytes 614408 | tf_op jit(solution)/shard_map/ppermute | solution.py:382
  110.0 6.0 %shard_map.160.refs_0_ = bf16[10,80,128]{2,1,0:T(8,128)(2,1)S(1)} custom-call(s32[1]{0:T(128)} %bitcast.me_ref, f32[4]{0:T(128)S(1)} %copy-done.3, bf16[5,640,128]{2,1,0:T(8,128)(2,1)S(1)} %get-tuple-element.39.q_ref, bf16[5,128,640]{2,1,0:T(8,128)(2,1)S(1)} %get-tuple-element.40.k_ref, bf16[5,640,256]{2,1,0:T(8,128)(2,1)S(1)} %get-tuple-element.41.v_ref, ...), custom_call_target="tpu_custom_call" | custom-call | flops 1048576 | bytes 65536 | tf_op jit(solution)/shard_map/pallas_call | solution.py:408
  117.1 1.9 %collective-permute-start.9 = (bf16[2,160,640]{2,1,0:T(8,128)(2,1)S(1)}, bf16[2,160,640]{2,1,0:T(8,128)(2,1)S(1)}, u32[]{:S(2)}, u32[]{:S(2)}) collective-permute-start(bf16[2,160,640]{2,1,0:T(8,128)(2,1)S(1)} %pad_maximum_fusion.refs_0_), channel_id=1, source_target_pairs={{0,66},{1,67},{2,64},{3,65},{4,70},{5,71},{6,68},{7,69},{8,74},{9,... | collective-permute-start | bytes 1228808 | tf_op jit(solution)/shard_map/ppermute | solution.py:382
  119.0 6.1 %shard_map.161.refs_1_ = bf16[10,80,128]{2,1,0:T(8,128)(2,1)S(1)} custom-call(s32[1]{0:T(128)} %bitcast.me_ref, f32[4]{0:T(128)S(1)} %copy-done.3, bf16[5,640,128]{2,1,0:T(8,128)(2,1)S(1)} %get-tuple-element.39.q_ref, bf16[5,128,640]{2,1,0:T(8,128)(2,1)S(1)} %get-tuple-element.40.k_ref, bf16[5,640,256]{2,1,0:T(8,128)(2,1)S(1)} %get-tuple-element.41.v_ref, ...), custom_call_target="tpu_custom_call" | custom-call | flops 1048576 | bytes 65536 | tf_op jit(solution)/shard_map/pallas_call | solution.py:408
  125.1 6.0 %shard_map.162.refs_2_ = bf16[10,80,128]{2,1,0:T(8,128)(2,1)S(1)} custom-call(s32[1]{0:T(128)} %bitcast.me_ref, f32[4]{0:T(128)S(1)} %copy-done.3, bf16[5,640,128]{2,1,0:T(8,128)(2,1)S(1)} %get-tuple-element.39.q_ref, bf16[5,128,640]{2,1,0:T(8,128)(2,1)S(1)} %get-tuple-element.40.k_ref, bf16[5,640,256]{2,1,0:T(8,128)(2,1)S(1)} %get-tuple-element.41.v_ref, ...), custom_call_target="tpu_custom_call" | custom-call | flops 1048576 | bytes 65536 | tf_op jit(solution)/shard_map/pallas_call | solution.py:408
  131.7 1.4 collective-permute-done.10.refs_1_
  133.1 6.0 %shard_map.163.refs_3_ = bf16[10,80,128]{2,1,0:T(8,128)(2,1)S(1)} custom-call(s32[1]{0:T(128)} %bitcast.me_ref, f32[4]{0:T(128)S(1)} %copy-done.3, bf16[5,640,128]{2,1,0:T(8,128)(2,1)S(1)} %get-tuple-element.39.q_ref, bf16[5,128,640]{2,1,0:T(8,128)(2,1)S(1)} %get-tuple-element.40.k_ref, bf16[5,640,256]{2,1,0:T(8,128)(2,1)S(1)} %get-tuple-element.41.v_ref, ...), custom_call_target="tpu_custom_call" | custom-call | flops 1048576 | bytes 65536 | tf_op jit(solution)/shard_map/pallas_call | solution.py:408
  139.2 17.9 %all_to_all.21.in_ref = bf16[40,80,128]{2,1,0:T(8,128)(2,1)S(1)} all-to-all(bf16[40,80,128]{2,1,0:T(8,128)(2,1)S(1)} %shard_map.164), channel_id=1, replica_groups=mesh['row'=8,'col'=16] {'row'}, dimensions={0} | all-to-all | bytes 1638400 | tf_op jit(solution)/shard_map/all_to_all | solution.py:434
  157.1 1.3 shard_map.165
  (68 shorter events, 4.6 us)
Async XLA Ops:
  51.0 4.9 %copy-start.5 = (f32[128]{0:T(128)S(1)}, f32[128]{0:T(128)}, u32[]{:S(2)}) copy-start(f32[128]{0:T(128)} %gain_hbm.1) | copy-start | bytes 1540
  51.0 4.9 %copy-start.6 = (f32[128]{0:T(128)S(1)}, f32[128]{0:T(128)}, u32[]{:S(2)}) copy-start(f32[128]{0:T(128)} %bias_hbm.1) | copy-start | bytes 1540
  51.0 4.9 %copy-start.10 = (f32[128]{0:T(128)S(1)}, f32[128]{0:T(128)}, u32[]{:S(2)}) copy-start(f32[128]{0:T(128)} %param.23) | copy-start | bytes 1540
  51.0 4.9 %copy-start.11 = (f32[128]{0:T(128)S(1)}, f32[128]{0:T(128)}, u32[]{:S(2)}) copy-start(f32[128]{0:T(128)} %param.24) | copy-start | bytes 1540
  51.0 4.9 %copy-start.12 = (f32[128]{0:T(128)S(1)}, f32[128]{0:T(128)}, u32[]{:S(2)}) copy-start(f32[128]{0:T(128)} %param.26) | copy-start | bytes 1540
  51.0 4.9 %copy-start.13 = (f32[128]{0:T(128)S(1)}, f32[128]{0:T(128)}, u32[]{:S(2)}) copy-start(f32[128]{0:T(128)} %param.27) | copy-start | bytes 1540
  51.0 5.0 %copy-start = (bf16[5,640,128]{2,1,0:T(8,128)(2,1)S(1)}, bf16[5,640,128]{2,1,0:T(8,128)(2,1)}, u32[]{:S(2)}) copy-start(bf16[5,640,128]{2,1,0:T(8,128)(2,1)} %get-tuple-element.34.x_ref) | copy-start | bytes 2457604
  51.1 4.9 %copy-start.2 = (bf16[128,128]{1,0:T(8,128)(2,1)S(1)}, bf16[128,128]{1,0:T(8,128)(2,1)}, u32[]{:S(2)}) copy-start(bf16[128,128]{1,0:T(8,128)(2,1)} %w_ref.1) | copy-start | bytes 98308
  51.1 24.0 %all-to-all-start.1 = ((bf16[128,32,128]{2,1,0:T(8,128)(2,1)}), bf16[128,32,128]{2,1,0:T(8,128)(2,1)S(1)}, u32[]{:S(2)}, u32[]{:S(2)}) async-start(bf16[128,32,128]{2,1,0:T(8,128)(2,1)} %shard_map.155), calls=%async_computation.1 | async-start | bytes 2097152 | tf_op jit(solution)/shard_map/all_to_all | solution.py:356
  79.5 4.3 %copy-start.4 = (bf16[128,512]{1,0:T(8,128)(2,1)S(1)}, bf16[128,512]{1,0:T(8,128)(2,1)}, u32[]{:S(2)}) copy-start(bf16[128,512]{1,0:T(8,128)(2,1)} %param.28) | copy-start | bytes 393220
  79.5 17.5 %all-to-all-start.2 = ((bf16[8,512,128]{2,1,0:T(8,128)(2,1)}), bf16[8,512,128]{2,1,0:T(8,128)(2,1)S(1)}, u32[]{:S(2)}, u32[]{:S(2)}) async-start(bf16[8,512,128]{2,1,0:T(8,128)(2,1)} %shard_map.157), calls=%async_computation.2 | async-start | bytes 2097152 | tf_op jit(solution)/shard_map/all_to_all | solution.py:365
  83.8 26.2 %copy-start.1 = (bf16[128,128]{1,0:T(8,128)(2,1)S(1)}, bf16[128,128]{1,0:T(8,128)(2,1)}, u32[]{:S(2)}) copy-start(bf16[128,128]{1,0:T(8,128)(2,1)} %wo_ref.7) | copy-start | bytes 98308
  83.8 26.2 %copy-start.3 = (f32[4]{0:T(128)S(1)}, f32[4]{0:T(128)}, u32[]{:S(2)}) copy-start(f32[4]{0:T(128)} %inter_ref.7) | copy-start | bytes 52
  97.5 9.7 %collective-permute-start = (bf16[160,640]{1,0:T(8,128)(2,1)S(1)}, bf16[160,640]{1,0:T(8,128)(2,1)S(1)}, u32[]{:S(2)}, u32[]{:S(2)}) collective-permute-start(bf16[160,640]{1,0:T(8,128)(2,1)S(1)} %shard_map.158.refs_0_), channel_id=1, source_target_pairs={{0,4},{1,5},{2,6},{3,7},{4,0},{5,1},{6,2},{7,3},{8,12},{9,13},{10,... | collective-permute-start | bytes 614408 | tf_op jit(solution)/shard_map/ppermute | solution.py:382
  98.4 9.7 %collective-permute-start.1 = (bf16[160,640]{1,0:T(8,128)(2,1)S(1)}, bf16[160,640]{1,0:T(8,128)(2,1)S(1)}, u32[]{:S(2)}, u32[]{:S(2)}) collective-permute-start(bf16[160,640]{1,0:T(8,128)(2,1)S(1)} %shard_map.158.refs_0_), channel_id=1, source_target_pairs={{0,1},{1,0},{2,3},{3,2},{4,5},{5,4},{6,7},{7,6},{8,9},{9,8},{10,11... | collective-permute-start | bytes 614408 | tf_op jit(solution)/shard_map/ppermute | solution.py:382
  103.0 13.1 %collective-permute-start.3 = (bf16[160,640]{1,0:T(8,128)(2,1)S(1)}, bf16[160,640]{1,0:T(8,128)(2,1)S(1)}, u32[]{:S(2)}, u32[]{:S(2)}) collective-permute-start(bf16[160,640]{1,0:T(8,128)(2,1)S(1)} %shard_map.158.refs_0_), channel_id=1, source_target_pairs={{0,8},{1,9},{2,10},{3,11},{4,12},{5,13},{6,14},{7,15},{8,0},{9,1},... | collective-permute-start | bytes 614408 | tf_op jit(solution)/shard_map/ppermute | solution.py:382
  105.0 11.1 %collective-permute-start.4 = (bf16[160,640]{1,0:T(8,128)(2,1)S(1)}, bf16[160,640]{1,0:T(8,128)(2,1)S(1)}, u32[]{:S(2)}, u32[]{:S(2)}) collective-permute-start(bf16[160,640]{1,0:T(8,128)(2,1)S(1)} %shard_map.158.refs_0_), channel_id=1, source_target_pairs={{0,12},{1,13},{2,14},{3,15},{4,8},{5,9},{6,10},{7,11},{8,4},{9,5},... | collective-permute-start | bytes 614408 | tf_op jit(solution)/shard_map/ppermute | solution.py:382
  106.9 9.1 %collective-permute-start.5 = (bf16[160,640]{1,0:T(8,128)(2,1)S(1)}, bf16[160,640]{1,0:T(8,128)(2,1)S(1)}, u32[]{:S(2)}, u32[]{:S(2)}) collective-permute-start(bf16[160,640]{1,0:T(8,128)(2,1)S(1)} %shard_map.158.refs_0_), channel_id=1, source_target_pairs={{0,2},{1,3},{2,0},{3,1},{4,6},{5,7},{6,4},{7,5},{8,10},{9,11},{10,... | collective-permute-start | bytes 614408 | tf_op jit(solution)/shard_map/ppermute | solution.py:382
  107.2 2.6 %collective-permute-start.2 = (bf16[160,640]{1,0:T(8,128)(2,1)S(1)}, bf16[160,640]{1,0:T(8,128)(2,1)S(1)}, u32[]{:S(2)}, u32[]{:S(2)}) collective-permute-start(bf16[160,640]{1,0:T(8,128)(2,1)S(1)} %collective-permute-done.refs_1_), channel_id=1, source_target_pairs={{0,1},{1,0},{2,3},{3,2},{4,5},{5,4},{6,7},{7,6},{8,9},{9,8},{10,11... | collective-permute-start | bytes 614408 | tf_op jit(solution)/shard_map/ppermute | solution.py:382
  108.1 8.0 %collective-permute-start.6 = (bf16[160,640]{1,0:T(8,128)(2,1)S(1)}, bf16[160,640]{1,0:T(8,128)(2,1)S(1)}, u32[]{:S(2)}, u32[]{:S(2)}) collective-permute-start(bf16[160,640]{1,0:T(8,128)(2,1)S(1)} %collective-permute-done.refs_1_), channel_id=1, source_target_pairs={{0,66},{1,67},{2,64},{3,65},{4,70},{5,71},{6,68},{7,69},{8,74},{9,... | collective-permute-start | bytes 614408 | tf_op jit(solution)/shard_map/ppermute | solution.py:382
  116.1 2.9 %collective-permute-start.7 = (bf16[2,160,640]{2,1,0:T(8,128)(2,1)S(1)}, bf16[2,160,640]{2,1,0:T(8,128)(2,1)S(1)}, u32[]{:S(2)}, u32[]{:S(2)}) collective-permute-start(bf16[2,160,640]{2,1,0:T(8,128)(2,1)S(1)} %pad_maximum_fusion.refs_0_), channel_id=1, source_target_pairs={{0,1},{1,0},{2,3},{3,2},{4,5},{5,4},{6,7},{7,6},{8,9},{9,8},{10,11... | collective-permute-start | bytes 1228808 | tf_op jit(solution)/shard_map/ppermute | solution.py:382
  117.0 2.0 %collective-permute-start.8 = (bf16[2,160,640]{2,1,0:T(8,128)(2,1)S(1)}, bf16[2,160,640]{2,1,0:T(8,128)(2,1)S(1)}, u32[]{:S(2)}, u32[]{:S(2)}) collective-permute-start(bf16[2,160,640]{2,1,0:T(8,128)(2,1)S(1)} %pad_maximum_fusion.1.refs_0_), channel_id=1, source_target_pairs={{0,1},{1,0},{2,3},{3,2},{4,5},{5,4},{6,7},{7,6},{8,9},{9,8},{10,11... | collective-permute-start | bytes 1228808 | tf_op jit(solution)/shard_map/ppermute | solution.py:382
  117.1 14.0 %collective-permute-start.9 = (bf16[2,160,640]{2,1,0:T(8,128)(2,1)S(1)}, bf16[2,160,640]{2,1,0:T(8,128)(2,1)S(1)}, u32[]{:S(2)}, u32[]{:S(2)}) collective-permute-start(bf16[2,160,640]{2,1,0:T(8,128)(2,1)S(1)} %pad_maximum_fusion.refs_0_), channel_id=1, source_target_pairs={{0,66},{1,67},{2,64},{3,65},{4,70},{5,71},{6,68},{7,69},{8,74},{9,... | collective-permute-start | bytes 1228808 | tf_op jit(solution)/shard_map/ppermute | solution.py:382
  131.1 1.9 %collective-permute-start.10 = (bf16[2,160,640]{2,1,0:T(8,128)(2,1)S(1)}, bf16[2,160,640]{2,1,0:T(8,128)(2,1)S(1)}, u32[]{:S(2)}, u32[]{:S(2)}) collective-permute-start(bf16[2,160,640]{2,1,0:T(8,128)(2,1)S(1)} %collective-permute-done.9.refs_0_), channel_id=1, source_target_pairs={{0,1},{1,0},{2,3},{3,2},{4,5},{5,4},{6,7},{7,6},{8,9},{9,8},{10,11... | collective-permute-start | bytes 1228808 | tf_op jit(solution)/shard_map/ppermute | solution.py:382
  (3 other events, 8.9 us)

commit v6 on v5

--- a/solution.py
+++ b/solution.py
@@ -23,8 +23,7 @@
 A = CJ // 8
 TURN = T * RI
 PAY = 112
-GROUP = 2
-CHUNK = GROUP * RI
+CALLS = ((0, 2), (4, 6, 1, 3), (5, 7))
 
 MASK_NEG = 10000.0
 EPS = 1e-05
@@ -238,11 +237,15 @@
     score, power = (score_a, score_b), (power_a, power_b)
     me = me_ref[0]
     chips = [(me // 2) ^ step for step in steps]
-    for n in range(GROUP):
+    count = len(chips)
+    chunk = count * RI
+    late = count == 2
+    for n in range(count):
         for other in range(2):
             core = (me % 2) ^ other
             first = chips[n] * RI + core * CJ
-            part = parts[other].at[n] if len(parts) == 2 else parts[other * GROUP + n]
+            half = parts[other * len(parts) // 2 : (other + 1) * len(parts) // 2]
+            part = half[n] if len(half) == count else half[n // 2].at[n % 2]
             for s in range(CJ // 8):
                 to = pl.multiple_of(n * RI + core * CJ + 8 * s, 8)
                 crossing = cross_ref[pl.ds((first + 8 * s) // MB, 1), :]
@@ -252,7 +255,7 @@
                         + inter_ref[h] * crossing
                         + key_ref[...]
                     )
-    lane_head = lax.broadcasted_iota(jnp.int32, (CHUNK, C), 1) // DH
+    lane_head = lax.broadcasted_iota(jnp.int32, (chunk, C), 1) // DH
 
     def rows_of(take):
         return jnp.concatenate([take(pl.ds(pl.multiple_of(chip * RI, RI), RI)) for chip in chips], axis=0)
@@ -266,24 +269,29 @@
             own = jnp.where(lane_head == h, queries, jnp.zeros_like(queries))
             score[h % 2][...] = dot(own, k_ref[t], ((1,), (0,))) + extra[h]
 
-        total = jnp.zeros((CHUNK, C), F32)
+        def weigh(h, total):
+            sums = dot(power[h % 2][...], v_ref[t], ((1,), (0,)))
+            return jnp.where(lane_head == h, sums[:, :C] / sums[:, C:], total)
+
+        total = jnp.zeros((chunk, C), F32)
         set_score(0)
-        for h in range(H + 1):
+        for h in range(H + late):
             if h + 1 < H:
                 set_score(h + 1)
-            if h > 0:
-                sums = dot(power[(h - 1) % 2][...], v_ref[t], ((1,), (0,)))
-                total = jnp.where(lane_head == h - 1, sums[:, :C] / sums[:, C:], total)
+            if late and h > 0:
+                total = weigh(h - 1, total)
             if h < H:
                 now = score[h % 2][...]
                 highest = jnp.max(now, axis=1, keepdims=True)
                 power[h % 2][...] = jnp.exp(now - highest).astype(BF16)
+            if not late:
+                total = weigh(h, total)
         gated = (rows_of(lambda rows: g_ref[t, rows, :]) * total).astype(BF16)
         update = dot(gated, wo_ref[...], ((1,), (0,)))
         own = pl.ds(pl.multiple_of(t * RI, RI), RI)
         mid = jnp.concatenate([mid_ref[chip, own, :] for chip in chips], axis=0).astype(F32)
         out = (mid + valid * valid_t_ref[t] * update).astype(BF16)
-        for n in range(GROUP):
+        for n in range(count):
             out_ref[n * T + t] = out[n * RI : (n + 1) * RI]
         return carry
 
@@ -292,10 +300,10 @@
 
 def order_kernel(me_ref, *refs):
     out_ref = refs[-1]
-    for step in range(ROWS):
+    for call_at, n, step in [(c, n, step) for c, steps in enumerate(CALLS) for n, step in enumerate(steps)]:
         chip = (me_ref[0] // 2) ^ step
         for t in range(T):
-            out_ref[chip * T + t] = refs[step % 2 * 2 + step // 4][step % 4 // 2 * T + t]
+            out_ref[chip * T + t] = refs[call_at][n * T + t]
 
 
 def on_device(
@@ -405,12 +413,13 @@
     two, three, beside = [swap(merged, 0, step) for step in (8, 12, 2)]
 
     def attend(steps, *parts):
+        chunk = len(steps) * RI
         return call(
-            functools.partial(attend_kernel, tuple(steps)),
-            struct((GROUP * T, RI, C)),
-            [pltpu.VMEM((H, CHUNK, N), F32)]
-            + [pltpu.VMEM((CHUNK, N), F32)] * 2
-            + [pltpu.VMEM((CHUNK, N), BF16)] * 2,
+            functools.partial(attend_kernel, steps),
+            struct((len(steps) * T, RI, C)),
+            [pltpu.VMEM((H, chunk, N), F32)]
+            + [pltpu.VMEM((chunk, N), F32)] * 2
+            + [pltpu.VMEM((chunk, N), BF16)] * 2,
             [SMEM, SMEM] + [VMEM] * 8 + [SMEM, VMEM] + [VMEM] * len(parts),
             pl.CostEstimate(flops=1 << 20, bytes_accessed=1 << 16, transcendentals=0),
         )(
@@ -420,17 +429,15 @@
 
     one_across = swap(one, ROWS // 2, 2)
     near = hold((merged, one, merged2, core(one)))
-    outs = [attend((0, 2), *near)]
+    outs = [attend(CALLS[0], *near)]
     outs[0], two, three, beside, one_across = hold((outs[0], two, three, beside, one_across))
     column, across = jnp.stack([two, three]), jnp.stack([beside, one_across])
     far = swap(column, ROWS // 2, 2)
     column, across, column2, across2 = hold((column, across, core(column), core(across)))
-    outs.append(attend((4, 6), column, column2))
-    outs[1], across = hold((outs[1], across))
-    outs.append(attend((1, 3), across, across2))
-    outs[2], far = hold((outs[2], far))
-    outs.append(attend((5, 7), far, core(far)))
-    out = call(order_kernel, struct((CJ, RI, C)), [], [SMEM] + [VMEM] * 4)(col_at[None], *outs)
+    outs.append(attend(CALLS[1], column, across, column2, across2))
+    outs[1], far = hold((outs[1], far))
+    outs.append(attend(CALLS[2], far, core(far)))
+    out = call(order_kernel, struct((CJ, RI, C)), [], [SMEM] + [VMEM] * 3)(col_at[None], *outs)
     home = lax.all_to_all(out, "row", 0, 0, tiled=True)
     return call(turn_back_kernel, struct((RI, CJ, C)), [pltpu.VMEM((RI * CJ, C), F32)], [VMEM])(home)
 

time: 159 us -> 158 us (level)
    pallas_call x5 -> x4, Pallas kernels: 24.2 us -> 23.2 us  [the longest x3 23.1 us: attend(): call(functools.partial(attend_kernel, steps), struct((len(steps) * T, RI,...]
  transfers between devices with their start and end apart: 13 -> 13, of which waited for: 3 -> 4; matrix products, arithmetic and copies ran while one was open for 1% -> 1% of each run, Pallas kernels for 13% -> 12%
where the time goes in v6:
time: 158 us; the launch traced here: 157 us
  blocking collectives  56.5 us (36%)
  Pallas kernels  44.2 us (28%)
  waiting for transfers between devices  31.9 us (20%)
  starting transfers between devices  22 us (14%)
    all_to_all x1, blocking collectives, on_device(): channel = lax.all_to_all(parcels, both, 0, 0, tiled=True)  39 us
    pallas_call x3, Pallas kernels, attend(): call(functools.partial(attend_kernel, steps), struct((len(steps) * T, RI,...  23.1 us
    all_to_all x1, blocking collectives, on_device(): home = lax.all_to_all(out, 'row', 0, 0, tiled=True)  17.6 us
    all_to_all x1, waiting for transfers between devices, on_device(): returned = lax.all_to_all(product, both, 0, 0, tiled=True)  17.1 us
    ppermute x11, starting transfers between devices, swap(): return lax.ppermute(values, both, pairs)  13.5 us
    all_to_all x1, waiting for transfers between devices, on_device(): mid = lax.all_to_all(turned, 'row', 0, 0, tiled=True)  13.2 us
    pallas_call x1, Pallas kernels, on_device(): call(product_kernel, struct((C, BACK, C)), [pltpu.VMEM((C * SEND, C), F32...  7.16 us
    pallas_call x1, Pallas kernels, on_device(): call(project_kernel, [struct((C, SEND, C)), struct((A, N, C))], [pltpu.VM...  4.86 us
  transfers between devices with their start and end apart: 13, of which 4 were waited for; matrix products, arithmetic and copies ran while one was open for 1% of the time, Pallas kernels for 12%

profile of v6, /device:TPU:1, one launch (start us, length us, event | category | flops | bytes accessed | tf_op | source)
XLA Modules:
  0.0 157.2 jit_solution(11816979477455987139)
XLA Ops:
  0.0 4.9 %shard_map.154 = (bf16[128,56,128]{2,1,0:T(8,128)(2,1)}, bf16[5,640,128]{2,1,0:T(8,128)(2,1)}) custom-call(bf16[80,40,128]{2,1,0:T(8,128)(2,1)} %pair_hbm.1, s32[10]{0:T(128)} %valid_hbm.1, f32[128]{0:T(128)} %gain_hbm.1, f32[128]{0:T(128)} %bias_hbm.1, bf16[128,512]{1,0:T(8,128)(2,1)} %w_hbm.1), custom_call_target="tpu_custom_call" | custom-call | tf_op jit(solution)/shard_map/pallas_call | solution.py:334
  4.9 39.0 %all_to_all.20.in_ref = bf16[128,56,128]{2,1,0:T(8,128)(2,1)S(1)} all-to-all(bf16[128,56,128]{2,1,0:T(8,128)(2,1)} %get-tuple-element.31), channel_id=1, replica_groups=mesh['row'=8,'col'=16] {'row','col'}, dimensions={0} | all-to-all | bytes 3670016 | tf_op jit(solution)/shard_map/all_to_all | solution.py:351
  43.9 7.2 %shard_map.155 = bf16[128,32,128]{2,1,0:T(8,128)(2,1)} custom-call(bf16[128,56,128]{2,1,0:T(8,128)(2,1)S(1)} %all_to_all.20.in_ref), custom_call_target="tpu_custom_call" | custom-call | tf_op jit(solution)/shard_map/pallas_call | solution.py:352
  51.1 4.8 %all-to-all-start.1 = ((bf16[128,32,128]{2,1,0:T(8,128)(2,1)}), bf16[128,32,128]{2,1,0:T(8,128)(2,1)S(1)}, u32[]{:S(2)}, u32[]{:S(2)}) async-start(bf16[128,32,128]{2,1,0:T(8,128)(2,1)} %shard_map.155), calls=%async_computation.1 | async-start | bytes 2097152 | tf_op jit(solution)/shard_map/all_to_all | solution.py:364
  56.0 1.1 shard_map.156.gate_ref
  57.9 17.1 %all-to-all-done.1.in_ref = bf16[128,32,128]{2,1,0:T(8,128)(2,1)S(1)} async-done(((bf16[128,32,128]{2,1,0:T(8,128)(2,1)}), bf16[128,32,128]{2,1,0:T(8,128)(2,1)S(1)}, u32[]{:S(2)}, u32[]{:S(2)}) %all-to-all-start.1) | async-done | bytes 1048608 | tf_op jit(solution)/shard_map/all_to_all | solution.py:364
  75.1 4.4 %shard_map.157 = bf16[8,512,128]{2,1,0:T(8,128)(2,1)} custom-call(bf16[128,32,128]{2,1,0:T(8,128)(2,1)S(1)} %all-to-all-done.1.in_ref, bf16[5,640,128]{2,1,0:T(8,128)(2,1)S(1)} %copy-done, f32[5,640,128]{2,1,0:T(8,128)S(1)} %shard_map.156.gate_ref, f32[6,128]{1,0:T(8,128)S(1)} %stack.45.norms_ref, bf16[136,128]{1,0:T(8,128)(2,1)S(1)} %fusion.1.w_ref), custom_call_target="tpu_custom_call" | custom-call | tf_op jit(solution)/shard_map/pallas_call | solution.py:367
  79.5 3.7 %all-to-all-start.2 = ((bf16[8,512,128]{2,1,0:T(8,128)(2,1)}), bf16[8,512,128]{2,1,0:T(8,128)(2,1)S(1)}, u32[]{:S(2)}, u32[]{:S(2)}) async-start(bf16[8,512,128]{2,1,0:T(8,128)(2,1)} %shard_map.157), calls=%async_computation.2 | async-start | bytes 2097152 | tf_op jit(solution)/shard_map/all_to_all | solution.py:373
  83.8 13.2 %all-to-all-done.2.in_ref.mid_ref = bf16[8,512,128]{2,1,0:T(8,128)(2,1)S(1)} async-done(((bf16[8,512,128]{2,1,0:T(8,128)(2,1)}), bf16[8,512,128]{2,1,0:T(8,128)(2,1)S(1)}, u32[]{:S(2)}, u32[]{:S(2)}) %all-to-all-start.2) | async-done | bytes 1048608 | tf_op jit(solution)/shard_map/all_to_all | solution.py:373
  97.5 0.9 collective-permute-start
  98.4 2.3 %collective-permute-start.1 = (bf16[160,640]{1,0:T(8,128)(2,1)S(1)}, bf16[160,640]{1,0:T(8,128)(2,1)S(1)}, u32[]{:S(2)}, u32[]{:S(2)}) collective-permute-start(bf16[160,640]{1,0:T(8,128)(2,1)S(1)} %shard_map.158.refs_0_), channel_id=1, source_target_pairs={{0,1},{1,0},{2,3},{3,2},{4,5},{5,4},{6,7},{7,6},{8,9},{9,8},{10,11... | collective-permute-start | bytes 614408 | tf_op jit(solution)/shard_map/ppermute | solution.py:390
  101.3 1.6 %shard_map.159 = (bf16[5,640,128]{2,1,0:T(8,128)(2,1)S(1)}, bf16[5,128,640]{2,1,0:T(8,128)(2,1)S(1)}, bf16[5,640,256]{2,1,0:T(8,128)(2,1)S(1)}, f32[5,640,128]{2,1,0:T(8,128)S(1)}) custom-call(bf16[8,512,128]{2,1,0:T(8,128)(2,1)S(1)} %all-to-all-done.2.in_ref.mid_ref, f32[6,128]{1,0:T(8,128)S(1)} %stack.45.norms_ref, ...), custom_call_target="tpu_custom_call" | custom-call | tf_op jit(solution)/shard_map/pallas_call | solution.py:405
  103.0 2.0 %collective-permute-start.3 = (bf16[160,640]{1,0:T(8,128)(2,1)S(1)}, bf16[160,640]{1,0:T(8,128)(2,1)S(1)}, u32[]{:S(2)}, u32[]{:S(2)}) collective-permute-start(bf16[160,640]{1,0:T(8,128)(2,1)S(1)} %shard_map.158.refs_0_), channel_id=1, source_target_pairs={{0,8},{1,9},{2,10},{3,11},{4,12},{5,13},{6,14},{7,15},{8,0},{9,1},... | collective-permute-start | bytes 614408 | tf_op jit(solution)/shard_map/ppermute | solution.py:390
  105.0 2.0 %collective-permute-start.4 = (bf16[160,640]{1,0:T(8,128)(2,1)S(1)}, bf16[160,640]{1,0:T(8,128)(2,1)S(1)}, u32[]{:S(2)}, u32[]{:S(2)}) collective-permute-start(bf16[160,640]{1,0:T(8,128)(2,1)S(1)} %shard_map.158.refs_0_), channel_id=1, source_target_pairs={{0,12},{1,13},{2,14},{3,15},{4,8},{5,9},{6,10},{7,11},{8,4},{9,5},... | collective-permute-start | bytes 614408 | tf_op jit(solution)/shard_map/ppermute | solution.py:390
  107.2 0.8 collective-permute-start.2
  108.1 1.6 %collective-permute-start.6 = (bf16[160,640]{1,0:T(8,128)(2,1)S(1)}, bf16[160,640]{1,0:T(8,128)(2,1)S(1)}, u32[]{:S(2)}, u32[]{:S(2)}) collective-permute-start(bf16[160,640]{1,0:T(8,128)(2,1)S(1)} %collective-permute-done.refs_1_), channel_id=1, source_target_pairs={{0,66},{1,67},{2,64},{3,65},{4,70},{5,71},{6,68},{7,69},{8,74},{9,... | collective-permute-start | bytes 614408 | tf_op jit(solution)/shard_map/ppermute | solution.py:390
  110.0 6.4 %shard_map.160.refs_0_ = bf16[10,80,128]{2,1,0:T(8,128)(2,1)S(1)} custom-call(s32[1]{0:T(128)} %bitcast.me_ref, f32[4]{0:T(128)S(1)} %copy-done.3, bf16[5,640,128]{2,1,0:T(8,128)(2,1)S(1)} %get-tuple-element.37.q_ref, bf16[5,128,640]{2,1,0:T(8,128)(2,1)S(1)} %get-tuple-element.38.k_ref, bf16[5,640,256]{2,1,0:T(8,128)(2,1)S(1)} %get-tuple-element.39.v_ref, ...), custom_call_target="tpu_custom_call" | custom-call | flops 1048576 | bytes 65536 | tf_op jit(solution)/shard_map/pallas_call | solution.py:417
  117.2 1.8 %collective-permute-start.9 = (bf16[2,160,640]{2,1,0:T(8,128)(2,1)S(1)}, bf16[2,160,640]{2,1,0:T(8,128)(2,1)S(1)}, u32[]{:S(2)}, u32[]{:S(2)}) collective-permute-start(bf16[2,160,640]{2,1,0:T(8,128)(2,1)S(1)} %pad_maximum_fusion.refs_0_), channel_id=1, source_target_pairs={{0,66},{1,67},{2,64},{3,65},{4,70},{5,71},{6,68},{7,69},{8,74},{9,... | collective-permute-start | bytes 1228808 | tf_op jit(solution)/shard_map/ppermute | solution.py:390
  119.0 10.3 %shard_map.161.refs_1_ = bf16[20,80,128]{2,1,0:T(8,128)(2,1)S(1)} custom-call(s32[1]{0:T(128)} %bitcast.me_ref, f32[4]{0:T(128)S(1)} %copy-done.3, bf16[5,640,128]{2,1,0:T(8,128)(2,1)S(1)} %get-tuple-element.37.q_ref, bf16[5,128,640]{2,1,0:T(8,128)(2,1)S(1)} %get-tuple-element.38.k_ref, bf16[5,640,256]{2,1,0:T(8,128)(2,1)S(1)} %get-tuple-element.39.v_ref, ...), custom_call_target="tpu_custom_call" | custom-call | flops 1048576 | bytes 65536 | tf_op jit(solution)/shard_map/pallas_call | solution.py:417
  129.5 1.0 collective-permute-start.10
  130.5 1.4 collective-permute-done.10.refs_1_
  131.8 6.4 %shard_map.162.refs_2_ = bf16[10,80,128]{2,1,0:T(8,128)(2,1)S(1)} custom-call(s32[1]{0:T(128)} %bitcast.me_ref, f32[4]{0:T(128)S(1)} %copy-done.3, bf16[5,640,128]{2,1,0:T(8,128)(2,1)S(1)} %get-tuple-element.37.q_ref, bf16[5,128,640]{2,1,0:T(8,128)(2,1)S(1)} %get-tuple-element.38.k_ref, bf16[5,640,256]{2,1,0:T(8,128)(2,1)S(1)} %get-tuple-element.39.v_ref, ...), custom_call_target="tpu_custom_call" | custom-call | flops 1048576 | bytes 65536 | tf_op jit(solution)/shard_map/pallas_call | solution.py:417
  138.3 17.6 %all_to_all.21.in_ref = bf16[40,80,128]{2,1,0:T(8,128)(2,1)S(1)} all-to-all(bf16[40,80,128]{2,1,0:T(8,128)(2,1)S(1)} %shard_map.163), channel_id=1, replica_groups=mesh['row'=8,'col'=16] {'row'}, dimensions={0} | all-to-all | bytes 1638400 | tf_op jit(solution)/shard_map/all_to_all | solution.py:441
  155.9 1.3 shard_map.164
  (67 shorter events, 4.0 us)
Async XLA Ops:
  51.0 4.9 %copy-start.5 = (f32[128]{0:T(128)S(1)}, f32[128]{0:T(128)}, u32[]{:S(2)}) copy-start(f32[128]{0:T(128)} %gain_hbm.1) | copy-start | bytes 1540
  51.0 4.9 %copy-start.6 = (f32[128]{0:T(128)S(1)}, f32[128]{0:T(128)}, u32[]{:S(2)}) copy-start(f32[128]{0:T(128)} %bias_hbm.1) | copy-start | bytes 1540
  51.0 4.9 %copy-start.10 = (f32[128]{0:T(128)S(1)}, f32[128]{0:T(128)}, u32[]{:S(2)}) copy-start(f32[128]{0:T(128)} %param.23) | copy-start | bytes 1540
  51.0 4.9 %copy-start.11 = (f32[128]{0:T(128)S(1)}, f32[128]{0:T(128)}, u32[]{:S(2)}) copy-start(f32[128]{0:T(128)} %param.24) | copy-start | bytes 1540
  51.0 4.9 %copy-start.12 = (f32[128]{0:T(128)S(1)}, f32[128]{0:T(128)}, u32[]{:S(2)}) copy-start(f32[128]{0:T(128)} %param.26) | copy-start | bytes 1540
  51.0 4.9 %copy-start.13 = (f32[128]{0:T(128)S(1)}, f32[128]{0:T(128)}, u32[]{:S(2)}) copy-start(f32[128]{0:T(128)} %param.27) | copy-start | bytes 1540
  51.0 5.0 %copy-start = (bf16[5,640,128]{2,1,0:T(8,128)(2,1)S(1)}, bf16[5,640,128]{2,1,0:T(8,128)(2,1)}, u32[]{:S(2)}) copy-start(bf16[5,640,128]{2,1,0:T(8,128)(2,1)} %get-tuple-element.32.x_ref) | copy-start | bytes 2457604
  51.1 4.9 %copy-start.2 = (bf16[128,128]{1,0:T(8,128)(2,1)S(1)}, bf16[128,128]{1,0:T(8,128)(2,1)}, u32[]{:S(2)}) copy-start(bf16[128,128]{1,0:T(8,128)(2,1)} %w_ref.1) | copy-start | bytes 98308
  51.1 24.0 %all-to-all-start.1 = ((bf16[128,32,128]{2,1,0:T(8,128)(2,1)}), bf16[128,32,128]{2,1,0:T(8,128)(2,1)S(1)}, u32[]{:S(2)}, u32[]{:S(2)}) async-start(bf16[128,32,128]{2,1,0:T(8,128)(2,1)} %shard_map.155), calls=%async_computation.1 | async-start | bytes 2097152 | tf_op jit(solution)/shard_map/all_to_all | solution.py:364
  79.5 4.3 %copy-start.4 = (bf16[128,512]{1,0:T(8,128)(2,1)S(1)}, bf16[128,512]{1,0:T(8,128)(2,1)}, u32[]{:S(2)}) copy-start(bf16[128,512]{1,0:T(8,128)(2,1)} %param.28) | copy-start | bytes 393220
  79.5 17.5 %all-to-all-start.2 = ((bf16[8,512,128]{2,1,0:T(8,128)(2,1)}), bf16[8,512,128]{2,1,0:T(8,128)(2,1)S(1)}, u32[]{:S(2)}, u32[]{:S(2)}) async-start(bf16[8,512,128]{2,1,0:T(8,128)(2,1)} %shard_map.157), calls=%async_computation.2 | async-start | bytes 2097152 | tf_op jit(solution)/shard_map/all_to_all | solution.py:373
  83.8 26.2 %copy-start.1 = (bf16[128,128]{1,0:T(8,128)(2,1)S(1)}, bf16[128,128]{1,0:T(8,128)(2,1)}, u32[]{:S(2)}) copy-start(bf16[128,128]{1,0:T(8,128)(2,1)} %wo_ref.5) | copy-start | bytes 98308
  83.8 26.2 %copy-start.3 = (f32[4]{0:T(128)S(1)}, f32[4]{0:T(128)}, u32[]{:S(2)}) copy-start(f32[4]{0:T(128)} %inter_ref.5) | copy-start | bytes 52
  97.5 9.7 %collective-permute-start = (bf16[160,640]{1,0:T(8,128)(2,1)S(1)}, bf16[160,640]{1,0:T(8,128)(2,1)S(1)}, u32[]{:S(2)}, u32[]{:S(2)}) collective-permute-start(bf16[160,640]{1,0:T(8,128)(2,1)S(1)} %shard_map.158.refs_0_), channel_id=1, source_target_pairs={{0,4},{1,5},{2,6},{3,7},{4,0},{5,1},{6,2},{7,3},{8,12},{9,13},{10,... | collective-permute-start | bytes 614408 | tf_op jit(solution)/shard_map/ppermute | solution.py:390
  98.4 9.7 %collective-permute-start.1 = (bf16[160,640]{1,0:T(8,128)(2,1)S(1)}, bf16[160,640]{1,0:T(8,128)(2,1)S(1)}, u32[]{:S(2)}, u32[]{:S(2)}) collective-permute-start(bf16[160,640]{1,0:T(8,128)(2,1)S(1)} %shard_map.158.refs_0_), channel_id=1, source_target_pairs={{0,1},{1,0},{2,3},{3,2},{4,5},{5,4},{6,7},{7,6},{8,9},{9,8},{10,11... | collective-permute-start | bytes 614408 | tf_op jit(solution)/shard_map/ppermute | solution.py:390
  103.0 13.4 %collective-permute-start.3 = (bf16[160,640]{1,0:T(8,128)(2,1)S(1)}, bf16[160,640]{1,0:T(8,128)(2,1)S(1)}, u32[]{:S(2)}, u32[]{:S(2)}) collective-permute-start(bf16[160,640]{1,0:T(8,128)(2,1)S(1)} %shard_map.158.refs_0_), channel_id=1, source_target_pairs={{0,8},{1,9},{2,10},{3,11},{4,12},{5,13},{6,14},{7,15},{8,0},{9,1},... | collective-permute-start | bytes 614408 | tf_op jit(solution)/shard_map/ppermute | solution.py:390
  105.0 11.4 %collective-permute-start.4 = (bf16[160,640]{1,0:T(8,128)(2,1)S(1)}, bf16[160,640]{1,0:T(8,128)(2,1)S(1)}, u32[]{:S(2)}, u32[]{:S(2)}) collective-permute-start(bf16[160,640]{1,0:T(8,128)(2,1)S(1)} %shard_map.158.refs_0_), channel_id=1, source_target_pairs={{0,12},{1,13},{2,14},{3,15},{4,8},{5,9},{6,10},{7,11},{8,4},{9,5},... | collective-permute-start | bytes 614408 | tf_op jit(solution)/shard_map/ppermute | solution.py:390
  106.9 9.5 %collective-permute-start.5 = (bf16[160,640]{1,0:T(8,128)(2,1)S(1)}, bf16[160,640]{1,0:T(8,128)(2,1)S(1)}, u32[]{:S(2)}, u32[]{:S(2)}) collective-permute-start(bf16[160,640]{1,0:T(8,128)(2,1)S(1)} %shard_map.158.refs_0_), channel_id=1, source_target_pairs={{0,2},{1,3},{2,0},{3,1},{4,6},{5,7},{6,4},{7,5},{8,10},{9,11},{10,... | collective-permute-start | bytes 614408 | tf_op jit(solution)/shard_map/ppermute | solution.py:390
  107.2 2.6 %collective-permute-start.2 = (bf16[160,640]{1,0:T(8,128)(2,1)S(1)}, bf16[160,640]{1,0:T(8,128)(2,1)S(1)}, u32[]{:S(2)}, u32[]{:S(2)}) collective-permute-start(bf16[160,640]{1,0:T(8,128)(2,1)S(1)} %collective-permute-done.refs_1_), channel_id=1, source_target_pairs={{0,1},{1,0},{2,3},{3,2},{4,5},{5,4},{6,7},{7,6},{8,9},{9,8},{10,11... | collective-permute-start | bytes 614408 | tf_op jit(solution)/shard_map/ppermute | solution.py:390
  108.1 8.3 %collective-permute-start.6 = (bf16[160,640]{1,0:T(8,128)(2,1)S(1)}, bf16[160,640]{1,0:T(8,128)(2,1)S(1)}, u32[]{:S(2)}, u32[]{:S(2)}) collective-permute-start(bf16[160,640]{1,0:T(8,128)(2,1)S(1)} %collective-permute-done.refs_1_), channel_id=1, source_target_pairs={{0,66},{1,67},{2,64},{3,65},{4,70},{5,71},{6,68},{7,69},{8,74},{9,... | collective-permute-start | bytes 614408 | tf_op jit(solution)/shard_map/ppermute | solution.py:390
  116.5 2.5 %collective-permute-start.7 = (bf16[2,160,640]{2,1,0:T(8,128)(2,1)S(1)}, bf16[2,160,640]{2,1,0:T(8,128)(2,1)S(1)}, u32[]{:S(2)}, u32[]{:S(2)}) collective-permute-start(bf16[2,160,640]{2,1,0:T(8,128)(2,1)S(1)} %pad_maximum_fusion.refs_0_), channel_id=1, source_target_pairs={{0,1},{1,0},{2,3},{3,2},{4,5},{5,4},{6,7},{7,6},{8,9},{9,8},{10,11... | collective-permute-start | bytes 1228808 | tf_op jit(solution)/shard_map/ppermute | solution.py:390
  117.0 2.0 %collective-permute-start.8 = (bf16[2,160,640]{2,1,0:T(8,128)(2,1)S(1)}, bf16[2,160,640]{2,1,0:T(8,128)(2,1)S(1)}, u32[]{:S(2)}, u32[]{:S(2)}) collective-permute-start(bf16[2,160,640]{2,1,0:T(8,128)(2,1)S(1)} %pad_maximum_fusion.1.refs_1_), channel_id=1, source_target_pairs={{0,1},{1,0},{2,3},{3,2},{4,5},{5,4},{6,7},{7,6},{8,9},{9,8},{10,11... | collective-permute-start | bytes 1228808 | tf_op jit(solution)/shard_map/ppermute | solution.py:390
  117.2 12.3 %collective-permute-start.9 = (bf16[2,160,640]{2,1,0:T(8,128)(2,1)S(1)}, bf16[2,160,640]{2,1,0:T(8,128)(2,1)S(1)}, u32[]{:S(2)}, u32[]{:S(2)}) collective-permute-start(bf16[2,160,640]{2,1,0:T(8,128)(2,1)S(1)} %pad_maximum_fusion.refs_0_), channel_id=1, source_target_pairs={{0,66},{1,67},{2,64},{3,65},{4,70},{5,71},{6,68},{7,69},{8,74},{9,... | collective-permute-start | bytes 1228808 | tf_op jit(solution)/shard_map/ppermute | solution.py:390
  129.5 2.4 %collective-permute-start.10 = (bf16[2,160,640]{2,1,0:T(8,128)(2,1)S(1)}, bf16[2,160,640]{2,1,0:T(8,128)(2,1)S(1)}, u32[]{:S(2)}, u32[]{:S(2)}) collective-permute-start(bf16[2,160,640]{2,1,0:T(8,128)(2,1)S(1)} %collective-permute-done.9.refs_0_), channel_id=1, source_target_pairs={{0,1},{1,0},{2,3},{3,2},{4,5},{5,4},{6,7},{7,6},{8,9},{9,8},{10,11... | collective-permute-start | bytes 1228808 | tf_op jit(solution)/shard_map/ppermute | solution.py:390
  (3 other events, 8.9 us)

commit v7 on v6

--- a/solution.py
+++ b/solution.py
@@ -427,7 +427,7 @@
             *parts,
         )
 
-    one_across = swap(one, ROWS // 2, 2)
+    one_across = swap(merged, ROWS // 2, 6)
     near = hold((merged, one, merged2, core(one)))
     outs = [attend(CALLS[0], *near)]
     outs[0], two, three, beside, one_across = hold((outs[0], two, three, beside, one_across))

time: 158 us -> 159 us (level)
  transfers between devices with their start and end apart: 13 -> 13, of which waited for: 4 -> 6; matrix products, arithmetic and copies ran while one was open for 1% -> 1% of each run, Pallas kernels for 12% -> 12%
where the time goes in v7:
time: 159 us; the launch traced here: 157 us
  blocking collectives  56.3 us (35%)
  Pallas kernels  44.2 us (28%)
  waiting for transfers between devices  33.2 us (21%)
  starting transfers between devices  21 us (13%)
    all_to_all x1, blocking collectives, on_device(): channel = lax.all_to_all(parcels, both, 0, 0, tiled=True)  39 us
    pallas_call x3, Pallas kernels, attend(): call(functools.partial(attend_kernel, steps), struct((len(steps) * T, RI,...  23.1 us
    all_to_all x1, blocking collectives, on_device(): home = lax.all_to_all(out, 'row', 0, 0, tiled=True)  17.3 us
    all_to_all x1, waiting for transfers between devices, on_device(): returned = lax.all_to_all(product, both, 0, 0, tiled=True)  17.1 us
    all_to_all x1, waiting for transfers between devices, on_device(): mid = lax.all_to_all(turned, 'row', 0, 0, tiled=True)  13.2 us
    ppermute x11, starting transfers between devices, swap(): return lax.ppermute(values, both, pairs)  12.5 us
    pallas_call x1, Pallas kernels, on_device(): call(product_kernel, struct((C, BACK, C)), [pltpu.VMEM((C * SEND, C), F32...  7.16 us
    pallas_call x1, Pallas kernels, on_device(): call(project_kernel, [struct((C, SEND, C)), struct((A, N, C))], [pltpu.VM...  4.86 us
  transfers between devices with their start and end apart: 13, of which 6 were waited for; matrix products, arithmetic and copies ran while one was open for 1% of the time, Pallas kernels for 12%

profile of v7, /device:TPU:1, one launch (start us, length us, event | category | flops | bytes accessed | tf_op | source)
XLA Modules:
  0.0 157.3 jit_solution(6402585308401460205)
XLA Ops:
  0.0 4.9 %shard_map.154 = (bf16[128,56,128]{2,1,0:T(8,128)(2,1)}, bf16[5,640,128]{2,1,0:T(8,128)(2,1)}) custom-call(bf16[80,40,128]{2,1,0:T(8,128)(2,1)} %pair_hbm.1, s32[10]{0:T(128)} %valid_hbm.1, f32[128]{0:T(128)} %gain_hbm.1, f32[128]{0:T(128)} %bias_hbm.1, bf16[128,512]{1,0:T(8,128)(2,1)} %w_hbm.1), custom_call_target="tpu_custom_call" | custom-call | tf_op jit(solution)/shard_map/pallas_call | solution.py:334
  4.9 39.0 %all_to_all.20.in_ref = bf16[128,56,128]{2,1,0:T(8,128)(2,1)S(1)} all-to-all(bf16[128,56,128]{2,1,0:T(8,128)(2,1)} %get-tuple-element.31), channel_id=1, replica_groups=mesh['row'=8,'col'=16] {'row','col'}, dimensions={0} | all-to-all | bytes 3670016 | tf_op jit(solution)/shard_map/all_to_all | solution.py:351
  43.9 7.2 %shard_map.155 = bf16[128,32,128]{2,1,0:T(8,128)(2,1)} custom-call(bf16[128,56,128]{2,1,0:T(8,128)(2,1)S(1)} %all_to_all.20.in_ref), custom_call_target="tpu_custom_call" | custom-call | tf_op jit(solution)/shard_map/pallas_call | solution.py:352
  51.1 4.8 %all-to-all-start.1 = ((bf16[128,32,128]{2,1,0:T(8,128)(2,1)}), bf16[128,32,128]{2,1,0:T(8,128)(2,1)S(1)}, u32[]{:S(2)}, u32[]{:S(2)}) async-start(bf16[128,32,128]{2,1,0:T(8,128)(2,1)} %shard_map.155), calls=%async_computation.1 | async-start | bytes 2097152 | tf_op jit(solution)/shard_map/all_to_all | solution.py:364
  56.0 1.1 shard_map.156.gate_ref
  57.9 17.1 %all-to-all-done.1.in_ref = bf16[128,32,128]{2,1,0:T(8,128)(2,1)S(1)} async-done(((bf16[128,32,128]{2,1,0:T(8,128)(2,1)}), bf16[128,32,128]{2,1,0:T(8,128)(2,1)S(1)}, u32[]{:S(2)}, u32[]{:S(2)}) %all-to-all-start.1) | async-done | bytes 1048608 | tf_op jit(solution)/shard_map/all_to_all | solution.py:364
  75.1 4.4 %shard_map.157 = bf16[8,512,128]{2,1,0:T(8,128)(2,1)} custom-call(bf16[128,32,128]{2,1,0:T(8,128)(2,1)S(1)} %all-to-all-done.1.in_ref, bf16[5,640,128]{2,1,0:T(8,128)(2,1)S(1)} %copy-done, f32[5,640,128]{2,1,0:T(8,128)S(1)} %shard_map.156.gate_ref, f32[6,128]{1,0:T(8,128)S(1)} %stack.45.norms_ref, bf16[136,128]{1,0:T(8,128)(2,1)S(1)} %fusion.1.w_ref), custom_call_target="tpu_custom_call" | custom-call | tf_op jit(solution)/shard_map/pallas_call | solution.py:367
  79.5 3.7 %all-to-all-start.2 = ((bf16[8,512,128]{2,1,0:T(8,128)(2,1)}), bf16[8,512,128]{2,1,0:T(8,128)(2,1)S(1)}, u32[]{:S(2)}, u32[]{:S(2)}) async-start(bf16[8,512,128]{2,1,0:T(8,128)(2,1)} %shard_map.157), calls=%async_computation.2 | async-start | bytes 2097152 | tf_op jit(solution)/shard_map/all_to_all | solution.py:373
  83.8 13.2 %all-to-all-done.2.in_ref.mid_ref = bf16[8,512,128]{2,1,0:T(8,128)(2,1)S(1)} async-done(((bf16[8,512,128]{2,1,0:T(8,128)(2,1)}), bf16[8,512,128]{2,1,0:T(8,128)(2,1)S(1)}, u32[]{:S(2)}, u32[]{:S(2)}) %all-to-all-start.2) | async-done | bytes 1048608 | tf_op jit(solution)/shard_map/all_to_all | solution.py:373
  97.5 0.9 collective-permute-start
  98.4 2.3 %collective-permute-start.1 = (bf16[160,640]{1,0:T(8,128)(2,1)S(1)}, bf16[160,640]{1,0:T(8,128)(2,1)S(1)}, u32[]{:S(2)}, u32[]{:S(2)}) collective-permute-start(bf16[160,640]{1,0:T(8,128)(2,1)S(1)} %shard_map.158.refs_0_), channel_id=1, source_target_pairs={{0,1},{1,0},{2,3},{3,2},{4,5},{5,4},{6,7},{7,6},{8,9},{9,8},{10,11... | collective-permute-start | bytes 614408 | tf_op jit(solution)/shard_map/ppermute | solution.py:390
  101.3 1.6 %shard_map.159 = (bf16[5,640,128]{2,1,0:T(8,128)(2,1)S(1)}, bf16[5,128,640]{2,1,0:T(8,128)(2,1)S(1)}, bf16[5,640,256]{2,1,0:T(8,128)(2,1)S(1)}, f32[5,640,128]{2,1,0:T(8,128)S(1)}) custom-call(bf16[8,512,128]{2,1,0:T(8,128)(2,1)S(1)} %all-to-all-done.2.in_ref.mid_ref, f32[6,128]{1,0:T(8,128)S(1)} %stack.45.norms_ref, ...), custom_call_target="tpu_custom_call" | custom-call | tf_op jit(solution)/shard_map/pallas_call | solution.py:405
  103.0 2.0 %collective-permute-start.3 = (bf16[160,640]{1,0:T(8,128)(2,1)S(1)}, bf16[160,640]{1,0:T(8,128)(2,1)S(1)}, u32[]{:S(2)}, u32[]{:S(2)}) collective-permute-start(bf16[160,640]{1,0:T(8,128)(2,1)S(1)} %shard_map.158.refs_0_), channel_id=1, source_target_pairs={{0,8},{1,9},{2,10},{3,11},{4,12},{5,13},{6,14},{7,15},{8,0},{9,1},... | collective-permute-start | bytes 614408 | tf_op jit(solution)/shard_map/ppermute | solution.py:390
  105.0 2.0 %collective-permute-start.4 = (bf16[160,640]{1,0:T(8,128)(2,1)S(1)}, bf16[160,640]{1,0:T(8,128)(2,1)S(1)}, u32[]{:S(2)}, u32[]{:S(2)}) collective-permute-start(bf16[160,640]{1,0:T(8,128)(2,1)S(1)} %shard_map.158.refs_0_), channel_id=1, source_target_pairs={{0,12},{1,13},{2,14},{3,15},{4,8},{5,9},{6,10},{7,11},{8,4},{9,5},... | collective-permute-start | bytes 614408 | tf_op jit(solution)/shard_map/ppermute | solution.py:390
  107.6 1.4 collective-permute-start.2
  109.1 1.0 collective-permute-done.2.refs_3_
  110.3 6.4 %shard_map.160.refs_0_ = bf16[10,80,128]{2,1,0:T(8,128)(2,1)S(1)} custom-call(s32[1]{0:T(128)} %bitcast.me_ref, f32[4]{0:T(128)S(1)} %copy-done.3, bf16[5,640,128]{2,1,0:T(8,128)(2,1)S(1)} %get-tuple-element.37.q_ref, bf16[5,128,640]{2,1,0:T(8,128)(2,1)S(1)} %get-tuple-element.38.k_ref, bf16[5,640,256]{2,1,0:T(8,128)(2,1)S(1)} %get-tuple-element.39.v_ref, ...), custom_call_target="tpu_custom_call" | custom-call | flops 1048576 | bytes 65536 | tf_op jit(solution)/shard_map/pallas_call | solution.py:417
  117.5 1.5 collective-permute-start.9
  119.2 10.3 %shard_map.161.refs_1_ = bf16[20,80,128]{2,1,0:T(8,128)(2,1)S(1)} custom-call(s32[1]{0:T(128)} %bitcast.me_ref, f32[4]{0:T(128)S(1)} %copy-done.3, bf16[5,640,128]{2,1,0:T(8,128)(2,1)S(1)} %get-tuple-element.37.q_ref, bf16[5,128,640]{2,1,0:T(8,128)(2,1)S(1)} %get-tuple-element.38.k_ref, bf16[5,640,256]{2,1,0:T(8,128)(2,1)S(1)} %get-tuple-element.39.v_ref, ...), custom_call_target="tpu_custom_call" | custom-call | flops 1048576 | bytes 65536 | tf_op jit(solution)/shard_map/pallas_call | solution.py:417
  129.8 1.0 collective-permute-start.10
  130.8 1.4 collective-permute-done.10.refs_1_
  132.1 6.4 %shard_map.162.refs_2_ = bf16[10,80,128]{2,1,0:T(8,128)(2,1)S(1)} custom-call(s32[1]{0:T(128)} %bitcast.me_ref, f32[4]{0:T(128)S(1)} %copy-done.3, bf16[5,640,128]{2,1,0:T(8,128)(2,1)S(1)} %get-tuple-element.37.q_ref, bf16[5,128,640]{2,1,0:T(8,128)(2,1)S(1)} %get-tuple-element.38.k_ref, bf16[5,640,256]{2,1,0:T(8,128)(2,1)S(1)} %get-tuple-element.39.v_ref, ...), custom_call_target="tpu_custom_call" | custom-call | flops 1048576 | bytes 65536 | tf_op jit(solution)/shard_map/pallas_call | solution.py:417
  138.6 17.3 %all_to_all.21.in_ref = bf16[40,80,128]{2,1,0:T(8,128)(2,1)S(1)} all-to-all(bf16[40,80,128]{2,1,0:T(8,128)(2,1)S(1)} %shard_map.163), channel_id=1, replica_groups=mesh['row'=8,'col'=16] {'row'}, dimensions={0} | all-to-all | bytes 1638400 | tf_op jit(solution)/shard_map/all_to_all | solution.py:441
  156.0 1.3 shard_map.164
  (67 shorter events, 4.6 us)
Async XLA Ops:
  51.0 4.9 %copy-start.5 = (f32[128]{0:T(128)S(1)}, f32[128]{0:T(128)}, u32[]{:S(2)}) copy-start(f32[128]{0:T(128)} %gain_hbm.1) | copy-start | bytes 1540
  51.0 4.9 %copy-start.6 = (f32[128]{0:T(128)S(1)}, f32[128]{0:T(128)}, u32[]{:S(2)}) copy-start(f32[128]{0:T(128)} %bias_hbm.1) | copy-start | bytes 1540
  51.0 4.9 %copy-start.10 = (f32[128]{0:T(128)S(1)}, f32[128]{0:T(128)}, u32[]{:S(2)}) copy-start(f32[128]{0:T(128)} %param.23) | copy-start | bytes 1540
  51.0 4.9 %copy-start.11 = (f32[128]{0:T(128)S(1)}, f32[128]{0:T(128)}, u32[]{:S(2)}) copy-start(f32[128]{0:T(128)} %param.24) | copy-start | bytes 1540
  51.0 4.9 %copy-start.12 = (f32[128]{0:T(128)S(1)}, f32[128]{0:T(128)}, u32[]{:S(2)}) copy-start(f32[128]{0:T(128)} %param.26) | copy-start | bytes 1540
  51.0 4.9 %copy-start.13 = (f32[128]{0:T(128)S(1)}, f32[128]{0:T(128)}, u32[]{:S(2)}) copy-start(f32[128]{0:T(128)} %param.27) | copy-start | bytes 1540
  51.0 5.0 %copy-start = (bf16[5,640,128]{2,1,0:T(8,128)(2,1)S(1)}, bf16[5,640,128]{2,1,0:T(8,128)(2,1)}, u32[]{:S(2)}) copy-start(bf16[5,640,128]{2,1,0:T(8,128)(2,1)} %get-tuple-element.32.x_ref) | copy-start | bytes 2457604
  51.1 4.9 %copy-start.2 = (bf16[128,128]{1,0:T(8,128)(2,1)S(1)}, bf16[128,128]{1,0:T(8,128)(2,1)}, u32[]{:S(2)}) copy-start(bf16[128,128]{1,0:T(8,128)(2,1)} %w_ref.1) | copy-start | bytes 98308
  51.1 24.0 %all-to-all-start.1 = ((bf16[128,32,128]{2,1,0:T(8,128)(2,1)}), bf16[128,32,128]{2,1,0:T(8,128)(2,1)S(1)}, u32[]{:S(2)}, u32[]{:S(2)}) async-start(bf16[128,32,128]{2,1,0:T(8,128)(2,1)} %shard_map.155), calls=%async_computation.1 | async-start | bytes 2097152 | tf_op jit(solution)/shard_map/all_to_all | solution.py:364
  79.5 4.3 %copy-start.4 = (bf16[128,512]{1,0:T(8,128)(2,1)S(1)}, bf16[128,512]{1,0:T(8,128)(2,1)}, u32[]{:S(2)}) copy-start(bf16[128,512]{1,0:T(8,128)(2,1)} %param.28) | copy-start | bytes 393220
  79.5 17.5 %all-to-all-start.2 = ((bf16[8,512,128]{2,1,0:T(8,128)(2,1)}), bf16[8,512,128]{2,1,0:T(8,128)(2,1)S(1)}, u32[]{:S(2)}, u32[]{:S(2)}) async-start(bf16[8,512,128]{2,1,0:T(8,128)(2,1)} %shard_map.157), calls=%async_computation.2 | async-start | bytes 2097152 | tf_op jit(solution)/shard_map/all_to_all | solution.py:373
  83.8 26.5 %copy-start.1 = (bf16[128,128]{1,0:T(8,128)(2,1)S(1)}, bf16[128,128]{1,0:T(8,128)(2,1)}, u32[]{:S(2)}) copy-start(bf16[128,128]{1,0:T(8,128)(2,1)} %wo_ref.5) | copy-start | bytes 98308
  83.8 26.5 %copy-start.3 = (f32[4]{0:T(128)S(1)}, f32[4]{0:T(128)}, u32[]{:S(2)}) copy-start(f32[4]{0:T(128)} %inter_ref.5) | copy-start | bytes 52
  97.5 9.7 %collective-permute-start = (bf16[160,640]{1,0:T(8,128)(2,1)S(1)}, bf16[160,640]{1,0:T(8,128)(2,1)S(1)}, u32[]{:S(2)}, u32[]{:S(2)}) collective-permute-start(bf16[160,640]{1,0:T(8,128)(2,1)S(1)} %shard_map.158.refs_0_), channel_id=1, source_target_pairs={{0,4},{1,5},{2,6},{3,7},{4,0},{5,1},{6,2},{7,3},{8,12},{9,13},{10,... | collective-permute-start | bytes 614408 | tf_op jit(solution)/shard_map/ppermute | solution.py:390
  98.4 9.2 %collective-permute-start.1 = (bf16[160,640]{1,0:T(8,128)(2,1)S(1)}, bf16[160,640]{1,0:T(8,128)(2,1)S(1)}, u32[]{:S(2)}, u32[]{:S(2)}) collective-permute-start(bf16[160,640]{1,0:T(8,128)(2,1)S(1)} %shard_map.158.refs_0_), channel_id=1, source_target_pairs={{0,1},{1,0},{2,3},{3,2},{4,5},{5,4},{6,7},{7,6},{8,9},{9,8},{10,11... | collective-permute-start | bytes 614408 | tf_op jit(solution)/shard_map/ppermute | solution.py:390
  103.0 13.7 %collective-permute-start.3 = (bf16[160,640]{1,0:T(8,128)(2,1)S(1)}, bf16[160,640]{1,0:T(8,128)(2,1)S(1)}, u32[]{:S(2)}, u32[]{:S(2)}) collective-permute-start(bf16[160,640]{1,0:T(8,128)(2,1)S(1)} %shard_map.158.refs_0_), channel_id=1, source_target_pairs={{0,8},{1,9},{2,10},{3,11},{4,12},{5,13},{6,14},{7,15},{8,0},{9,1},... | collective-permute-start | bytes 614408 | tf_op jit(solution)/shard_map/ppermute | solution.py:390
  105.0 11.7 %collective-permute-start.4 = (bf16[160,640]{1,0:T(8,128)(2,1)S(1)}, bf16[160,640]{1,0:T(8,128)(2,1)S(1)}, u32[]{:S(2)}, u32[]{:S(2)}) collective-permute-start(bf16[160,640]{1,0:T(8,128)(2,1)S(1)} %shard_map.158.refs_0_), channel_id=1, source_target_pairs={{0,12},{1,13},{2,14},{3,15},{4,8},{5,9},{6,10},{7,11},{8,4},{9,5},... | collective-permute-start | bytes 614408 | tf_op jit(solution)/shard_map/ppermute | solution.py:390
  106.9 9.8 %collective-permute-start.5 = (bf16[160,640]{1,0:T(8,128)(2,1)S(1)}, bf16[160,640]{1,0:T(8,128)(2,1)S(1)}, u32[]{:S(2)}, u32[]{:S(2)}) collective-permute-start(bf16[160,640]{1,0:T(8,128)(2,1)S(1)} %shard_map.158.refs_0_), channel_id=1, source_target_pairs={{0,2},{1,3},{2,0},{3,1},{4,6},{5,7},{6,4},{7,5},{8,10},{9,11},{10,... | collective-permute-start | bytes 614408 | tf_op jit(solution)/shard_map/ppermute | solution.py:390
  107.2 9.5 %collective-permute-start.6 = (bf16[160,640]{1,0:T(8,128)(2,1)S(1)}, bf16[160,640]{1,0:T(8,128)(2,1)S(1)}, u32[]{:S(2)}, u32[]{:S(2)}) collective-permute-start(bf16[160,640]{1,0:T(8,128)(2,1)S(1)} %shard_map.158.refs_0_), channel_id=1, source_target_pairs={{0,70},{1,71},{2,68},{3,69},{4,66},{5,67},{6,64},{7,65},{8,78},{9,... | collective-permute-start | bytes 614408 | tf_op jit(solution)/shard_map/ppermute | solution.py:390
  107.6 2.5 %collective-permute-start.2 = (bf16[160,640]{1,0:T(8,128)(2,1)S(1)}, bf16[160,640]{1,0:T(8,128)(2,1)S(1)}, u32[]{:S(2)}, u32[]{:S(2)}) collective-permute-start(bf16[160,640]{1,0:T(8,128)(2,1)S(1)} %collective-permute-done.refs_1_), channel_id=1, source_target_pairs={{0,1},{1,0},{2,3},{3,2},{4,5},{5,4},{6,7},{7,6},{8,9},{9,8},{10,11... | collective-permute-start | bytes 614408 | tf_op jit(solution)/shard_map/ppermute | solution.py:390
  116.8 2.3 %collective-permute-start.7 = (bf16[2,160,640]{2,1,0:T(8,128)(2,1)S(1)}, bf16[2,160,640]{2,1,0:T(8,128)(2,1)S(1)}, u32[]{:S(2)}, u32[]{:S(2)}) collective-permute-start(bf16[2,160,640]{2,1,0:T(8,128)(2,1)S(1)} %pad_maximum_fusion.refs_0_), channel_id=1, source_target_pairs={{0,1},{1,0},{2,3},{3,2},{4,5},{5,4},{6,7},{7,6},{8,9},{9,8},{10,11... | collective-permute-start | bytes 1228808 | tf_op jit(solution)/shard_map/ppermute | solution.py:390
  117.3 1.9 %collective-permute-start.8 = (bf16[2,160,640]{2,1,0:T(8,128)(2,1)S(1)}, bf16[2,160,640]{2,1,0:T(8,128)(2,1)S(1)}, u32[]{:S(2)}, u32[]{:S(2)}) collective-permute-start(bf16[2,160,640]{2,1,0:T(8,128)(2,1)S(1)} %pad_maximum_fusion.1.refs_1_), channel_id=1, source_target_pairs={{0,1},{1,0},{2,3},{3,2},{4,5},{5,4},{6,7},{7,6},{8,9},{9,8},{10,11... | collective-permute-start | bytes 1228808 | tf_op jit(solution)/shard_map/ppermute | solution.py:390
  117.5 12.3 %collective-permute-start.9 = (bf16[2,160,640]{2,1,0:T(8,128)(2,1)S(1)}, bf16[2,160,640]{2,1,0:T(8,128)(2,1)S(1)}, u32[]{:S(2)}, u32[]{:S(2)}) collective-permute-start(bf16[2,160,640]{2,1,0:T(8,128)(2,1)S(1)} %pad_maximum_fusion.refs_0_), channel_id=1, source_target_pairs={{0,66},{1,67},{2,64},{3,65},{4,70},{5,71},{6,68},{7,69},{8,74},{9,... | collective-permute-start | bytes 1228808 | tf_op jit(solution)/shard_map/ppermute | solution.py:390
  129.8 2.4 %collective-permute-start.10 = (bf16[2,160,640]{2,1,0:T(8,128)(2,1)S(1)}, bf16[2,160,640]{2,1,0:T(8,128)(2,1)S(1)}, u32[]{:S(2)}, u32[]{:S(2)}) collective-permute-start(bf16[2,160,640]{2,1,0:T(8,128)(2,1)S(1)} %collective-permute-done.9.refs_0_), channel_id=1, source_target_pairs={{0,1},{1,0},{2,3},{3,2},{4,5},{5,4},{6,7},{7,6},{8,9},{9,8},{10,11... | collective-permute-start | bytes 1228808 | tf_op jit(solution)/shard_map/ppermute | solution.py:390
  (3 other events, 8.9 us)
